TPU v7x, 32 devices: a whole 2x2x4 slice. The times are simulated.
32 devices in a mesh: outer: 2 (over x), dp: 16 (over z, y, core).
Axes of the slice: x: 2, y: 2, z: 4, core: 2. Of those that a mesh axis runs over, the one named last changes fastest.
Arguments:
- grads: float32 [2, 2, 1024, 576], P('outer', None, 'dp'), may hold values from -64 to 64
- momentum: float32 [2, 1024, 576], P(None, 'dp'), may hold values from -4 to 4
Outputs:
- momentum_new: float32 [2, 1024, 576], P(None, 'dp')
- update: float32 [2, 1024, 576], P(None, 'dp')
All inputs are finite; a program needn't handle non-finite values.
Results may differ from a plain program's by a relative error of at most 0.0057.
Values may be sent and summed in bfloat16 or wider, within the bound.
No kernel may reach another device: no remote copies, remote signals or barrier semaphores. Data moves between devices by JAX's collectives and lax.ppermute only.
A program may use at most 64 MiB of HBM per device.

v0:
```python
import math

import jax
import jax.numpy as jnp
from jax import lax
from jax.sharding import PartitionSpec as P

ITERS = 2


coef_a = 3.4445
coef_b = -4.775
coef_c = 2.0315
momentum_rate = 0.95
epsilon = 1e-06


def broadcast(value, axis, source):
    kept = jnp.where(lax.axis_index(axis) == source, value, 0).astype(value.dtype)
    return lax.psum(kept, axis)


def gram_product(matrix):
    return lax.dot_general(
        matrix, matrix, (((0,), (0,)), ((), ())), preferred_element_type=jnp.float32
    )


def newton_steps(matrix):
    for iteration in range(ITERS):
        product = gram_product(matrix)
        gram_matrix = product.astype(jnp.bfloat16)
        squared = jnp.dot(gram_matrix, gram_matrix, preferred_element_type=jnp.float32)
        polynomial = (coef_b * gram_matrix.astype(jnp.float32) + coef_c * squared).astype(
            jnp.bfloat16
        )
        mixed = jnp.dot(matrix, polynomial, preferred_element_type=jnp.float32)
        matrix = (coef_a * matrix.astype(jnp.float32) + mixed).astype(jnp.bfloat16)
    return matrix


def per_device(grads, momentum):
    pods = lax.axis_size("outer")
    pod_index = lax.axis_index("outer")
    devices = lax.axis_size("dp")
    dp_index = lax.axis_index("dp")
    local = grads[0]
    count = local.shape[0]
    per_pod = count // pods
    rows = local.shape[1]
    width = local.shape[2]
    height = rows * devices
    update_scale = 0.2 * math.sqrt(max(height, width))
    summed = lax.psum(local, "outer")
    momentum_new = momentum_rate * momentum + summed
    steering_all = summed + momentum_rate * momentum_new
    steering = lax.dynamic_slice_in_dim(steering_all, pod_index * per_pod, per_pod, 0)
    steering = steering.astype(jnp.bfloat16)
    stride = max(devices // count, 1)
    piece = steering[0]
    whole = lax.all_gather(piece, "dp", axis=0, tiled=True)
    values = whole.astype(jnp.float32)
    norm_value = jnp.sqrt(jnp.sum(values * values))
    start = (values / (norm_value + epsilon)).astype(jnp.bfloat16)
    owner_index = (pod_index * per_pod + 0) * stride % devices
    finished = lax.cond(
        dp_index == owner_index, lambda: newton_steps(start), lambda: jnp.zeros_like(start)
    )
    finished = broadcast(finished, "dp", owner_index)
    results = [lax.dynamic_slice_in_dim(finished, dp_index * rows, rows, 0)]
    mine = jnp.stack(results)
    gathered = lax.all_gather(mine, "outer", axis=0, tiled=True)
    return (momentum_new, update_scale * gathered.astype(jnp.float32))


def solution(mesh):
    in_specs = (P("outer", None, "dp", None), P(None, "dp", None))
    out_specs = (P(None, "dp", None), P(None, "dp", None))
    return jax.shard_map(
        per_device, mesh=mesh, in_specs=in_specs, out_specs=out_specs, check_vma=False
    )
```

profile of v0, /device:TPU:0, one launch (start us, length us, event | category | flops | bytes accessed | tf_op | source)
XLA Modules:
  0.0 199.1 jit_solution(14644280212323841054)
XLA Ops:
  7.2 0.0 all-reduce.3.cloned.1.call-start
  7.2 0.7 all-reduce.3.cloned.1.call-update
  7.9 0.0 all-gather.4.cloned.1.call-start
  7.9 29.3 %all-reduce.3.cloned.1.call-done = f32[2,64,576]{2,1,0:T(8,128)} async-done(((f32[2,64,576]{2,1,0:T(8,128)}), f32[2,64,576]{2,1,0:T(8,128)}) %all-reduce.3.cloned.1.call-update) | async-done | bytes 294928 | tf_op jit(solution)/shard_map/psum | solution.py:54
  37.3 1.1 multiply_add_fusion
  38.4 0.0 copy-start.1
  38.4 1.7 fusion.12
  40.1 0.0 all-gather.4.cloned.1.call-update
  40.1 0.0 all-reduce.5.cloned.1.call-start
  40.2 39.0 %all-gather.4.cloned.1.call-done = bf16[1,1024,576]{2,1,0:T(8,128)(2,1)} async-done(((bf16[1,64,576]{2,1,0:T(8,128)(2,1)}), bf16[1,1024,576]{2,1,0:T(8,128)(2,1)}) %all-gather.4.cloned.1.call-update) | async-done | bytes 1179664 | tf_op jit(solution)/shard_map/all_gather | solution.py:61
  79.2 0.0 copy-start
  79.2 2.7 %fusion.10 = f32[]{:T(128)} fusion(bf16[1,1024,576]{2,1,0:T(8,128)(2,1)} %all-gather.4.cloned.1.call-done), kind=kLoop, calls=%fused_computation.18 | loop fusion | flops 1769471 | bytes 1179652 | tf_op jit(solution)/shard_map/reduce_sum | solution.py:63
  82.6 0.0 copy-done
  82.7 0.2 fusion.11
  82.9 0.0 copy-done.1
  82.9 10.7 %conditional.1 = (bf16[1024,576]{1,0:T(8,128)(2,1)S(1)}) conditional(s32[]{:T(128)} %convert_element_type.50, () %tuple.14, bf16[1024,576]{1,0:T(8,128)(2,1)S(1)} %fusion.11), branch_computations={%region_2.3_spmd, %region_3.4_spmd} | conditional | flops 3491020800 | bytes 20348964 | solution.py:66
  82.9 1.1 convolution_convert_fusion.1
  84.1 0.6 copy.6
  84.7 2.7 %fusion = bf16[1024,576]{0,1:T(8,128)(2,1)} fusion(bf16[1024,576]{0,1:T(8,128)(2,1)S(1)} %copy.6, bf16[1024,576]{1,0:T(8,128)(2,1)S(1)} %param.1, bf16[576,576]{1,0:T(8,128)(2,1)S(1)} %convolution_convert_fusion.1), kind=kOutput, calls=%fused_computation.1 | convolution fusion | flops 1065701376 | bytes 4202496 | tf_op jit(solution)/shard_map/cond/branch_1_fun/dot_general | solution.py:37
  87.4 0.0 copy-start.2
  87.4 2.9 %convolution_convert_fusion = bf16[576,576]{1,0:T(8,128)(2,1)S(1)} fusion(bf16[1024,576]{0,1:T(8,128)(2,1)} %fusion), kind=kOutput, calls=%fused_computation.5 | convolution fusion | flops 679809024 | bytes 1843200 | tf_op jit(solution)/shard_map/cond/branch_1_fun/dot_general | solution.py:24
  90.3 0.0 copy-done.2
  90.3 2.5 %add_convert_fusion = bf16[1024,576]{0,1:T(8,128)(2,1)S(1)} fusion(bf16[1024,576]{0,1:T(8,128)(2,1)S(1)} %copy-done.2, bf16[576,576]{1,0:T(8,128)(2,1)S(1)} %convolution_convert_fusion), kind=kOutput, calls=%fused_computation.2 | convolution fusion | flops 1065701376 | bytes 3022848 | tf_op jit(solution)/shard_map/cond/branch_1_fun/dot_general | solution.py:37
  92.9 0.7 copy.10
  93.6 1.2 broadcast_select_fusion
  94.8 0.0 all-reduce.5.cloned.1.call-update
  94.8 91.0 %all-reduce.5.cloned.1.call-done = bf16[1024,576]{1,0:T(8,128)(2,1)} async-done(((bf16[1024,576]{1,0:T(8,128)(2,1)}), bf16[1024,576]{1,0:T(8,128)(2,1)}) %all-reduce.5.cloned.1.call-update) | async-done | bytes 1179664 | tf_op jit(solution)/shard_map/psum | solution.py:20
  185.8 0.9 constant_dynamic-slice_fusion
  186.7 5.1 %all-gather.1 = bf16[128,576]{1,0:T(8,128)(2,1)S(1)} all-gather(bf16[64,576]{1,0:T(8,128)(2,1)S(1)} %constant_dynamic-slice_fusion), channel_id=3, replica_groups=mesh['outer'=2,'dp'=16] {'outer'}, dimensions={0}, use_global_device_ids=true | all-gather | bytes 221184 | tf_op jit(solution)/shard_map/all_gather | solution.py:72
  191.8 0.8 convert_multiply_fusion.1
Async XLA Ops:
  7.2 30.1 %all-reduce.3.cloned.1.call-start = ((), (), s32[]{:S(2)}) async-start(), calls=%async_computation | async-start | bytes 655360 | tf_op jit(solution)/shard_map/psum | solution.py:54
  7.9 71.3 %all-gather.4.cloned.1.call-start = ((), (), s32[]{:S(2)}) async-start(), calls=%async_computation.2 | async-start | bytes 1392640 | tf_op jit(solution)/shard_map/all_gather | solution.py:61
  38.4 44.5 %copy-start.1 = (f32[2,64,576]{2,1,0:T(8,128)}, f32[2,64,576]{2,1,0:T(8,128)S(1)}, u32[]{:S(2)}) copy-start(f32[2,64,576]{2,1,0:T(8,128)S(1)} %multiply_add_fusion) | copy-start | bytes 884740
  40.1 145.7 %all-reduce.5.cloned.1.call-start = ((), (), s32[]{:S(2)}) async-start(), calls=%async_computation.1 | async-start | bytes 2621440 | tf_op jit(solution)/shard_map/psum | solution.py:20
  79.2 3.4 %copy-start = (bf16[1,1024,576]{2,1,0:T(8,128)(2,1)S(1)}, bf16[1,1024,576]{2,1,0:T(8,128)(2,1)}, u32[]{:S(2)}) copy-start(bf16[1,1024,576]{2,1,0:T(8,128)(2,1)} %all-gather.4.cloned.1.call-done) | copy-start | bytes 3538948
  87.4 2.9 %copy-start.2 = (bf16[1024,576]{0,1:T(8,128)(2,1)S(1)}, bf16[1024,576]{0,1:T(8,128)(2,1)}, u32[]{:S(2)}) copy-start(bf16[1024,576]{0,1:T(8,128)(2,1)} %fusion) | copy-start | bytes 3538948 | tf_op jit(solution)/shard_map/cond
Sparse Core Ops, SparseCore 0:
  10.3 26.9 all-reduce.2
  40.4 38.7 all-gather.3
  94.9 90.8 all-reduce.4
where the time goes:
time: 199 us
  waiting for transfers between devices  160 us (80%)
  between operations  14.5 us (7%)
  matrix products  9.26 us (5%)
  other arithmetic  7.67 us (4%)
  blocking collectives  5.1 us (3%)
  local copies, waits for them, and re-layouts  2.25 us (1%)
    psum x1, waiting for transfers between devices, broadcast(): return lax.psum(kept, axis)  91 us
    all_gather x1, waiting for transfers between devices, per_device(): whole = lax.all_gather(piece, 'dp', axis=0, tiled=True)  39 us
    psum x1, waiting for transfers between devices, per_device(): summed = lax.psum(local, 'outer')  29.3 us
    dot_general x2, matrix products, newton_steps(): mixed = jnp.dot(matrix, polynomial, preferred_element_type=jnp.float32)  5.26 us
    all_gather x1, blocking collectives, per_device(): gathered = lax.all_gather(mine, 'outer', axis=0, tiled=True)  5.1 us
    dot_general x2, matrix products, gram_product(): lax.dot_general(matrix, matrix, (((0,), (0,)), ((), ())), preferred_eleme...  4 us
  transfers between devices with their start and end apart: 3, of which 3 were waited for; matrix products, arithmetic and copies ran while one was open for 0% of the time, Pallas kernels for 0%

commit v1 on v0

v1 whole, which is shorter than its diff:
```python
import functools
import math

import jax
import jax.numpy as jnp
from jax import lax
from jax.experimental import pallas as pl
from jax.experimental.pallas import tpu as pltpu
from jax.sharding import PartitionSpec as P

ITERS = 2

coef_a = 3.4445
coef_b = -4.775
coef_c = 2.0315
momentum_rate = 0.95
epsilon = 1e-06

BF16 = jnp.bfloat16
F32 = jnp.float32
VMEM = pl.BlockSpec(memory_space=pltpu.VMEM)
SMEM = pl.BlockSpec(memory_space=pltpu.SMEM)
PARAMS = pltpu.CompilerParams(vmem_limit_bytes=40 * 1024 * 1024)


def dot(left, right):
    return jnp.dot(left, right, preferred_element_type=F32)


def gram_product(matrix):
    return lax.dot_general(matrix, matrix, (((0,), (0,)), ((), ())), preferred_element_type=F32)


def trace_of(gram):
    size = gram.shape[0]
    total = jnp.zeros((1, 1), F32)
    for at in range(0, size, 128):
        part = min(128, size - at)
        block = gram[at : at + part, at : at + part]
        row = lax.broadcasted_iota(jnp.int32, (part, part), 0)
        column = lax.broadcasted_iota(jnp.int32, (part, part), 1)
        total = total + jnp.sum(jnp.where(row == column, block, 0.0), keepdims=True)
    return total


def own_rows(gram_raw, rows):
    inverse = 1.0 / (jnp.sqrt(trace_of(gram_raw)) + epsilon)
    gram = (gram_raw * (inverse * inverse)).astype(BF16)
    polynomial = (coef_b * gram.astype(F32) + coef_c * dot(gram, gram)).astype(BF16)

    def by_q(value):
        return coef_a * value.astype(F32) + dot(value, polynomial)

    def by_second_gram(value):
        return by_q(dot(by_q(value).astype(BF16), gram).astype(BF16)).astype(BF16)

    start = (rows.astype(F32) * inverse).astype(BF16)
    first = by_q(start)
    once = by_second_gram(first.astype(BF16))
    twice = by_second_gram(once)
    return coef_a * first + coef_b * once.astype(F32) + coef_c * twice.astype(F32)


def finish_kernel(rows_ref, *refs):
    blocks, out_ref, held = refs[:-2], refs[-2], refs[-1]
    at = 0
    for block in blocks:
        held[at : at + block.shape[0], :] = block[...]
        at += block.shape[0]
    out_ref[...] = own_rows(gram_product(held[...]), rows_ref[...]).astype(BF16)


def finish(rows, blocks):
    height = sum(block.shape[0] for block in blocks)
    width = rows.shape[1]
    return pl.pallas_call(
        finish_kernel,
        out_shape=jax.ShapeDtypeStruct(rows.shape, BF16),
        in_specs=[VMEM] * (1 + len(blocks)),
        out_specs=VMEM,
        scratch_shapes=[pltpu.VMEM((height, width), BF16)],
        compiler_params=PARAMS,
    )(rows, *blocks)


def exchange(value, axis, distance):
    size = lax.axis_size(axis)
    return lax.ppermute(value, axis, [(at, at ^ distance) for at in range(size)])


def gather_blocks(block):
    size = lax.axis_size("dp")
    if size != 16:
        return [lax.all_gather(block, "dp", axis=0, tiled=True)]
    z2 = exchange(block, "dp", 8)
    z1 = exchange(block, "dp", 4)
    y0 = exchange(block, "dp", 2)
    z3 = exchange(z2, "dp", 4)
    y1 = exchange(z1, "dp", 2)
    y2 = exchange(z2, "dp", 2)
    y3 = exchange(z3, "dp", 2)
    mine = [block, y0, z1, z2, y1, z3, y2, y3]
    return mine + [exchange(value, "dp", 1) for value in mine]


def two_pods(local, momentum):
    pod = lax.axis_index("outer")
    update_scale = 0.2 * math.sqrt(max(local.shape[1] * lax.axis_size("dp"), local.shape[2]))
    first = pod == 0

    def pick(array, other=False):
        return jnp.where(first != other, array[0], array[1])

    away = pick(local, True).astype(BF16)
    kept = pick(local).astype(BF16)
    arrived = exchange(away, "outer", 1)
    summed = kept.astype(F32) + arrived.astype(F32)
    mine_new = momentum_rate * pick(momentum) + summed
    steering = (summed + momentum_rate * mine_new).astype(BF16)

    arrived_too = exchange(kept, "outer", 1)
    other_new = momentum_rate * pick(momentum, True) + (away.astype(F32) + arrived_too.astype(F32))
    momentum_new = jnp.where(first, jnp.stack([mine_new, other_new]), jnp.stack([other_new, mine_new]))

    mine = finish(steering, gather_blocks(steering))
    other = exchange(mine, "outer", 1)
    both = jnp.where(first, jnp.stack([mine, other]), jnp.stack([other, mine]))
    return momentum_new, update_scale * both.astype(F32)


def any_pods(local, momentum):
    pods = lax.axis_size("outer")
    pod = lax.axis_index("outer")
    count, rows, width = local.shape
    per_pod = count // pods
    update_scale = 0.2 * math.sqrt(max(rows * lax.axis_size("dp"), width))
    summed = lax.psum(local, "outer")
    momentum_new = momentum_rate * momentum + summed
    steering = summed + momentum_rate * momentum_new
    steering = lax.dynamic_slice_in_dim(steering, pod * per_pod, per_pod, 0).astype(BF16)
    mine = jnp.stack([finish(steering[at], gather_blocks(steering[at])) for at in range(per_pod)])
    gathered = lax.all_gather(mine, "outer", axis=0, tiled=True)
    return momentum_new, update_scale * gathered.astype(F32)


def per_device(grads, momentum):
    local = grads[0]
    if lax.axis_size("outer") == 2 and local.shape[0] == 2:
        return two_pods(local, momentum)
    return any_pods(local, momentum)


def solution(mesh):
    in_specs = (P("outer", None, "dp", None), P(None, "dp", None))
    out_specs = (P(None, "dp", None), P(None, "dp", None))
    return jax.shard_map(
        per_device, mesh=mesh, in_specs=in_specs, out_specs=out_specs, check_vma=False
    )
```

time: 199 us -> 36 us (0.18)
  waiting for transfers between devices: 160 us -> 11.4 us
  starting transfers between devices: 0.12 us -> 15.8 us
  between operations: 14.5 us -> 0.72 us
  matrix products: 9.26 us -> 0 us
  blocking collectives: 5.1 us -> 0 us
  Pallas kernels: 0 us -> 4.07 us
  other arithmetic: 7.67 us -> 3.83 us
  local copies, waits for them, and re-layouts: 2.25 us -> 0.01 us
    psum x2 -> x0, waiting for transfers between devices: 120 us -> none  [the longest x1 91 us: broadcast(): return lax.psum(kept, axis)]
    all_gather x1 -> x0, waiting for transfers between devices: 39 us -> none  [per_device(): whole = lax.all_gather(piece, 'dp', axis=0, tiled=True)]
    ppermute x0 -> x18, starting transfers between devices: none -> 15.8 us  [exchange(): lax.ppermute(value, axis, [(at, at ^ distance) for at in range(size)])]
    ppermute x0 -> x18, waiting for transfers between devices: none -> 11.4 us  [exchange(): lax.ppermute(value, axis, [(at, at ^ distance) for at in range(size)])]
    dot_general x4 -> x0, matrix products: 9.26 us -> none  [the longest x2 5.26 us: newton_steps(): mixed = jnp.dot(matrix, polynomial, preferred_element_type=jnp.float32)]
    all_gather x1 -> x0, blocking collectives: 5.1 us -> none  [per_device(): gathered = lax.all_gather(mine, 'outer', axis=0, tiled=True)]
    pallas_call x0 -> x1, Pallas kernels: none -> 4.07 us  [finish(): pl.pallas_call(finish_kernel, out_shape=jax.ShapeDtypeStruct(rows.shape,...]
    reduce_sum x1 -> x0, other arithmetic: 2.7 us -> none  [per_device(): norm_value = jnp.sqrt(jnp.sum(values * values))]
  transfers between devices with their start and end apart: 3 -> 18, of which waited for: 3 -> 9; matrix products, arithmetic and copies ran while one was open for 0% -> 2% of each run, Pallas kernels for 0% -> 0%
where the time goes in v1:
time: 36 us; the launch traced here: 35.8 us
  starting transfers between devices  15.8 us (44%)
  waiting for transfers between devices  11.4 us (32%)
  Pallas kernels  4.07 us (11%)
  other arithmetic  3.83 us (11%)
  between operations  0.72 us (2%)
    ppermute x18, starting transfers between devices, exchange(): lax.ppermute(value, axis, [(at, at ^ distance) for at in range(size)])  15.8 us
    ppermute x18, waiting for transfers between devices, exchange(): lax.ppermute(value, axis, [(at, at ^ distance) for at in range(size)])  11.4 us
    pallas_call x1, Pallas kernels, finish(): pl.pallas_call(finish_kernel, out_shape=jax.ShapeDtypeStruct(rows.shape,...  4.07 us
    convert_element_type x1, other arithmetic, two_pods(): steering = (summed + momentum_rate * mine_new).astype(BF16)  1.21 us
    convert_element_type x1, other arithmetic, two_pods(): away = pick(local, True).astype(BF16)  1.02 us
    mul x1, other arithmetic, two_pods(): return (momentum_new, update_scale * both.astype(F32))  0.78 us
    select_n x1, other arithmetic, two_pods(): jnp.where(first, jnp.stack([mine_new, other_new]), jnp.stack([other_new,...  0.75 us
  transfers between devices with their start and end apart: 18, of which 9 were waited for; matrix products, arithmetic and copies ran while one was open for 2% of the time, Pallas kernels for 0%

profile of v1, /device:TPU:0, one launch (start us, length us, event | category | flops | bytes accessed | tf_op | source)
XLA Modules:
  0.0 35.8 jit_solution(16069699287030683866)
XLA Ops:
  0.6 1.0 %fusion.2 = bf16[64,576]{1,0:T(8,128)(2,1)S(1)} fusion(f32[1,2,64,576]{3,2,1,0:T(8,128)} %param.2, pred[]{:T(512)S(6)} %ne.4), kind=kLoop, calls=%fused_computation.11 | loop fusion | flops 36864 | bytes 221185 | tf_op jit(solution)/shard_map/convert_element_type | solution.py:114
  1.7 0.0 copy-start
  1.7 0.0 copy-start.1
  1.7 3.0 %collective-permute-start = (bf16[64,576]{1,0:T(8,128)(2,1)S(1)}, bf16[64,576]{1,0:T(8,128)(2,1)S(1)}, u32[]{:S(2)}, u32[]{:S(2)}) collective-permute-start(bf16[64,576]{1,0:T(8,128)(2,1)S(1)} %fusion.2), channel_id=1, source_target_pairs={{0,16},{16,0},{1,17},{17,1},{2,18},{18,2},{3,19},{19,3},{4,20},{20... | collective-permute-start | bytes 221192 | tf_op jit(solution)/shard_map/ppermute | solution.py:88
  4.7 2.4 %collective-permute-done = bf16[64,576]{1,0:T(8,128)(2,1)S(1)} collective-permute-done((bf16[64,576]{1,0:T(8,128)(2,1)S(1)}, bf16[64,576]{1,0:T(8,128)(2,1)S(1)}, u32[]{:S(2)}, u32[]{:S(2)}) %collective-permute-start) | collective-permute-done | bytes 73760 | tf_op jit(solution)/shard_map/ppermute | solution.py:88
  7.1 1.2 %add_convert_fusion = (bf16[64,576]{1,0:T(8,128)(2,1)S(1)}, bf16[64,576]{1,0:T(8,128)(2,1)S(1)}) fusion(bf16[64,576]{1,0:T(8,128)(2,1)S(1)} %collective-permute-done, f32[2,64,576]{2,1,0:T(8,128)} %param.3, pred[]{:T(512)S(6)} %eq.3, f32[1,2,64,576]{3,2,1,0:T(8,128)} %param.2), kind=kLoop, calls=%fused_computation.6 | loop fusion | flops 368640 | bytes 664576 | tf_op jit(solution)/shard_map/convert_element_type | solution.py:119
  8.3 3.2 %collective-permute-start.4 = (bf16[64,576]{1,0:T(8,128)(2,1)S(1)}, bf16[64,576]{1,0:T(8,128)(2,1)S(1)}, u32[]{:S(2)}, u32[]{:S(2)}) collective-permute-start(bf16[64,576]{1,0:T(8,128)(2,1)S(1)} %get-tuple-element.2.rows_ref.refs_0_), channel_id=1, source_target_pairs={{0,8},{1,9},{2,10},{3,11},{4,12},{5,13},{6,14},{7,15},{8,0},{9,1},... | collective-permute-start | bytes 221192 | tf_op jit(solution)/shard_map/ppermute | solution.py:88
  11.5 1.6 %collective-permute-start.3 = (bf16[64,576]{1,0:T(8,128)(2,1)S(1)}, bf16[64,576]{1,0:T(8,128)(2,1)S(1)}, u32[]{:S(2)}, u32[]{:S(2)}) collective-permute-start(bf16[64,576]{1,0:T(8,128)(2,1)S(1)} %get-tuple-element.2.rows_ref.refs_0_), channel_id=1, source_target_pairs={{0,4},{1,5},{2,6},{3,7},{4,0},{5,1},{6,2},{7,3},{8,12},{9,13},{10,... | collective-permute-start | bytes 221192 | tf_op jit(solution)/shard_map/ppermute | solution.py:88
  13.1 1.5 %collective-permute-start.2 = (bf16[64,576]{1,0:T(8,128)(2,1)S(1)}, bf16[64,576]{1,0:T(8,128)(2,1)S(1)}, u32[]{:S(2)}, u32[]{:S(2)}) collective-permute-start(bf16[64,576]{1,0:T(8,128)(2,1)S(1)} %get-tuple-element.2.rows_ref.refs_0_), channel_id=1, source_target_pairs={{0,2},{1,3},{2,0},{3,1},{4,6},{5,7},{6,4},{7,5},{8,10},{9,11},{10,... | collective-permute-start | bytes 221192 | tf_op jit(solution)/shard_map/ppermute | solution.py:88
  14.6 0.0 collective-permute-start.9
  14.6 1.5 %collective-permute-start.1 = (bf16[64,576]{1,0:T(8,128)(2,1)S(1)}, bf16[64,576]{1,0:T(8,128)(2,1)S(1)}, u32[]{:S(2)}, u32[]{:S(2)}) collective-permute-start(bf16[64,576]{1,0:T(8,128)(2,1)S(1)} %get-tuple-element.3), channel_id=1, source_target_pairs={{0,16},{16,0},{1,17},{17,1},{2,18},{18,2},{3,19},{19,3},{4,20},{20... | collective-permute-start | bytes 221192 | tf_op jit(solution)/shard_map/ppermute | solution.py:88
  16.1 0.0 collective-permute-done.4.refs_3_
  16.1 0.5 %collective-permute-start.6 = (bf16[64,576]{1,0:T(8,128)(2,1)S(1)}, bf16[64,576]{1,0:T(8,128)(2,1)S(1)}, u32[]{:S(2)}, u32[]{:S(2)}) collective-permute-start(bf16[64,576]{1,0:T(8,128)(2,1)S(1)} %collective-permute-done.4.refs_3_), channel_id=1, source_target_pairs={{0,4},{1,5},{2,6},{3,7},{4,0},{5,1},{6,2},{7,3},{8,12},{9,13},{10,... | collective-permute-start | bytes 221192 | tf_op jit(solution)/shard_map/ppermute | solution.py:88
  16.5 0.9 %collective-permute-start.7 = (bf16[64,576]{1,0:T(8,128)(2,1)S(1)}, bf16[64,576]{1,0:T(8,128)(2,1)S(1)}, u32[]{:S(2)}, u32[]{:S(2)}) collective-permute-start(bf16[64,576]{1,0:T(8,128)(2,1)S(1)} %collective-permute-done.4.refs_3_), channel_id=1, source_target_pairs={{0,2},{1,3},{2,0},{3,1},{4,6},{5,7},{6,4},{7,5},{8,10},{9,11},{10,... | collective-permute-start | bytes 221192 | tf_op jit(solution)/shard_map/ppermute | solution.py:88
  17.5 0.1 collective-permute-done.2.refs_1_
  17.5 1.5 %collective-permute-start.5 = (bf16[64,576]{1,0:T(8,128)(2,1)S(1)}, bf16[64,576]{1,0:T(8,128)(2,1)S(1)}, u32[]{:S(2)}, u32[]{:S(2)}) collective-permute-start(bf16[64,576]{1,0:T(8,128)(2,1)S(1)} %collective-permute-done.3.refs_2_), channel_id=1, source_target_pairs={{0,2},{1,3},{2,0},{3,1},{4,6},{5,7},{6,4},{7,5},{8,10},{9,11},{10,... | collective-permute-start | bytes 221192 | tf_op jit(solution)/shard_map/ppermute | solution.py:88
  19.0 0.4 %collective-permute-done.1 = bf16[64,576]{1,0:T(8,128)(2,1)S(1)} collective-permute-done((bf16[64,576]{1,0:T(8,128)(2,1)S(1)}, bf16[64,576]{1,0:T(8,128)(2,1)S(1)}, u32[]{:S(2)}, u32[]{:S(2)}) %collective-permute-start.1) | collective-permute-done | bytes 73760 | tf_op jit(solution)/shard_map/ppermute | solution.py:88
  19.5 0.1 collective-permute-start.11
  19.6 1.1 %collective-permute-done.6.refs_5_ = bf16[64,576]{1,0:T(8,128)(2,1)S(1)} collective-permute-done((bf16[64,576]{1,0:T(8,128)(2,1)S(1)}, bf16[64,576]{1,0:T(8,128)(2,1)S(1)}, u32[]{:S(2)}, u32[]{:S(2)}) %collective-permute-start.6) | collective-permute-done | bytes 73760 | tf_op jit(solution)/shard_map/ppermute | solution.py:88
  20.7 0.5 %collective-permute-start.8 = (bf16[64,576]{1,0:T(8,128)(2,1)S(1)}, bf16[64,576]{1,0:T(8,128)(2,1)S(1)}, u32[]{:S(2)}, u32[]{:S(2)}) collective-permute-start(bf16[64,576]{1,0:T(8,128)(2,1)S(1)} %collective-permute-done.6.refs_5_), channel_id=1, source_target_pairs={{0,2},{1,3},{2,0},{3,1},{4,6},{5,7},{6,4},{7,5},{8,10},{9,11},{10,... | collective-permute-start | bytes 221192 | tf_op jit(solution)/shard_map/ppermute | solution.py:88
  21.2 0.5 %collective-permute-done.7.refs_6_ = bf16[64,576]{1,0:T(8,128)(2,1)S(1)} collective-permute-done((bf16[64,576]{1,0:T(8,128)(2,1)S(1)}, bf16[64,576]{1,0:T(8,128)(2,1)S(1)}, u32[]{:S(2)}, u32[]{:S(2)}) %collective-permute-start.7) | collective-permute-done | bytes 73760 | tf_op jit(solution)/shard_map/ppermute | solution.py:88
  21.7 0.9 %collective-permute-done.5.refs_4_ = bf16[64,576]{1,0:T(8,128)(2,1)S(1)} collective-permute-done((bf16[64,576]{1,0:T(8,128)(2,1)S(1)}, bf16[64,576]{1,0:T(8,128)(2,1)S(1)}, u32[]{:S(2)}, u32[]{:S(2)}) %collective-permute-start.5) | collective-permute-done | bytes 73760 | tf_op jit(solution)/shard_map/ppermute | solution.py:88
  22.6 0.5 %collective-permute-start.15 = (bf16[64,576]{1,0:T(8,128)(2,1)S(1)}, bf16[64,576]{1,0:T(8,128)(2,1)S(1)}, u32[]{:S(2)}, u32[]{:S(2)}) collective-permute-start(bf16[64,576]{1,0:T(8,128)(2,1)S(1)} %collective-permute-done.7.refs_6_), channel_id=1, source_target_pairs={{0,1},{1,0},{2,3},{3,2},{4,5},{5,4},{6,7},{7,6},{8,9},{9,8},{10,11... | collective-permute-start | bytes 221192 | tf_op jit(solution)/shard_map/ppermute | solution.py:88
  23.1 0.1 collective-permute-start.13
  23.2 1.9 %collective-permute-done.8.refs_7_ = bf16[64,576]{1,0:T(8,128)(2,1)S(1)} collective-permute-done((bf16[64,576]{1,0:T(8,128)(2,1)S(1)}, bf16[64,576]{1,0:T(8,128)(2,1)S(1)}, u32[]{:S(2)}, u32[]{:S(2)}) %collective-permute-start.8) | collective-permute-done | bytes 73760 | tf_op jit(solution)/shard_map/ppermute | solution.py:88
  25.1 0.1 fusion.3
  25.2 1.1 %collective-permute-done.16.refs_15_ = bf16[64,576]{1,0:T(8,128)(2,1)S(1)} collective-permute-done((bf16[64,576]{1,0:T(8,128)(2,1)S(1)}, bf16[64,576]{1,0:T(8,128)(2,1)S(1)}, u32[]{:S(2)}, u32[]{:S(2)}) %collective-permute-start.16) | collective-permute-done | bytes 73760 | tf_op jit(solution)/shard_map/ppermute | solution.py:88
  26.4 4.1 %shard_map.41 = bf16[64,576]{1,0:T(8,128)(2,1)S(1)} custom-call(bf16[64,576]{1,0:T(8,128)(2,1)S(1)} %get-tuple-element.2.rows_ref.refs_0_, bf16[64,576]{1,0:T(8,128)(2,1)S(1)} %get-tuple-element.2.rows_ref.refs_0_, bf16[64,576]{1,0:T(8,128)(2,1)S(1)} %collective-permute-done.2.refs_1_, bf16[64,576]{1,0:T(8,128)(2,1)S(1)} %collective-permute-done.3.refs_2_, ...), custom_call_target="tpu_custom_call" | custom-call | tf_op jit(solution)/shard_map/pallas_call | solution.py:76
  30.5 0.9 %collective-permute-start.17 = (bf16[64,576]{1,0:T(8,128)(2,1)S(1)}, bf16[64,576]{1,0:T(8,128)(2,1)S(1)}, u32[]{:S(2)}, u32[]{:S(2)}) collective-permute-start(bf16[64,576]{1,0:T(8,128)(2,1)S(1)} %shard_map.41), channel_id=1, source_target_pairs={{0,16},{16,0},{1,17},{17,1},{2,18},{18,2},{3,19},{19,3},{4,20},{20... | collective-permute-start | bytes 221192 | tf_op jit(solution)/shard_map/ppermute | solution.py:88
  31.4 0.7 %maximum_select_fusion = f32[2,64,576]{2,1,0:T(8,128)} fusion(f32[1,64,576]{2,1,0:T(8,128)S(1)} %get-tuple-element.5, f32[1,64,576]{2,1,0:T(8,128)S(1)} %get-tuple-element.4, pred[]{:T(512)S(6)} %eq.3), kind=kLoop, calls=%fused_computation | loop fusion | flops 221184 | bytes 589825 | tf_op jit(solution)/shard_map/jit(_where)/select_n | solution.py:123
  32.1 2.9 %collective-permute-done.17 = bf16[64,576]{1,0:T(8,128)(2,1)S(1)} collective-permute-done((bf16[64,576]{1,0:T(8,128)(2,1)S(1)}, bf16[64,576]{1,0:T(8,128)(2,1)S(1)}, u32[]{:S(2)}, u32[]{:S(2)}) %collective-permute-start.17) | collective-permute-done | bytes 73760 | tf_op jit(solution)/shard_map/ppermute | solution.py:88
  35.0 0.8 %convert_multiply_fusion = f32[2,64,576]{2,1,0:T(8,128)} fusion(bf16[1,64,576]{2,1,0:T(8,128)(2,1)S(1)} %bitcast.24, bf16[1,64,576]{2,1,0:T(8,128)(2,1)S(1)} %bitcast.23, pred[]{:T(512)S(6)} %eq.3), kind=kLoop, calls=%fused_computation.1 | loop fusion | flops 368640 | bytes 442369 | tf_op jit(solution)/shard_map/mul | solution.py:128
  (14 shorter events, 0.0 us)
Async XLA Ops:
  1.7 23.5 %copy-start = (f32[2,64,576]{2,1,0:T(8,128)S(1)}, f32[2,64,576]{2,1,0:T(8,128)}, u32[]{:S(2)}) copy-start(f32[2,64,576]{2,1,0:T(8,128)} %param.3) | copy-start | bytes 884740
  1.7 23.5 %copy-start.1 = (f32[1,2,64,576]{3,2,1,0:T(8,128)S(1)}, f32[1,2,64,576]{3,2,1,0:T(8,128)}, u32[]{:S(2)}) copy-start(f32[1,2,64,576]{3,2,1,0:T(8,128)} %param.2) | copy-start | bytes 884740
  1.7 5.4 %collective-permute-start = (bf16[64,576]{1,0:T(8,128)(2,1)S(1)}, bf16[64,576]{1,0:T(8,128)(2,1)S(1)}, u32[]{:S(2)}, u32[]{:S(2)}) collective-permute-start(bf16[64,576]{1,0:T(8,128)(2,1)S(1)} %fusion.2), channel_id=1, source_target_pairs={{0,16},{16,0},{1,17},{17,1},{2,18},{18,2},{3,19},{19,3},{4,20},{20... | collective-permute-start | bytes 221192 | tf_op jit(solution)/shard_map/ppermute | solution.py:88
  8.3 7.8 %collective-permute-start.4 = (bf16[64,576]{1,0:T(8,128)(2,1)S(1)}, bf16[64,576]{1,0:T(8,128)(2,1)S(1)}, u32[]{:S(2)}, u32[]{:S(2)}) collective-permute-start(bf16[64,576]{1,0:T(8,128)(2,1)S(1)} %get-tuple-element.2.rows_ref.refs_0_), channel_id=1, source_target_pairs={{0,8},{1,9},{2,10},{3,11},{4,12},{5,13},{6,14},{7,15},{8,0},{9,1},... | collective-permute-start | bytes 221192 | tf_op jit(solution)/shard_map/ppermute | solution.py:88
  11.5 5.0 %collective-permute-start.3 = (bf16[64,576]{1,0:T(8,128)(2,1)S(1)}, bf16[64,576]{1,0:T(8,128)(2,1)S(1)}, u32[]{:S(2)}, u32[]{:S(2)}) collective-permute-start(bf16[64,576]{1,0:T(8,128)(2,1)S(1)} %get-tuple-element.2.rows_ref.refs_0_), channel_id=1, source_target_pairs={{0,4},{1,5},{2,6},{3,7},{4,0},{5,1},{6,2},{7,3},{8,12},{9,13},{10,... | collective-permute-start | bytes 221192 | tf_op jit(solution)/shard_map/ppermute | solution.py:88
  13.1 4.4 %collective-permute-start.2 = (bf16[64,576]{1,0:T(8,128)(2,1)S(1)}, bf16[64,576]{1,0:T(8,128)(2,1)S(1)}, u32[]{:S(2)}, u32[]{:S(2)}) collective-permute-start(bf16[64,576]{1,0:T(8,128)(2,1)S(1)} %get-tuple-element.2.rows_ref.refs_0_), channel_id=1, source_target_pairs={{0,2},{1,3},{2,0},{3,1},{4,6},{5,7},{6,4},{7,5},{8,10},{9,11},{10,... | collective-permute-start | bytes 221192 | tf_op jit(solution)/shard_map/ppermute | solution.py:88
  14.6 4.4 %collective-permute-start.9 = (bf16[64,576]{1,0:T(8,128)(2,1)S(1)}, bf16[64,576]{1,0:T(8,128)(2,1)S(1)}, u32[]{:S(2)}, u32[]{:S(2)}) collective-permute-start(bf16[64,576]{1,0:T(8,128)(2,1)S(1)} %get-tuple-element.2.rows_ref.refs_0_), channel_id=1, source_target_pairs={{0,1},{1,0},{2,3},{3,2},{4,5},{5,4},{6,7},{7,6},{8,9},{9,8},{10,11... | collective-permute-start | bytes 221192 | tf_op jit(solution)/shard_map/ppermute | solution.py:88
  14.6 4.9 %collective-permute-start.1 = (bf16[64,576]{1,0:T(8,128)(2,1)S(1)}, bf16[64,576]{1,0:T(8,128)(2,1)S(1)}, u32[]{:S(2)}, u32[]{:S(2)}) collective-permute-start(bf16[64,576]{1,0:T(8,128)(2,1)S(1)} %get-tuple-element.3), channel_id=1, source_target_pairs={{0,16},{16,0},{1,17},{17,1},{2,18},{18,2},{3,19},{19,3},{4,20},{20... | collective-permute-start | bytes 221192 | tf_op jit(solution)/shard_map/ppermute | solution.py:88
  16.1 4.6 %collective-permute-start.6 = (bf16[64,576]{1,0:T(8,128)(2,1)S(1)}, bf16[64,576]{1,0:T(8,128)(2,1)S(1)}, u32[]{:S(2)}, u32[]{:S(2)}) collective-permute-start(bf16[64,576]{1,0:T(8,128)(2,1)S(1)} %collective-permute-done.4.refs_3_), channel_id=1, source_target_pairs={{0,4},{1,5},{2,6},{3,7},{4,0},{5,1},{6,2},{7,3},{8,12},{9,13},{10,... | collective-permute-start | bytes 221192 | tf_op jit(solution)/shard_map/ppermute | solution.py:88
  16.5 5.2 %collective-permute-start.7 = (bf16[64,576]{1,0:T(8,128)(2,1)S(1)}, bf16[64,576]{1,0:T(8,128)(2,1)S(1)}, u32[]{:S(2)}, u32[]{:S(2)}) collective-permute-start(bf16[64,576]{1,0:T(8,128)(2,1)S(1)} %collective-permute-done.4.refs_3_), channel_id=1, source_target_pairs={{0,2},{1,3},{2,0},{3,1},{4,6},{5,7},{6,4},{7,5},{8,10},{9,11},{10,... | collective-permute-start | bytes 221192 | tf_op jit(solution)/shard_map/ppermute | solution.py:88
  17.5 5.1 %collective-permute-start.5 = (bf16[64,576]{1,0:T(8,128)(2,1)S(1)}, bf16[64,576]{1,0:T(8,128)(2,1)S(1)}, u32[]{:S(2)}, u32[]{:S(2)}) collective-permute-start(bf16[64,576]{1,0:T(8,128)(2,1)S(1)} %collective-permute-done.3.refs_2_), channel_id=1, source_target_pairs={{0,2},{1,3},{2,0},{3,1},{4,6},{5,7},{6,4},{7,5},{8,10},{9,11},{10,... | collective-permute-start | bytes 221192 | tf_op jit(solution)/shard_map/ppermute | solution.py:88
  19.0 3.6 %collective-permute-start.12 = (bf16[64,576]{1,0:T(8,128)(2,1)S(1)}, bf16[64,576]{1,0:T(8,128)(2,1)S(1)}, u32[]{:S(2)}, u32[]{:S(2)}) collective-permute-start(bf16[64,576]{1,0:T(8,128)(2,1)S(1)} %collective-permute-done.4.refs_3_), channel_id=1, source_target_pairs={{0,1},{1,0},{2,3},{3,2},{4,5},{5,4},{6,7},{7,6},{8,9},{9,8},{10,11... | collective-permute-start | bytes 221192 | tf_op jit(solution)/shard_map/ppermute | solution.py:88
  19.5 3.7 %collective-permute-start.11 = (bf16[64,576]{1,0:T(8,128)(2,1)S(1)}, bf16[64,576]{1,0:T(8,128)(2,1)S(1)}, u32[]{:S(2)}, u32[]{:S(2)}) collective-permute-start(bf16[64,576]{1,0:T(8,128)(2,1)S(1)} %collective-permute-done.3.refs_2_), channel_id=1, source_target_pairs={{0,1},{1,0},{2,3},{3,2},{4,5},{5,4},{6,7},{7,6},{8,9},{9,8},{10,11... | collective-permute-start | bytes 221192 | tf_op jit(solution)/shard_map/ppermute | solution.py:88
  20.7 4.4 %collective-permute-start.8 = (bf16[64,576]{1,0:T(8,128)(2,1)S(1)}, bf16[64,576]{1,0:T(8,128)(2,1)S(1)}, u32[]{:S(2)}, u32[]{:S(2)}) collective-permute-start(bf16[64,576]{1,0:T(8,128)(2,1)S(1)} %collective-permute-done.6.refs_5_), channel_id=1, source_target_pairs={{0,2},{1,3},{2,0},{3,1},{4,6},{5,7},{6,4},{7,5},{8,10},{9,11},{10,... | collective-permute-start | bytes 221192 | tf_op jit(solution)/shard_map/ppermute | solution.py:88
  21.7 3.5 %collective-permute-start.10 = (bf16[64,576]{1,0:T(8,128)(2,1)S(1)}, bf16[64,576]{1,0:T(8,128)(2,1)S(1)}, u32[]{:S(2)}, u32[]{:S(2)}) collective-permute-start(bf16[64,576]{1,0:T(8,128)(2,1)S(1)} %collective-permute-done.2.refs_1_), channel_id=1, source_target_pairs={{0,1},{1,0},{2,3},{3,2},{4,5},{5,4},{6,7},{7,6},{8,9},{9,8},{10,11... | collective-permute-start | bytes 221192 | tf_op jit(solution)/shard_map/ppermute | solution.py:88
  22.6 2.6 %collective-permute-start.14 = (bf16[64,576]{1,0:T(8,128)(2,1)S(1)}, bf16[64,576]{1,0:T(8,128)(2,1)S(1)}, u32[]{:S(2)}, u32[]{:S(2)}) collective-permute-start(bf16[64,576]{1,0:T(8,128)(2,1)S(1)} %collective-permute-done.6.refs_5_), channel_id=1, source_target_pairs={{0,1},{1,0},{2,3},{3,2},{4,5},{5,4},{6,7},{7,6},{8,9},{9,8},{10,11... | collective-permute-start | bytes 221192 | tf_op jit(solution)/shard_map/ppermute | solution.py:88
  22.6 2.6 %collective-permute-start.15 = (bf16[64,576]{1,0:T(8,128)(2,1)S(1)}, bf16[64,576]{1,0:T(8,128)(2,1)S(1)}, u32[]{:S(2)}, u32[]{:S(2)}) collective-permute-start(bf16[64,576]{1,0:T(8,128)(2,1)S(1)} %collective-permute-done.7.refs_6_), channel_id=1, source_target_pairs={{0,1},{1,0},{2,3},{3,2},{4,5},{5,4},{6,7},{7,6},{8,9},{9,8},{10,11... | collective-permute-start | bytes 221192 | tf_op jit(solution)/shard_map/ppermute | solution.py:88
  23.1 2.1 %collective-permute-start.13 = (bf16[64,576]{1,0:T(8,128)(2,1)S(1)}, bf16[64,576]{1,0:T(8,128)(2,1)S(1)}, u32[]{:S(2)}, u32[]{:S(2)}) collective-permute-start(bf16[64,576]{1,0:T(8,128)(2,1)S(1)} %collective-permute-done.5.refs_4_), channel_id=1, source_target_pairs={{0,1},{1,0},{2,3},{3,2},{4,5},{5,4},{6,7},{7,6},{8,9},{9,8},{10,11... | collective-permute-start | bytes 221192 | tf_op jit(solution)/shard_map/ppermute | solution.py:88
  25.1 1.3 %collective-permute-start.16 = (bf16[64,576]{1,0:T(8,128)(2,1)S(1)}, bf16[64,576]{1,0:T(8,128)(2,1)S(1)}, u32[]{:S(2)}, u32[]{:S(2)}) collective-permute-start(bf16[64,576]{1,0:T(8,128)(2,1)S(1)} %collective-permute-done.8.refs_7_), channel_id=1, source_target_pairs={{0,1},{1,0},{2,3},{3,2},{4,5},{5,4},{6,7},{7,6},{8,9},{9,8},{10,11... | collective-permute-start | bytes 221192 | tf_op jit(solution)/shard_map/ppermute | solution.py:88
  30.5 4.6 %collective-permute-start.17 = (bf16[64,576]{1,0:T(8,128)(2,1)S(1)}, bf16[64,576]{1,0:T(8,128)(2,1)S(1)}, u32[]{:S(2)}, u32[]{:S(2)}) collective-permute-start(bf16[64,576]{1,0:T(8,128)(2,1)S(1)} %shard_map.41), channel_id=1, source_target_pairs={{0,16},{16,0},{1,17},{17,1},{2,18},{18,2},{3,19},{19,3},{4,20},{20... | collective-permute-start | bytes 221192 | tf_op jit(solution)/shard_map/ppermute | solution.py:88

commit v2 on v1

v2 whole, which is shorter than its diff:
```python
import functools
import math

import jax
import jax.numpy as jnp
from jax import lax
from jax.experimental import pallas as pl
from jax.experimental.pallas import tpu as pltpu
from jax.sharding import PartitionSpec as P

ITERS = 2

coef_a = 3.4445
coef_b = -4.775
coef_c = 2.0315
momentum_rate = 0.95
epsilon = 1e-06

BF16 = jnp.bfloat16
F32 = jnp.float32
VMEM = pl.BlockSpec(memory_space=pltpu.VMEM)
SMEM = pl.BlockSpec(memory_space=pltpu.SMEM)
PARAMS = pltpu.CompilerParams(vmem_limit_bytes=16 * 1024 * 1024)
SMALL = pltpu.CompilerParams(vmem_limit_bytes=4 * 1024 * 1024)


def dot(left, right):
    return jnp.dot(left, right, preferred_element_type=F32)


def gram_product(matrix):
    return lax.dot_general(matrix, matrix, (((0,), (0,)), ((), ())), preferred_element_type=F32)


def trace_of(gram):
    size = gram.shape[0]
    total = jnp.zeros((1, 1), F32)
    for at in range(0, size, 128):
        part = min(128, size - at)
        block = gram[at : at + part, at : at + part]
        row = lax.broadcasted_iota(jnp.int32, (part, part), 0)
        column = lax.broadcasted_iota(jnp.int32, (part, part), 1)
        total = total + jnp.sum(jnp.where(row == column, block, 0.0), keepdims=True)
    return total


def own_rows(gram_raw, rows):
    gram = gram_raw.astype(BF16)
    squared = dot(gram, gram)
    inverse = 1.0 / (jnp.sqrt(trace_of(gram_raw)) + epsilon)
    scale = inverse * inverse
    polynomial = ((coef_b * scale) * gram.astype(F32) + (coef_c * scale * scale) * squared).astype(BF16)

    def by_q(value):
        return coef_a * value.astype(F32) + dot(value, polynomial)

    def by_second_gram(value):
        return by_q((scale * dot(by_q(value).astype(BF16), gram)).astype(BF16)).astype(BF16)

    first = by_q(rows)
    once = by_second_gram(first.astype(BF16))
    twice = by_second_gram(once)
    return inverse * (coef_a * first + coef_b * once.astype(F32) + coef_c * twice.astype(F32))


def pack(value, ref, at=0):
    rows, width = value.shape
    whole = width // 128
    for tile in range(whole):
        ref[at + rows * tile : at + rows * (tile + 1), :] = value[:, 128 * tile : 128 * (tile + 1)]
    rest = value[:, 128 * whole :]
    half = rows // 2
    ref[at + rows * whole : at + rows * whole + half, :] = jnp.concatenate([rest[:half], rest[half:]], axis=1)


def unpack(ref, at, held, to, rows, width):
    whole = width // 128
    for tile in range(whole):
        part = ref[at + rows * tile : at + rows * (tile + 1), :]
        held[to : to + rows, 128 * tile : 128 * (tile + 1)] = part.astype(held.dtype)
    half = rows // 2
    rest = ref[at + rows * whole : at + rows * whole + half, :].astype(held.dtype)
    held[to : to + half, 128 * whole :] = rest[:, :64]
    held[to + half : to + rows, 128 * whole :] = rest[:, 64:]


def unpack_all(blocks, held, rows, width):
    size = rows * width // 128
    to = 0
    for block in blocks:
        for at in range(0, block.shape[0], size):
            unpack(block, at, held, to, rows, width)
            to += rows
    return held[...]


def rows_in(blocks, width):
    return sum(block.shape[0] for block in blocks) * 128 // width


def gram_kernel(rows, more, *refs):
    blocks, out_ref, held = refs[more:-2], refs[-2], refs[-1]
    gram = gram_product(unpack_all(blocks, held, rows, held.shape[1]))
    out_ref[...] = refs[0][...] + gram if more else gram


def gram_of(blocks, rows, width, so_far=None):
    before = [] if so_far is None else [so_far]
    return pl.pallas_call(
        functools.partial(gram_kernel, rows, len(before)),
        out_shape=jax.ShapeDtypeStruct((width, width), F32),
        in_specs=[VMEM] * (len(before) + len(blocks)),
        out_specs=VMEM,
        scratch_shapes=[pltpu.VMEM((rows_in(blocks, width), width), BF16)],
        compiler_params=PARAMS,
    )(*before, *blocks)


def finish_kernel(rows, sum_ref, rows_ref, *refs):
    blocks, out_ref, held, own = refs[:-3], refs[-3], refs[-2], refs[-1]
    unpack(rows_ref, 0, own, 0, rows, own.shape[1])
    gram = sum_ref[...] + gram_product(unpack_all(blocks, held, rows, held.shape[1]))
    pack(own_rows(gram, own[...]).astype(BF16), out_ref)


def finish(so_far, own, blocks, rows, width):
    return pl.pallas_call(
        functools.partial(finish_kernel, rows),
        out_shape=jax.ShapeDtypeStruct(own.shape, BF16),
        in_specs=[VMEM] * (2 + len(blocks)),
        out_specs=VMEM,
        scratch_shapes=[pltpu.VMEM((rows_in(blocks, width), width), BF16), pltpu.VMEM((rows, width), BF16)],
        compiler_params=PARAMS,
    )(so_far, own, *blocks)


def whole_kernel(rows_ref, whole_ref, out_ref):
    out_ref[...] = own_rows(gram_product(whole_ref[...]), rows_ref[...]).astype(BF16)


def whole_finish(own):
    return pl.pallas_call(
        whole_kernel,
        out_shape=jax.ShapeDtypeStruct(own.shape, BF16),
        in_specs=[VMEM] * 2,
        out_specs=VMEM,
        compiler_params=PARAMS,
    )(own, lax.all_gather(own, "dp", axis=0, tiled=True))


def join_kernel(*refs):
    at = 0
    for ref in refs[:-1]:
        refs[-1][at : at + ref.shape[0], :] = ref[...]
        at += ref.shape[0]


def join(blocks):
    height = sum(block.shape[0] for block in blocks)
    return pl.pallas_call(
        join_kernel,
        out_shape=jax.ShapeDtypeStruct((height, 128), BF16),
        in_specs=[VMEM] * len(blocks),
        out_specs=VMEM,
        compiler_params=SMALL,
    )(*blocks)


def exchange(value, axis, distance):
    size = lax.axis_size(axis)
    return lax.ppermute(value, axis, [(at, at ^ distance) for at in range(size)])


def after(value, *others):
    return lax.optimization_barrier((value, *others))[0]


def gather_and_finish(block, kept, rows, width):
    z2 = exchange(block, "dp", 8)
    z1 = exchange(block, "dp", 4)
    y0 = exchange(block, "dp", 2)
    beside = exchange(kept, "outer", 1)
    z2, beside = lax.optimization_barrier((z2, beside))
    z3 = exchange(z2, "dp", 4)
    y1 = exchange(z1, "dp", 2)
    y2 = exchange(z2, "dp", 2)
    y3 = exchange(z3, "dp", 2)
    near = [block, z1, z2]
    near = near + [exchange(v, "dp", 1) for v in near]
    gram = gram_of(near, rows, width)
    far = [y0, z3, y1, y2]
    far = far + [exchange(v, "dp", 1) for v in far]
    return finish(gram, block, far + [y3, exchange(y3, "dp", 1)], rows, width), beside


def away_kernel(grads_ref, away_ref, held, done):
    copy = pltpu.make_async_copy(grads_ref.at[1 - lax.axis_index("outer")], held, done)
    copy.start()
    copy.wait()
    pack(held[...].astype(BF16), away_ref)


def base_kernel(grads_ref, momentum_ref, kept_ref, base_ref, held, done):
    mine = lax.axis_index("outer")
    copies = [
        pltpu.make_async_copy(grads_ref.at[mine], held.at[0], done.at[0]),
        pltpu.make_async_copy(momentum_ref.at[mine], held.at[1], done.at[1]),
    ]
    for copy in copies:
        copy.start()
    for copy in copies:
        copy.wait()
    pack(held[0].astype(BF16), kept_ref)
    pack((1.0 + momentum_rate) * held[0] + (momentum_rate * momentum_rate) * held[1], base_ref)


def steering_kernel(base_ref, arrived_ref, out_ref):
    out_ref[...] = (base_ref[...] + (1.0 + momentum_rate) * arrived_ref[...].astype(F32)).astype(BF16)


def momentum_kernel(momentum_ref, kept_ref, arrived_ref, away_ref, arrived_too_ref, out_ref, held):
    mine = lax.axis_index("outer")
    rows, width = held.shape
    for at, sent, came in ((mine, kept_ref, arrived_ref), (1 - mine, away_ref, arrived_too_ref)):
        unpack(sent[...].astype(F32) + came[...].astype(F32), 0, held, 0, rows, width)
        out_ref[at] = momentum_rate * momentum_ref[at] + held[...]


def update_kernel(scale, own, rows_ref, *refs):
    out_ref, held, done = refs[-3:]
    mine = lax.axis_index("outer")
    unpack(scale * rows_ref[...].astype(F32), 0, held, 0, *held.shape)
    copy = pltpu.make_async_copy(held, out_ref.at[mine if own else 1 - mine], done)
    copy.start()
    copy.wait()


def two_pods(local, momentum):
    _, rows, width = local.shape
    update_scale = 0.2 * math.sqrt(max(rows * lax.axis_size("dp"), width))
    anywhere = pl.BlockSpec(memory_space=pl.ANY)
    one = (rows, width)
    packed = (rows * width // 128, 128)
    rounded = jax.ShapeDtypeStruct(packed, BF16)
    wide = jax.ShapeDtypeStruct(packed, F32)
    both = jax.ShapeDtypeStruct(local.shape, F32)
    away = pl.pallas_call(
        away_kernel,
        out_shape=rounded,
        in_specs=[anywhere],
        out_specs=VMEM,
        scratch_shapes=[pltpu.VMEM(one, F32), pltpu.SemaphoreType.DMA],
        compiler_params=SMALL,
    )(local)
    arrived = exchange(away, "outer", 1)
    kept, base = pl.pallas_call(
        base_kernel,
        out_shape=(rounded, wide),
        in_specs=[anywhere] * 2,
        out_specs=(VMEM, VMEM),
        scratch_shapes=[pltpu.VMEM((2,) + one, F32), pltpu.SemaphoreType.DMA((2,))],
        compiler_params=SMALL,
    )(local, momentum)
    steering = pl.pallas_call(
        steering_kernel, out_shape=rounded, in_specs=[VMEM] * 2, out_specs=VMEM, compiler_params=SMALL
    )(base, arrived)

    mine, arrived_too = gather_and_finish(steering, kept, rows, width)

    momentum_new = pl.pallas_call(
        momentum_kernel,
        out_shape=both,
        in_specs=[VMEM] * 5,
        scratch_shapes=[pltpu.VMEM(one, F32)],
        compiler_params=SMALL,
    )(momentum, kept, arrived, away, arrived_too)

    other = exchange(mine, "outer", 1)
    scratch = [pltpu.VMEM(one, F32), pltpu.SemaphoreType.DMA]
    half = pl.pallas_call(
        functools.partial(update_kernel, update_scale, True),
        out_shape=both,
        in_specs=[VMEM],
        out_specs=anywhere,
        scratch_shapes=scratch,
        compiler_params=SMALL,
    )(mine)
    update = pl.pallas_call(
        functools.partial(update_kernel, update_scale, False),
        out_shape=both,
        in_specs=[VMEM, anywhere],
        out_specs=anywhere,
        scratch_shapes=scratch,
        input_output_aliases={1: 0},
        compiler_params=SMALL,
    )(other, half)
    return momentum_new, update


def any_pods(local, momentum):
    pods = lax.axis_size("outer")
    pod = lax.axis_index("outer")
    count, rows, width = local.shape
    per_pod = count // pods
    update_scale = 0.2 * math.sqrt(max(rows * lax.axis_size("dp"), width))
    summed = lax.psum(local, "outer")
    momentum_new = momentum_rate * momentum + summed
    steering = summed + momentum_rate * momentum_new
    steering = lax.dynamic_slice_in_dim(steering, pod * per_pod, per_pod, 0).astype(BF16)
    mine = jnp.stack([whole_finish(steering[at]) for at in range(per_pod)])
    gathered = lax.all_gather(mine, "outer", axis=0, tiled=True)
    return momentum_new, update_scale * gathered.astype(F32)


def per_device(grads, momentum):
    local = grads[0]
    _, rows, width = local.shape
    halves = width % 128 == 64 and rows % 32 == 0
    if lax.axis_size("outer") == 2 and local.shape[0] == 2 and lax.axis_size("dp") == 16 and halves:
        return two_pods(local, momentum)
    return any_pods(local, momentum)


def solution(mesh):
    in_specs = (P("outer", None, "dp", None), P(None, "dp", None))
    out_specs = (P(None, "dp", None), P(None, "dp", None))
    return jax.shard_map(
        per_device, mesh=mesh, in_specs=in_specs, out_specs=out_specs, check_vma=False
    )
```

time: 36 us -> 32.2 us (0.89)
  waiting for transfers between devices: 11.4 us -> 5.71 us
  other arithmetic: 3.83 us -> 0 us
  Pallas kernels: 4.07 us -> 6.73 us
  local copies, waits for them, and re-layouts: 0.01 us -> 1.94 us
  starting transfers between devices: 15.8 us -> 16.9 us
    ppermute x18, waiting for transfers between devices: 11.4 us -> 5.71 us  [exchange(): lax.ppermute(value, axis, [(at, at ^ distance) for at in range(size)])]
    pallas_call x1 -> x8, Pallas kernels: 4.07 us -> 6.73 us  [the longest x1 2.93 us: finish(): pl.pallas_call(functools.partial(finish_kernel, rows), out_shape=jax.Shap...]
    convert_element_type x2 -> x0, other arithmetic: 2.22 us -> none  [the longest x1 1.21 us: two_pods(): steering = (summed + momentum_rate * mine_new).astype(BF16)]
    unnamed x4 -> x6, local copies, waits for them, and re-layouts: 0.01 us -> 1.94 us
    ppermute x18, starting transfers between devices: 15.8 us -> 16.9 us  [exchange(): lax.ppermute(value, axis, [(at, at ^ distance) for at in range(size)])]
    mul x1 -> x0, other arithmetic: 0.78 us -> none  [two_pods(): return (momentum_new, update_scale * both.astype(F32))]
    select_n x1 -> x0, other arithmetic: 0.75 us -> none  [two_pods(): jnp.where(first, jnp.stack([mine_new, other_new]), jnp.stack([other_new,...]
  transfers between devices with their start and end apart: 18 -> 18, of which waited for: 9 -> 7; matrix products, arithmetic and copies ran while one was open for 2% -> 0% of each run, Pallas kernels for 0% -> 9%
where the time goes in v2:
time: 32.2 us; the launch traced here: 32 us
  starting transfers between devices  16.9 us (52%)
  Pallas kernels  6.73 us (21%)
  waiting for transfers between devices  5.71 us (18%)
  local copies, waits for them, and re-layouts  1.94 us (6%)
  between operations  0.73 us (2%)
    ppermute x18, starting transfers between devices, exchange(): lax.ppermute(value, axis, [(at, at ^ distance) for at in range(size)])  16.9 us
    ppermute x18, waiting for transfers between devices, exchange(): lax.ppermute(value, axis, [(at, at ^ distance) for at in range(size)])  5.71 us
    pallas_call x1, Pallas kernels, finish(): pl.pallas_call(functools.partial(finish_kernel, rows), out_shape=jax.Shap...  2.93 us
    unnamed x6, local copies, waits for them, and re-layouts  1.94 us
    pallas_call x1, Pallas kernels, two_pods(): pl.pallas_call(momentum_kernel, out_shape=both, in_specs=[VMEM] * 5, scra...  0.81 us
    pallas_call x1, Pallas kernels, two_pods(): pl.pallas_call(functools.partial(update_kernel, update_scale, False), out...  0.76 us
    pallas_call x1, Pallas kernels, two_pods(): pl.pallas_call(functools.partial(update_kernel, update_scale, True), out_...  0.76 us
    pallas_call x1, Pallas kernels, gram_of(): pl.pallas_call(functools.partial(gram_kernel, rows, len(before)), out_sha...  0.68 us
  transfers between devices with their start and end apart: 18, of which 7 were waited for; matrix products, arithmetic and copies ran while one was open for 0% of the time, Pallas kernels for 9%

profile of v2, /device:TPU:0, one launch (start us, length us, event | category | flops | bytes accessed | tf_op | source)
XLA Modules:
  0.0 32.0 jit_solution(6040020020333264642)
XLA Ops:
  0.6 1.0 %copy-done = f32[1,2,64,576]{3,2,1,0:T(8,128)S(1)} copy-done((f32[1,2,64,576]{3,2,1,0:T(8,128)S(1)}, f32[1,2,64,576]{3,2,1,0:T(8,128)}, u32[]{:S(2)}) %copy-start) | copy-done | bytes 294936
  1.6 0.3 shard_map.42.away_ref
  1.9 3.0 %collective-permute-start = (bf16[288,128]{1,0:T(8,128)(2,1)S(1)}, bf16[288,128]{1,0:T(8,128)(2,1)S(1)}, u32[]{:S(2)}, u32[]{:S(2)}) collective-permute-start(bf16[288,128]{1,0:T(8,128)(2,1)S(1)} %shard_map.42.away_ref), channel_id=1, source_target_pairs={{0,16},{16,0},{1,17},{17,1},{2,18},{18,2},{3,19},{19,3},{4,20},{20... | collective-permute-start | bytes 221192 | tf_op jit(solution)/shard_map/ppermute | solution.py:171
  4.9 1.0 %copy-done.1 = f32[2,64,576]{2,1,0:T(8,128)S(1)} copy-done((f32[2,64,576]{2,1,0:T(8,128)S(1)}, f32[2,64,576]{2,1,0:T(8,128)}, u32[]{:S(2)}) %copy-start.1) | copy-done | bytes 294936
  5.9 0.5 %shard_map.41 = (bf16[288,128]{1,0:T(8,128)(2,1)S(1)}, f32[288,128]{1,0:T(8,128)S(1)}) custom-call(f32[2,64,576]{2,1,0:T(8,128)S(1)} %bitcast.2, f32[2,64,576]{2,1,0:T(8,128)S(1)} %copy-done.1), custom_call_target="tpu_custom_call" | custom-call | tf_op jit(solution)/shard_map/pallas_call | solution.py:256
  6.4 0.1 collective-permute-start.2
  6.4 0.8 %collective-permute-done.arrived_ref = bf16[288,128]{1,0:T(8,128)(2,1)S(1)} collective-permute-done((bf16[288,128]{1,0:T(8,128)(2,1)S(1)}, bf16[288,128]{1,0:T(8,128)(2,1)S(1)}, u32[]{:S(2)}, u32[]{:S(2)}) %collective-permute-start) | collective-permute-done | bytes 73760 | tf_op jit(solution)/shard_map/ppermute | solution.py:171
  7.2 3.2 %collective-permute-start.1 = (bf16[288,128]{1,0:T(8,128)(2,1)S(1)}, bf16[288,128]{1,0:T(8,128)(2,1)S(1)}, u32[]{:S(2)}, u32[]{:S(2)}) collective-permute-start(bf16[288,128]{1,0:T(8,128)(2,1)S(1)} %shard_map.43.refs_0_.rows_ref), channel_id=1, source_target_pairs={{0,8},{1,9},{2,10},{3,11},{4,12},{5,13},{6,14},{7,15},{8,0},{9,1},... | collective-permute-start | bytes 221192 | tf_op jit(solution)/shard_map/ppermute | solution.py:171
  10.4 1.6 %collective-permute-start.3 = (bf16[288,128]{1,0:T(8,128)(2,1)S(1)}, bf16[288,128]{1,0:T(8,128)(2,1)S(1)}, u32[]{:S(2)}, u32[]{:S(2)}) collective-permute-start(bf16[288,128]{1,0:T(8,128)(2,1)S(1)} %shard_map.43.refs_0_.rows_ref), channel_id=1, source_target_pairs={{0,4},{1,5},{2,6},{3,7},{4,0},{5,1},{6,2},{7,3},{8,12},{9,13},{10,... | collective-permute-start | bytes 221192 | tf_op jit(solution)/shard_map/ppermute | solution.py:171
  12.0 0.0 collective-permute-start.4
  12.0 1.5 %collective-permute-start.7 = (bf16[288,128]{1,0:T(8,128)(2,1)S(1)}, bf16[288,128]{1,0:T(8,128)(2,1)S(1)}, u32[]{:S(2)}, u32[]{:S(2)}) collective-permute-start(bf16[288,128]{1,0:T(8,128)(2,1)S(1)} %shard_map.43.refs_0_.rows_ref), channel_id=1, source_target_pairs={{0,2},{1,3},{2,0},{3,1},{4,6},{5,7},{6,4},{7,5},{8,10},{9,11},{10,... | collective-permute-start | bytes 221192 | tf_op jit(solution)/shard_map/ppermute | solution.py:171
  13.5 1.1 %collective-permute-start.8 = (bf16[288,128]{1,0:T(8,128)(2,1)S(1)}, bf16[288,128]{1,0:T(8,128)(2,1)S(1)}, u32[]{:S(2)}, u32[]{:S(2)}) collective-permute-start(bf16[288,128]{1,0:T(8,128)(2,1)S(1)} %collective-permute-done.1.refs_2_), channel_id=1, source_target_pairs={{0,4},{1,5},{2,6},{3,7},{4,0},{5,1},{6,2},{7,3},{8,12},{9,13},{10,... | collective-permute-start | bytes 221192 | tf_op jit(solution)/shard_map/ppermute | solution.py:171
  14.7 0.1 collective-permute-done.3.refs_1_
  14.8 0.4 %collective-permute-start.5 = (bf16[288,128]{1,0:T(8,128)(2,1)S(1)}, bf16[288,128]{1,0:T(8,128)(2,1)S(1)}, u32[]{:S(2)}, u32[]{:S(2)}) collective-permute-start(bf16[288,128]{1,0:T(8,128)(2,1)S(1)} %collective-permute-done.3.refs_1_), channel_id=1, source_target_pairs={{0,1},{1,0},{2,3},{3,2},{4,5},{5,4},{6,7},{7,6},{8,9},{9,8},{10,11... | collective-permute-start | bytes 221192 | tf_op jit(solution)/shard_map/ppermute | solution.py:171
  15.2 1.5 %collective-permute-start.10 = (bf16[288,128]{1,0:T(8,128)(2,1)S(1)}, bf16[288,128]{1,0:T(8,128)(2,1)S(1)}, u32[]{:S(2)}, u32[]{:S(2)}) collective-permute-start(bf16[288,128]{1,0:T(8,128)(2,1)S(1)} %collective-permute-done.1.refs_2_), channel_id=1, source_target_pairs={{0,2},{1,3},{2,0},{3,1},{4,6},{5,7},{6,4},{7,5},{8,10},{9,11},{10,... | collective-permute-start | bytes 221192 | tf_op jit(solution)/shard_map/ppermute | solution.py:171
  16.7 0.0 collective-permute-done.7.refs_0_
  16.7 1.5 %collective-permute-start.9 = (bf16[288,128]{1,0:T(8,128)(2,1)S(1)}, bf16[288,128]{1,0:T(8,128)(2,1)S(1)}, u32[]{:S(2)}, u32[]{:S(2)}) collective-permute-start(bf16[288,128]{1,0:T(8,128)(2,1)S(1)} %collective-permute-done.3.refs_1_), channel_id=1, source_target_pairs={{0,2},{1,3},{2,0},{3,1},{4,6},{5,7},{6,4},{7,5},{8,10},{9,11},{10,... | collective-permute-start | bytes 221192 | tf_op jit(solution)/shard_map/ppermute | solution.py:171
  18.2 0.8 %collective-permute-start.15 = (bf16[288,128]{1,0:T(8,128)(2,1)S(1)}, bf16[288,128]{1,0:T(8,128)(2,1)S(1)}, u32[]{:S(2)}, u32[]{:S(2)}) collective-permute-start(bf16[288,128]{1,0:T(8,128)(2,1)S(1)} %collective-permute-done.8.refs_1_), channel_id=1, source_target_pairs={{0,2},{1,3},{2,0},{3,1},{4,6},{5,7},{6,4},{7,5},{8,10},{9,11},{10,... | collective-permute-start | bytes 221192 | tf_op jit(solution)/shard_map/ppermute | solution.py:171
  19.0 0.0 collective-permute-done.6.refs_5_
  19.0 0.5 %collective-permute-start.12 = (bf16[288,128]{1,0:T(8,128)(2,1)S(1)}, bf16[288,128]{1,0:T(8,128)(2,1)S(1)}, u32[]{:S(2)}, u32[]{:S(2)}) collective-permute-start(bf16[288,128]{1,0:T(8,128)(2,1)S(1)} %collective-permute-done.8.refs_1_), channel_id=1, source_target_pairs={{0,1},{1,0},{2,3},{3,2},{4,5},{5,4},{6,7},{7,6},{8,9},{9,8},{10,11... | collective-permute-start | bytes 221192 | tf_op jit(solution)/shard_map/ppermute | solution.py:171
  19.5 0.6 %collective-permute-done.10.refs_3_ = bf16[288,128]{1,0:T(8,128)(2,1)S(1)} collective-permute-done((bf16[288,128]{1,0:T(8,128)(2,1)S(1)}, bf16[288,128]{1,0:T(8,128)(2,1)S(1)}, u32[]{:S(2)}, u32[]{:S(2)}) %collective-permute-start.10) | collective-permute-done | bytes 73760 | tf_op jit(solution)/shard_map/ppermute | solution.py:171
  20.0 1.8 %collective-permute-done.9.refs_2_ = bf16[288,128]{1,0:T(8,128)(2,1)S(1)} collective-permute-done((bf16[288,128]{1,0:T(8,128)(2,1)S(1)}, bf16[288,128]{1,0:T(8,128)(2,1)S(1)}, u32[]{:S(2)}, u32[]{:S(2)}) %collective-permute-start.9) | collective-permute-done | bytes 73760 | tf_op jit(solution)/shard_map/ppermute | solution.py:171
  21.9 0.8 %collective-permute-done.15.refs_8_ = bf16[288,128]{1,0:T(8,128)(2,1)S(1)} collective-permute-done((bf16[288,128]{1,0:T(8,128)(2,1)S(1)}, bf16[288,128]{1,0:T(8,128)(2,1)S(1)}, u32[]{:S(2)}, u32[]{:S(2)}) %collective-permute-start.15) | collective-permute-done | bytes 73760 | tf_op jit(solution)/shard_map/ppermute | solution.py:171
  22.7 0.7 %shard_map.45.sum_ref = f32[576,576]{1,0:T(8,128)S(1)} custom-call(bf16[288,128]{1,0:T(8,128)(2,1)S(1)} %shard_map.43.refs_0_.rows_ref, bf16[288,128]{1,0:T(8,128)(2,1)S(1)} %collective-permute-done.3.refs_1_, bf16[288,128]{1,0:T(8,128)(2,1)S(1)} %collective-permute-done.1.refs_2_, bf16[288,128]{1,0:T(8,128)(2,1)S(1)} %collective-permute-done.4.refs_3_, ...), custom_call_target="tpu_custom_call" | custom-call | tf_op jit(solution)/shard_map/pallas_call | solution.py:109
  23.4 0.0 copy-start.2
  23.4 0.5 %collective-permute-done.16.refs_9_ = bf16[288,128]{1,0:T(8,128)(2,1)S(1)} collective-permute-done((bf16[288,128]{1,0:T(8,128)(2,1)S(1)}, bf16[288,128]{1,0:T(8,128)(2,1)S(1)}, u32[]{:S(2)}, u32[]{:S(2)}) %collective-permute-start.16) | collective-permute-done | bytes 73760 | tf_op jit(solution)/shard_map/ppermute | solution.py:171
  24.0 2.9 %shard_map.46.rows_ref = bf16[288,128]{1,0:T(8,128)(2,1)S(1)} custom-call(f32[576,576]{1,0:T(8,128)S(1)} %shard_map.45.sum_ref, bf16[288,128]{1,0:T(8,128)(2,1)S(1)} %shard_map.43.refs_0_.rows_ref, bf16[288,128]{1,0:T(8,128)(2,1)S(1)} %collective-permute-done.7.refs_0_, bf16[288,128]{1,0:T(8,128)(2,1)S(1)} %collective-permute-done.8.refs_1_, ...), custom_call_target="tpu_custom_call" | custom-call | tf_op jit(solution)/shard_map/pallas_call | solution.py:127
  26.9 1.7 %collective-permute-start.17 = (bf16[288,128]{1,0:T(8,128)(2,1)S(1)}, bf16[288,128]{1,0:T(8,128)(2,1)S(1)}, u32[]{:S(2)}, u32[]{:S(2)}) collective-permute-start(bf16[288,128]{1,0:T(8,128)(2,1)S(1)} %shard_map.46.rows_ref), channel_id=1, source_target_pairs={{0,16},{16,0},{1,17},{17,1},{2,18},{18,2},{3,19},{19,3},{4,20},{20... | collective-permute-start | bytes 221192 | tf_op jit(solution)/shard_map/ppermute | solution.py:171
  28.6 0.8 %shard_map.44 = f32[2,64,576]{2,1,0:T(8,128)} custom-call(f32[2,64,576]{2,1,0:T(8,128)S(1)} %copy-done.2, bf16[288,128]{1,0:T(8,128)(2,1)S(1)} %get-tuple-element.6.kept_ref, bf16[288,128]{1,0:T(8,128)(2,1)S(1)} %collective-permute-done.arrived_ref, bf16[288,128]{1,0:T(8,128)(2,1)S(1)} %shard_map.42.away_ref, ...), custom_call_target="tpu_custom_call" | custom-call | tf_op jit(solution)/shard_map/pallas_call | solution.py:270
  29.4 0.8 %shard_map.47.refs_0_ = f32[2,64,576]{2,1,0:T(8,128)} custom-call(bf16[288,128]{1,0:T(8,128)(2,1)S(1)} %shard_map.46.rows_ref), custom_call_target="tpu_custom_call" | custom-call | tf_op jit(solution)/shard_map/pallas_call | solution.py:280
  30.2 1.1 %collective-permute-done.17.rows_ref = bf16[288,128]{1,0:T(8,128)(2,1)S(1)} collective-permute-done((bf16[288,128]{1,0:T(8,128)(2,1)S(1)}, bf16[288,128]{1,0:T(8,128)(2,1)S(1)}, u32[]{:S(2)}, u32[]{:S(2)}) %collective-permute-start.17) | collective-permute-done | bytes 73760 | tf_op jit(solution)/shard_map/ppermute | solution.py:171
  31.3 0.8 %shard_map.48 = f32[2,64,576]{2,1,0:T(8,128)} custom-call(bf16[288,128]{1,0:T(8,128)(2,1)S(1)} %collective-permute-done.17.rows_ref, f32[2,64,576]{2,1,0:T(8,128)} %shard_map.47.refs_0_), custom_call_target="tpu_custom_call", output_to_operand_aliasing={{}: (1, {})} | custom-call | tf_op jit(solution)/shard_map/pallas_call | solution.py:288
  (18 shorter events, 0.1 us)
Async XLA Ops:
  0.6 1.0 %copy-start = (f32[1,2,64,576]{3,2,1,0:T(8,128)S(1)}, f32[1,2,64,576]{3,2,1,0:T(8,128)}, u32[]{:S(2)}) copy-start(f32[1,2,64,576]{3,2,1,0:T(8,128)} %param.2) | copy-start | bytes 884740
  1.9 5.3 %collective-permute-start = (bf16[288,128]{1,0:T(8,128)(2,1)S(1)}, bf16[288,128]{1,0:T(8,128)(2,1)S(1)}, u32[]{:S(2)}, u32[]{:S(2)}) collective-permute-start(bf16[288,128]{1,0:T(8,128)(2,1)S(1)} %shard_map.42.away_ref), channel_id=1, source_target_pairs={{0,16},{16,0},{1,17},{17,1},{2,18},{18,2},{3,19},{19,3},{4,20},{20... | collective-permute-start | bytes 221192 | tf_op jit(solution)/shard_map/ppermute | solution.py:171
  4.9 1.0 %copy-start.1 = (f32[2,64,576]{2,1,0:T(8,128)S(1)}, f32[2,64,576]{2,1,0:T(8,128)}, u32[]{:S(2)}) copy-start(f32[2,64,576]{2,1,0:T(8,128)} %momentum_ref.3) | copy-start | bytes 884740
  6.4 7.2 %collective-permute-start.2 = (bf16[288,128]{1,0:T(8,128)(2,1)S(1)}, bf16[288,128]{1,0:T(8,128)(2,1)S(1)}, u32[]{:S(2)}, u32[]{:S(2)}) collective-permute-start(bf16[288,128]{1,0:T(8,128)(2,1)S(1)} %get-tuple-element.6.kept_ref), channel_id=1, source_target_pairs={{0,16},{16,0},{1,17},{17,1},{2,18},{18,2},{3,19},{19,3},{4,20},{20... | collective-permute-start | bytes 221192 | tf_op jit(solution)/shard_map/ppermute | solution.py:171
  7.2 6.3 %collective-permute-start.1 = (bf16[288,128]{1,0:T(8,128)(2,1)S(1)}, bf16[288,128]{1,0:T(8,128)(2,1)S(1)}, u32[]{:S(2)}, u32[]{:S(2)}) collective-permute-start(bf16[288,128]{1,0:T(8,128)(2,1)S(1)} %shard_map.43.refs_0_.rows_ref), channel_id=1, source_target_pairs={{0,8},{1,9},{2,10},{3,11},{4,12},{5,13},{6,14},{7,15},{8,0},{9,1},... | collective-permute-start | bytes 221192 | tf_op jit(solution)/shard_map/ppermute | solution.py:171
  10.4 4.4 %collective-permute-start.3 = (bf16[288,128]{1,0:T(8,128)(2,1)S(1)}, bf16[288,128]{1,0:T(8,128)(2,1)S(1)}, u32[]{:S(2)}, u32[]{:S(2)}) collective-permute-start(bf16[288,128]{1,0:T(8,128)(2,1)S(1)} %shard_map.43.refs_0_.rows_ref), channel_id=1, source_target_pairs={{0,4},{1,5},{2,6},{3,7},{4,0},{5,1},{6,2},{7,3},{8,12},{9,13},{10,... | collective-permute-start | bytes 221192 | tf_op jit(solution)/shard_map/ppermute | solution.py:171
  12.0 3.2 %collective-permute-start.4 = (bf16[288,128]{1,0:T(8,128)(2,1)S(1)}, bf16[288,128]{1,0:T(8,128)(2,1)S(1)}, u32[]{:S(2)}, u32[]{:S(2)}) collective-permute-start(bf16[288,128]{1,0:T(8,128)(2,1)S(1)} %shard_map.43.refs_0_.rows_ref), channel_id=1, source_target_pairs={{0,1},{1,0},{2,3},{3,2},{4,5},{5,4},{6,7},{7,6},{8,9},{9,8},{10,11... | collective-permute-start | bytes 221192 | tf_op jit(solution)/shard_map/ppermute | solution.py:171
  12.0 4.7 %collective-permute-start.7 = (bf16[288,128]{1,0:T(8,128)(2,1)S(1)}, bf16[288,128]{1,0:T(8,128)(2,1)S(1)}, u32[]{:S(2)}, u32[]{:S(2)}) collective-permute-start(bf16[288,128]{1,0:T(8,128)(2,1)S(1)} %shard_map.43.refs_0_.rows_ref), channel_id=1, source_target_pairs={{0,2},{1,3},{2,0},{3,1},{4,6},{5,7},{6,4},{7,5},{8,10},{9,11},{10,... | collective-permute-start | bytes 221192 | tf_op jit(solution)/shard_map/ppermute | solution.py:171
  13.5 4.7 %collective-permute-start.8 = (bf16[288,128]{1,0:T(8,128)(2,1)S(1)}, bf16[288,128]{1,0:T(8,128)(2,1)S(1)}, u32[]{:S(2)}, u32[]{:S(2)}) collective-permute-start(bf16[288,128]{1,0:T(8,128)(2,1)S(1)} %collective-permute-done.1.refs_2_), channel_id=1, source_target_pairs={{0,4},{1,5},{2,6},{3,7},{4,0},{5,1},{6,2},{7,3},{8,12},{9,13},{10,... | collective-permute-start | bytes 221192 | tf_op jit(solution)/shard_map/ppermute | solution.py:171
  14.7 4.3 %collective-permute-start.6 = (bf16[288,128]{1,0:T(8,128)(2,1)S(1)}, bf16[288,128]{1,0:T(8,128)(2,1)S(1)}, u32[]{:S(2)}, u32[]{:S(2)}) collective-permute-start(bf16[288,128]{1,0:T(8,128)(2,1)S(1)} %collective-permute-done.1.refs_2_), channel_id=1, source_target_pairs={{0,1},{1,0},{2,3},{3,2},{4,5},{5,4},{6,7},{7,6},{8,9},{9,8},{10,11... | collective-permute-start | bytes 221192 | tf_op jit(solution)/shard_map/ppermute | solution.py:171
  14.8 4.2 %collective-permute-start.5 = (bf16[288,128]{1,0:T(8,128)(2,1)S(1)}, bf16[288,128]{1,0:T(8,128)(2,1)S(1)}, u32[]{:S(2)}, u32[]{:S(2)}) collective-permute-start(bf16[288,128]{1,0:T(8,128)(2,1)S(1)} %collective-permute-done.3.refs_1_), channel_id=1, source_target_pairs={{0,1},{1,0},{2,3},{3,2},{4,5},{5,4},{6,7},{7,6},{8,9},{9,8},{10,11... | collective-permute-start | bytes 221192 | tf_op jit(solution)/shard_map/ppermute | solution.py:171
  15.2 4.8 %collective-permute-start.10 = (bf16[288,128]{1,0:T(8,128)(2,1)S(1)}, bf16[288,128]{1,0:T(8,128)(2,1)S(1)}, u32[]{:S(2)}, u32[]{:S(2)}) collective-permute-start(bf16[288,128]{1,0:T(8,128)(2,1)S(1)} %collective-permute-done.1.refs_2_), channel_id=1, source_target_pairs={{0,2},{1,3},{2,0},{3,1},{4,6},{5,7},{6,4},{7,5},{8,10},{9,11},{10,... | collective-permute-start | bytes 221192 | tf_op jit(solution)/shard_map/ppermute | solution.py:171
  16.7 5.2 %collective-permute-start.9 = (bf16[288,128]{1,0:T(8,128)(2,1)S(1)}, bf16[288,128]{1,0:T(8,128)(2,1)S(1)}, u32[]{:S(2)}, u32[]{:S(2)}) collective-permute-start(bf16[288,128]{1,0:T(8,128)(2,1)S(1)} %collective-permute-done.3.refs_1_), channel_id=1, source_target_pairs={{0,2},{1,3},{2,0},{3,1},{4,6},{5,7},{6,4},{7,5},{8,10},{9,11},{10,... | collective-permute-start | bytes 221192 | tf_op jit(solution)/shard_map/ppermute | solution.py:171
  18.2 4.5 %collective-permute-start.15 = (bf16[288,128]{1,0:T(8,128)(2,1)S(1)}, bf16[288,128]{1,0:T(8,128)(2,1)S(1)}, u32[]{:S(2)}, u32[]{:S(2)}) collective-permute-start(bf16[288,128]{1,0:T(8,128)(2,1)S(1)} %collective-permute-done.8.refs_1_), channel_id=1, source_target_pairs={{0,2},{1,3},{2,0},{3,1},{4,6},{5,7},{6,4},{7,5},{8,10},{9,11},{10,... | collective-permute-start | bytes 221192 | tf_op jit(solution)/shard_map/ppermute | solution.py:171
  19.0 4.4 %collective-permute-start.11 = (bf16[288,128]{1,0:T(8,128)(2,1)S(1)}, bf16[288,128]{1,0:T(8,128)(2,1)S(1)}, u32[]{:S(2)}, u32[]{:S(2)}) collective-permute-start(bf16[288,128]{1,0:T(8,128)(2,1)S(1)} %collective-permute-done.7.refs_0_), channel_id=1, source_target_pairs={{0,1},{1,0},{2,3},{3,2},{4,5},{5,4},{6,7},{7,6},{8,9},{9,8},{10,11... | collective-permute-start | bytes 221192 | tf_op jit(solution)/shard_map/ppermute | solution.py:171
  19.0 4.4 %collective-permute-start.12 = (bf16[288,128]{1,0:T(8,128)(2,1)S(1)}, bf16[288,128]{1,0:T(8,128)(2,1)S(1)}, u32[]{:S(2)}, u32[]{:S(2)}) collective-permute-start(bf16[288,128]{1,0:T(8,128)(2,1)S(1)} %collective-permute-done.8.refs_1_), channel_id=1, source_target_pairs={{0,1},{1,0},{2,3},{3,2},{4,5},{5,4},{6,7},{7,6},{8,9},{9,8},{10,11... | collective-permute-start | bytes 221192 | tf_op jit(solution)/shard_map/ppermute | solution.py:171
  20.0 3.4 %collective-permute-start.14 = (bf16[288,128]{1,0:T(8,128)(2,1)S(1)}, bf16[288,128]{1,0:T(8,128)(2,1)S(1)}, u32[]{:S(2)}, u32[]{:S(2)}) collective-permute-start(bf16[288,128]{1,0:T(8,128)(2,1)S(1)} %collective-permute-done.10.refs_3_), channel_id=1, source_target_pairs={{0,1},{1,0},{2,3},{3,2},{4,5},{5,4},{6,7},{7,6},{8,9},{9,8},{10,11... | collective-permute-start | bytes 221192 | tf_op jit(solution)/shard_map/ppermute | solution.py:171
  21.9 1.6 %collective-permute-start.13 = (bf16[288,128]{1,0:T(8,128)(2,1)S(1)}, bf16[288,128]{1,0:T(8,128)(2,1)S(1)}, u32[]{:S(2)}, u32[]{:S(2)}) collective-permute-start(bf16[288,128]{1,0:T(8,128)(2,1)S(1)} %collective-permute-done.9.refs_2_), channel_id=1, source_target_pairs={{0,1},{1,0},{2,3},{3,2},{4,5},{5,4},{6,7},{7,6},{8,9},{9,8},{10,11... | collective-permute-start | bytes 221192 | tf_op jit(solution)/shard_map/ppermute | solution.py:171
  22.7 1.3 %collective-permute-start.16 = (bf16[288,128]{1,0:T(8,128)(2,1)S(1)}, bf16[288,128]{1,0:T(8,128)(2,1)S(1)}, u32[]{:S(2)}, u32[]{:S(2)}) collective-permute-start(bf16[288,128]{1,0:T(8,128)(2,1)S(1)} %collective-permute-done.15.refs_8_), channel_id=1, source_target_pairs={{0,1},{1,0},{2,3},{3,2},{4,5},{5,4},{6,7},{7,6},{8,9},{9,8},{10,11... | collective-permute-start | bytes 221192 | tf_op jit(solution)/shard_map/ppermute | solution.py:171
  23.4 5.2 %copy-start.2 = (f32[2,64,576]{2,1,0:T(8,128)S(1)}, f32[2,64,576]{2,1,0:T(8,128)}, u32[]{:S(2)}) copy-start(f32[2,64,576]{2,1,0:T(8,128)} %momentum_ref.3) | copy-start | bytes 884740
  26.9 4.4 %collective-permute-start.17 = (bf16[288,128]{1,0:T(8,128)(2,1)S(1)}, bf16[288,128]{1,0:T(8,128)(2,1)S(1)}, u32[]{:S(2)}, u32[]{:S(2)}) collective-permute-start(bf16[288,128]{1,0:T(8,128)(2,1)S(1)} %shard_map.46.rows_ref), channel_id=1, source_target_pairs={{0,16},{16,0},{1,17},{17,1},{2,18},{18,2},{3,19},{19,3},{4,20},{20... | collective-permute-start | bytes 221192 | tf_op jit(solution)/shard_map/ppermute | solution.py:171

commit v3 on v2

--- a/solution.py
+++ b/solution.py
@@ -190,7 +190,9 @@
     gram = gram_of(near, rows, width)
     far = [y0, z3, y1, y2]
     far = far + [exchange(v, "dp", 1) for v in far]
-    return finish(gram, block, far + [y3, exchange(y3, "dp", 1)], rows, width), beside
+    gram, last = lax.optimization_barrier((gram, y3))
+    gram = gram_of(far, rows, width, gram)
+    return finish(gram, block, [last, exchange(last, "dp", 1)], rows, width), beside
 
 
 def away_kernel(grads_ref, away_ref, held, done):

time: 32.2 us -> 32.1 us (level)
  waiting for transfers between devices: 5.71 us -> 4.9 us
  starting transfers between devices: 16.9 us -> 17.3 us
    ppermute x18, waiting for transfers between devices: 5.71 us -> 4.9 us  [exchange(): lax.ppermute(value, axis, [(at, at ^ distance) for at in range(size)])]
    pallas_call x1 -> x2, Pallas kernels: 0.68 us -> 1.37 us  [gram_of(): pl.pallas_call(functools.partial(gram_kernel, rows, len(before)), out_sha...]
    pallas_call x1, Pallas kernels: 2.93 us -> 2.54 us  [finish(): pl.pallas_call(functools.partial(finish_kernel, rows), out_shape=jax.Shap...]
    ppermute x18, starting transfers between devices: 16.9 us -> 17.3 us  [exchange(): lax.ppermute(value, axis, [(at, at ^ distance) for at in range(size)])]
  transfers between devices with their start and end apart: 18 -> 18, of which waited for: 7 -> 7; matrix products, arithmetic and copies ran while one was open for 0% -> 0% of each run, Pallas kernels for 9% -> 11%
where the time goes in v3:
time: 32.1 us; the launch traced here: 31.9 us
  starting transfers between devices  17.3 us (54%)
  Pallas kernels  7.04 us (22%)
  waiting for transfers between devices  4.9 us (15%)
  local copies, waits for them, and re-layouts  1.94 us (6%)
  between operations  0.72 us (2%)
    ppermute x18, starting transfers between devices, exchange(): lax.ppermute(value, axis, [(at, at ^ distance) for at in range(size)])  17.3 us
    ppermute x18, waiting for transfers between devices, exchange(): lax.ppermute(value, axis, [(at, at ^ distance) for at in range(size)])  4.9 us
    pallas_call x1, Pallas kernels, finish(): pl.pallas_call(functools.partial(finish_kernel, rows), out_shape=jax.Shap...  2.54 us
    unnamed x6, local copies, waits for them, and re-layouts  1.94 us
    pallas_call x2, Pallas kernels, gram_of(): pl.pallas_call(functools.partial(gram_kernel, rows, len(before)), out_sha...  1.37 us
    pallas_call x1, Pallas kernels, two_pods(): pl.pallas_call(momentum_kernel, out_shape=both, in_specs=[VMEM] * 5, scra...  0.81 us
    pallas_call x1, Pallas kernels, two_pods(): pl.pallas_call(functools.partial(update_kernel, update_scale, False), out...  0.76 us
    pallas_call x1, Pallas kernels, two_pods(): pl.pallas_call(functools.partial(update_kernel, update_scale, True), out_...  0.76 us
  transfers between devices with their start and end apart: 18, of which 7 were waited for; matrix products, arithmetic and copies ran while one was open for 0% of the time, Pallas kernels for 11%

profile of v3, /device:TPU:0, one launch (start us, length us, event | category | flops | bytes accessed | tf_op | source)
XLA Modules:
  0.0 31.9 jit_solution(12847223747711339925)
XLA Ops:
  0.6 1.0 %copy-done = f32[1,2,64,576]{3,2,1,0:T(8,128)S(1)} copy-done((f32[1,2,64,576]{3,2,1,0:T(8,128)S(1)}, f32[1,2,64,576]{3,2,1,0:T(8,128)}, u32[]{:S(2)}) %copy-start) | copy-done | bytes 294936
  1.6 0.3 shard_map.42.away_ref
  1.9 3.0 %collective-permute-start = (bf16[288,128]{1,0:T(8,128)(2,1)S(1)}, bf16[288,128]{1,0:T(8,128)(2,1)S(1)}, u32[]{:S(2)}, u32[]{:S(2)}) collective-permute-start(bf16[288,128]{1,0:T(8,128)(2,1)S(1)} %shard_map.42.away_ref), channel_id=1, source_target_pairs={{0,16},{16,0},{1,17},{17,1},{2,18},{18,2},{3,19},{19,3},{4,20},{20... | collective-permute-start | bytes 221192 | tf_op jit(solution)/shard_map/ppermute | solution.py:171
  4.9 1.0 %copy-done.1 = f32[2,64,576]{2,1,0:T(8,128)S(1)} copy-done((f32[2,64,576]{2,1,0:T(8,128)S(1)}, f32[2,64,576]{2,1,0:T(8,128)}, u32[]{:S(2)}) %copy-start.1) | copy-done | bytes 294936
  5.9 0.5 %shard_map.41 = (bf16[288,128]{1,0:T(8,128)(2,1)S(1)}, f32[288,128]{1,0:T(8,128)S(1)}) custom-call(f32[2,64,576]{2,1,0:T(8,128)S(1)} %bitcast.2, f32[2,64,576]{2,1,0:T(8,128)S(1)} %copy-done.1), custom_call_target="tpu_custom_call" | custom-call | tf_op jit(solution)/shard_map/pallas_call | solution.py:258
  6.4 0.1 collective-permute-start.2
  6.4 0.8 %collective-permute-done.arrived_ref = bf16[288,128]{1,0:T(8,128)(2,1)S(1)} collective-permute-done((bf16[288,128]{1,0:T(8,128)(2,1)S(1)}, bf16[288,128]{1,0:T(8,128)(2,1)S(1)}, u32[]{:S(2)}, u32[]{:S(2)}) %collective-permute-start) | collective-permute-done | bytes 73760 | tf_op jit(solution)/shard_map/ppermute | solution.py:171
  7.2 3.2 %collective-permute-start.1 = (bf16[288,128]{1,0:T(8,128)(2,1)S(1)}, bf16[288,128]{1,0:T(8,128)(2,1)S(1)}, u32[]{:S(2)}, u32[]{:S(2)}) collective-permute-start(bf16[288,128]{1,0:T(8,128)(2,1)S(1)} %shard_map.43.refs_0_.rows_ref), channel_id=1, source_target_pairs={{0,8},{1,9},{2,10},{3,11},{4,12},{5,13},{6,14},{7,15},{8,0},{9,1},... | collective-permute-start | bytes 221192 | tf_op jit(solution)/shard_map/ppermute | solution.py:171
  10.4 1.6 %collective-permute-start.3 = (bf16[288,128]{1,0:T(8,128)(2,1)S(1)}, bf16[288,128]{1,0:T(8,128)(2,1)S(1)}, u32[]{:S(2)}, u32[]{:S(2)}) collective-permute-start(bf16[288,128]{1,0:T(8,128)(2,1)S(1)} %shard_map.43.refs_0_.rows_ref), channel_id=1, source_target_pairs={{0,4},{1,5},{2,6},{3,7},{4,0},{5,1},{6,2},{7,3},{8,12},{9,13},{10,... | collective-permute-start | bytes 221192 | tf_op jit(solution)/shard_map/ppermute | solution.py:171
  12.0 0.0 collective-permute-start.4
  12.0 1.5 %collective-permute-start.9 = (bf16[288,128]{1,0:T(8,128)(2,1)S(1)}, bf16[288,128]{1,0:T(8,128)(2,1)S(1)}, u32[]{:S(2)}, u32[]{:S(2)}) collective-permute-start(bf16[288,128]{1,0:T(8,128)(2,1)S(1)} %shard_map.43.refs_0_.rows_ref), channel_id=1, source_target_pairs={{0,2},{1,3},{2,0},{3,1},{4,6},{5,7},{6,4},{7,5},{8,10},{9,11},{10,... | collective-permute-start | bytes 221192 | tf_op jit(solution)/shard_map/ppermute | solution.py:171
  13.5 1.1 %collective-permute-start.7 = (bf16[288,128]{1,0:T(8,128)(2,1)S(1)}, bf16[288,128]{1,0:T(8,128)(2,1)S(1)}, u32[]{:S(2)}, u32[]{:S(2)}) collective-permute-start(bf16[288,128]{1,0:T(8,128)(2,1)S(1)} %collective-permute-done.1.refs_2_), channel_id=1, source_target_pairs={{0,4},{1,5},{2,6},{3,7},{4,0},{5,1},{6,2},{7,3},{8,12},{9,13},{10,... | collective-permute-start | bytes 221192 | tf_op jit(solution)/shard_map/ppermute | solution.py:171
  14.7 0.1 collective-permute-done.3.refs_1_
  14.8 0.4 %collective-permute-start.5 = (bf16[288,128]{1,0:T(8,128)(2,1)S(1)}, bf16[288,128]{1,0:T(8,128)(2,1)S(1)}, u32[]{:S(2)}, u32[]{:S(2)}) collective-permute-start(bf16[288,128]{1,0:T(8,128)(2,1)S(1)} %collective-permute-done.3.refs_1_), channel_id=1, source_target_pairs={{0,1},{1,0},{2,3},{3,2},{4,5},{5,4},{6,7},{7,6},{8,9},{9,8},{10,11... | collective-permute-start | bytes 221192 | tf_op jit(solution)/shard_map/ppermute | solution.py:171
  15.2 1.5 %collective-permute-start.11 = (bf16[288,128]{1,0:T(8,128)(2,1)S(1)}, bf16[288,128]{1,0:T(8,128)(2,1)S(1)}, u32[]{:S(2)}, u32[]{:S(2)}) collective-permute-start(bf16[288,128]{1,0:T(8,128)(2,1)S(1)} %collective-permute-done.1.refs_2_), channel_id=1, source_target_pairs={{0,2},{1,3},{2,0},{3,1},{4,6},{5,7},{6,4},{7,5},{8,10},{9,11},{10,... | collective-permute-start | bytes 221192 | tf_op jit(solution)/shard_map/ppermute | solution.py:171
  16.7 1.5 %collective-permute-start.10 = (bf16[288,128]{1,0:T(8,128)(2,1)S(1)}, bf16[288,128]{1,0:T(8,128)(2,1)S(1)}, u32[]{:S(2)}, u32[]{:S(2)}) collective-permute-start(bf16[288,128]{1,0:T(8,128)(2,1)S(1)} %collective-permute-done.3.refs_1_), channel_id=1, source_target_pairs={{0,2},{1,3},{2,0},{3,1},{4,6},{5,7},{6,4},{7,5},{8,10},{9,11},{10,... | collective-permute-start | bytes 221192 | tf_op jit(solution)/shard_map/ppermute | solution.py:171
  18.2 0.8 %collective-permute-start.8 = (bf16[288,128]{1,0:T(8,128)(2,1)S(1)}, bf16[288,128]{1,0:T(8,128)(2,1)S(1)}, u32[]{:S(2)}, u32[]{:S(2)}) collective-permute-start(bf16[288,128]{1,0:T(8,128)(2,1)S(1)} %collective-permute-done.7.refs_2_), channel_id=1, source_target_pairs={{0,2},{1,3},{2,0},{3,1},{4,6},{5,7},{6,4},{7,5},{8,10},{9,11},{10,... | collective-permute-start | bytes 221192 | tf_op jit(solution)/shard_map/ppermute | solution.py:171
  19.0 0.5 %collective-permute-start.13 = (bf16[288,128]{1,0:T(8,128)(2,1)S(1)}, bf16[288,128]{1,0:T(8,128)(2,1)S(1)}, u32[]{:S(2)}, u32[]{:S(2)}) collective-permute-start(bf16[288,128]{1,0:T(8,128)(2,1)S(1)} %collective-permute-done.7.refs_2_), channel_id=1, source_target_pairs={{0,1},{1,0},{2,3},{3,2},{4,5},{5,4},{6,7},{7,6},{8,9},{9,8},{10,11... | collective-permute-start | bytes 221192 | tf_op jit(solution)/shard_map/ppermute | solution.py:171
  19.5 0.6 %collective-permute-done.11.refs_4_ = bf16[288,128]{1,0:T(8,128)(2,1)S(1)} collective-permute-done((bf16[288,128]{1,0:T(8,128)(2,1)S(1)}, bf16[288,128]{1,0:T(8,128)(2,1)S(1)}, u32[]{:S(2)}, u32[]{:S(2)}) %collective-permute-start.11) | collective-permute-done | bytes 73760 | tf_op jit(solution)/shard_map/ppermute | solution.py:171
  20.0 1.8 %collective-permute-done.10.refs_3_ = bf16[288,128]{1,0:T(8,128)(2,1)S(1)} collective-permute-done((bf16[288,128]{1,0:T(8,128)(2,1)S(1)}, bf16[288,128]{1,0:T(8,128)(2,1)S(1)}, u32[]{:S(2)}, u32[]{:S(2)}) %collective-permute-start.10) | collective-permute-done | bytes 73760 | tf_op jit(solution)/shard_map/ppermute | solution.py:171
  21.9 0.7 %shard_map.45.refs_0_ = f32[576,576]{1,0:T(8,128)S(1)} custom-call(bf16[288,128]{1,0:T(8,128)(2,1)S(1)} %shard_map.43.refs_0_.rows_ref, bf16[288,128]{1,0:T(8,128)(2,1)S(1)} %collective-permute-done.3.refs_1_, bf16[288,128]{1,0:T(8,128)(2,1)S(1)} %collective-permute-done.1.refs_2_, bf16[288,128]{1,0:T(8,128)(2,1)S(1)} %collective-permute-done.4.refs_3_, ...), custom_call_target="tpu_custom_call" | custom-call | tf_op jit(solution)/shard_map/pallas_call | solution.py:109
  22.6 0.1 collective-permute-done.8.refs_0_
  22.7 0.4 %collective-permute-start.16 = (bf16[288,128]{1,0:T(8,128)(2,1)S(1)}, bf16[288,128]{1,0:T(8,128)(2,1)S(1)}, u32[]{:S(2)}, u32[]{:S(2)}) collective-permute-start(bf16[288,128]{1,0:T(8,128)(2,1)S(1)} %collective-permute-done.8.refs_0_), channel_id=1, source_target_pairs={{0,1},{1,0},{2,3},{3,2},{4,5},{5,4},{6,7},{7,6},{8,9},{9,8},{10,11... | collective-permute-start | bytes 221192 | tf_op jit(solution)/shard_map/ppermute | solution.py:171
  23.2 0.7 %shard_map.46.sum_ref = f32[576,576]{1,0:T(8,128)S(1)} custom-call(f32[576,576]{1,0:T(8,128)S(1)} %shard_map.45.refs_0_, bf16[288,128]{1,0:T(8,128)(2,1)S(1)} %collective-permute-done.9.refs_1_, bf16[288,128]{1,0:T(8,128)(2,1)S(1)} %collective-permute-done.7.refs_2_, bf16[288,128]{1,0:T(8,128)(2,1)S(1)} %collective-permute-done.10.refs_3_, ...), custom_call_target="tpu_custom_call" | custom-call | tf_op jit(solution)/shard_map/pallas_call | solution.py:109
  23.9 0.0 copy-start.2
  23.9 0.2 collective-permute-done.16.refs_1_
  24.0 2.5 %shard_map.47.rows_ref = bf16[288,128]{1,0:T(8,128)(2,1)S(1)} custom-call(f32[576,576]{1,0:T(8,128)S(1)} %shard_map.46.sum_ref, bf16[288,128]{1,0:T(8,128)(2,1)S(1)} %shard_map.43.refs_0_.rows_ref, bf16[288,128]{1,0:T(8,128)(2,1)S(1)} %collective-permute-done.8.refs_0_, bf16[288,128]{1,0:T(8,128)(2,1)S(1)} %collective-permute-done.16.refs_1_), custom_call_target="tpu_custom_call" | custom-call | tf_op jit(solution)/shard_map/pallas_call | solution.py:127
  26.6 1.7 %collective-permute-start.17 = (bf16[288,128]{1,0:T(8,128)(2,1)S(1)}, bf16[288,128]{1,0:T(8,128)(2,1)S(1)}, u32[]{:S(2)}, u32[]{:S(2)}) collective-permute-start(bf16[288,128]{1,0:T(8,128)(2,1)S(1)} %shard_map.47.rows_ref), channel_id=1, source_target_pairs={{0,16},{16,0},{1,17},{17,1},{2,18},{18,2},{3,19},{19,3},{4,20},{20... | collective-permute-start | bytes 221192 | tf_op jit(solution)/shard_map/ppermute | solution.py:171
  28.3 0.8 %shard_map.44 = f32[2,64,576]{2,1,0:T(8,128)} custom-call(f32[2,64,576]{2,1,0:T(8,128)S(1)} %copy-done.2, bf16[288,128]{1,0:T(8,128)(2,1)S(1)} %get-tuple-element.8.kept_ref, bf16[288,128]{1,0:T(8,128)(2,1)S(1)} %collective-permute-done.arrived_ref, bf16[288,128]{1,0:T(8,128)(2,1)S(1)} %shard_map.42.away_ref, ...), custom_call_target="tpu_custom_call" | custom-call | tf_op jit(solution)/shard_map/pallas_call | solution.py:272
  29.1 0.8 %shard_map.48.refs_0_ = f32[2,64,576]{2,1,0:T(8,128)} custom-call(bf16[288,128]{1,0:T(8,128)(2,1)S(1)} %shard_map.47.rows_ref), custom_call_target="tpu_custom_call" | custom-call | tf_op jit(solution)/shard_map/pallas_call | solution.py:282
  29.8 1.3 %collective-permute-done.17.rows_ref = bf16[288,128]{1,0:T(8,128)(2,1)S(1)} collective-permute-done((bf16[288,128]{1,0:T(8,128)(2,1)S(1)}, bf16[288,128]{1,0:T(8,128)(2,1)S(1)}, u32[]{:S(2)}, u32[]{:S(2)}) %collective-permute-start.17) | collective-permute-done | bytes 73760 | tf_op jit(solution)/shard_map/ppermute | solution.py:171
  31.1 0.8 %shard_map.49 = f32[2,64,576]{2,1,0:T(8,128)} custom-call(bf16[288,128]{1,0:T(8,128)(2,1)S(1)} %collective-permute-done.17.rows_ref, f32[2,64,576]{2,1,0:T(8,128)} %shard_map.48.refs_0_), custom_call_target="tpu_custom_call", output_to_operand_aliasing={{}: (1, {})} | custom-call | tf_op jit(solution)/shard_map/pallas_call | solution.py:290
  (19 shorter events, 0.1 us)
Async XLA Ops:
  0.6 1.0 %copy-start = (f32[1,2,64,576]{3,2,1,0:T(8,128)S(1)}, f32[1,2,64,576]{3,2,1,0:T(8,128)}, u32[]{:S(2)}) copy-start(f32[1,2,64,576]{3,2,1,0:T(8,128)} %param.2) | copy-start | bytes 884740
  1.9 5.3 %collective-permute-start = (bf16[288,128]{1,0:T(8,128)(2,1)S(1)}, bf16[288,128]{1,0:T(8,128)(2,1)S(1)}, u32[]{:S(2)}, u32[]{:S(2)}) collective-permute-start(bf16[288,128]{1,0:T(8,128)(2,1)S(1)} %shard_map.42.away_ref), channel_id=1, source_target_pairs={{0,16},{16,0},{1,17},{17,1},{2,18},{18,2},{3,19},{19,3},{4,20},{20... | collective-permute-start | bytes 221192 | tf_op jit(solution)/shard_map/ppermute | solution.py:171
  4.9 1.0 %copy-start.1 = (f32[2,64,576]{2,1,0:T(8,128)S(1)}, f32[2,64,576]{2,1,0:T(8,128)}, u32[]{:S(2)}) copy-start(f32[2,64,576]{2,1,0:T(8,128)} %momentum_ref.3) | copy-start | bytes 884740
  6.4 7.2 %collective-permute-start.2 = (bf16[288,128]{1,0:T(8,128)(2,1)S(1)}, bf16[288,128]{1,0:T(8,128)(2,1)S(1)}, u32[]{:S(2)}, u32[]{:S(2)}) collective-permute-start(bf16[288,128]{1,0:T(8,128)(2,1)S(1)} %get-tuple-element.8.kept_ref), channel_id=1, source_target_pairs={{0,16},{16,0},{1,17},{17,1},{2,18},{18,2},{3,19},{19,3},{4,20},{20... | collective-permute-start | bytes 221192 | tf_op jit(solution)/shard_map/ppermute | solution.py:171
  7.2 6.3 %collective-permute-start.1 = (bf16[288,128]{1,0:T(8,128)(2,1)S(1)}, bf16[288,128]{1,0:T(8,128)(2,1)S(1)}, u32[]{:S(2)}, u32[]{:S(2)}) collective-permute-start(bf16[288,128]{1,0:T(8,128)(2,1)S(1)} %shard_map.43.refs_0_.rows_ref), channel_id=1, source_target_pairs={{0,8},{1,9},{2,10},{3,11},{4,12},{5,13},{6,14},{7,15},{8,0},{9,1},... | collective-permute-start | bytes 221192 | tf_op jit(solution)/shard_map/ppermute | solution.py:171
  10.4 4.4 %collective-permute-start.3 = (bf16[288,128]{1,0:T(8,128)(2,1)S(1)}, bf16[288,128]{1,0:T(8,128)(2,1)S(1)}, u32[]{:S(2)}, u32[]{:S(2)}) collective-permute-start(bf16[288,128]{1,0:T(8,128)(2,1)S(1)} %shard_map.43.refs_0_.rows_ref), channel_id=1, source_target_pairs={{0,4},{1,5},{2,6},{3,7},{4,0},{5,1},{6,2},{7,3},{8,12},{9,13},{10,... | collective-permute-start | bytes 221192 | tf_op jit(solution)/shard_map/ppermute | solution.py:171
  12.0 3.2 %collective-permute-start.4 = (bf16[288,128]{1,0:T(8,128)(2,1)S(1)}, bf16[288,128]{1,0:T(8,128)(2,1)S(1)}, u32[]{:S(2)}, u32[]{:S(2)}) collective-permute-start(bf16[288,128]{1,0:T(8,128)(2,1)S(1)} %shard_map.43.refs_0_.rows_ref), channel_id=1, source_target_pairs={{0,1},{1,0},{2,3},{3,2},{4,5},{5,4},{6,7},{7,6},{8,9},{9,8},{10,11... | collective-permute-start | bytes 221192 | tf_op jit(solution)/shard_map/ppermute | solution.py:171
  12.0 4.7 %collective-permute-start.9 = (bf16[288,128]{1,0:T(8,128)(2,1)S(1)}, bf16[288,128]{1,0:T(8,128)(2,1)S(1)}, u32[]{:S(2)}, u32[]{:S(2)}) collective-permute-start(bf16[288,128]{1,0:T(8,128)(2,1)S(1)} %shard_map.43.refs_0_.rows_ref), channel_id=1, source_target_pairs={{0,2},{1,3},{2,0},{3,1},{4,6},{5,7},{6,4},{7,5},{8,10},{9,11},{10,... | collective-permute-start | bytes 221192 | tf_op jit(solution)/shard_map/ppermute | solution.py:171
  13.5 4.7 %collective-permute-start.7 = (bf16[288,128]{1,0:T(8,128)(2,1)S(1)}, bf16[288,128]{1,0:T(8,128)(2,1)S(1)}, u32[]{:S(2)}, u32[]{:S(2)}) collective-permute-start(bf16[288,128]{1,0:T(8,128)(2,1)S(1)} %collective-permute-done.1.refs_2_), channel_id=1, source_target_pairs={{0,4},{1,5},{2,6},{3,7},{4,0},{5,1},{6,2},{7,3},{8,12},{9,13},{10,... | collective-permute-start | bytes 221192 | tf_op jit(solution)/shard_map/ppermute | solution.py:171
  14.7 4.3 %collective-permute-start.6 = (bf16[288,128]{1,0:T(8,128)(2,1)S(1)}, bf16[288,128]{1,0:T(8,128)(2,1)S(1)}, u32[]{:S(2)}, u32[]{:S(2)}) collective-permute-start(bf16[288,128]{1,0:T(8,128)(2,1)S(1)} %collective-permute-done.1.refs_2_), channel_id=1, source_target_pairs={{0,1},{1,0},{2,3},{3,2},{4,5},{5,4},{6,7},{7,6},{8,9},{9,8},{10,11... | collective-permute-start | bytes 221192 | tf_op jit(solution)/shard_map/ppermute | solution.py:171
  14.8 4.2 %collective-permute-start.5 = (bf16[288,128]{1,0:T(8,128)(2,1)S(1)}, bf16[288,128]{1,0:T(8,128)(2,1)S(1)}, u32[]{:S(2)}, u32[]{:S(2)}) collective-permute-start(bf16[288,128]{1,0:T(8,128)(2,1)S(1)} %collective-permute-done.3.refs_1_), channel_id=1, source_target_pairs={{0,1},{1,0},{2,3},{3,2},{4,5},{5,4},{6,7},{7,6},{8,9},{9,8},{10,11... | collective-permute-start | bytes 221192 | tf_op jit(solution)/shard_map/ppermute | solution.py:171
  15.2 4.8 %collective-permute-start.11 = (bf16[288,128]{1,0:T(8,128)(2,1)S(1)}, bf16[288,128]{1,0:T(8,128)(2,1)S(1)}, u32[]{:S(2)}, u32[]{:S(2)}) collective-permute-start(bf16[288,128]{1,0:T(8,128)(2,1)S(1)} %collective-permute-done.1.refs_2_), channel_id=1, source_target_pairs={{0,2},{1,3},{2,0},{3,1},{4,6},{5,7},{6,4},{7,5},{8,10},{9,11},{10,... | collective-permute-start | bytes 221192 | tf_op jit(solution)/shard_map/ppermute | solution.py:171
  16.7 5.2 %collective-permute-start.10 = (bf16[288,128]{1,0:T(8,128)(2,1)S(1)}, bf16[288,128]{1,0:T(8,128)(2,1)S(1)}, u32[]{:S(2)}, u32[]{:S(2)}) collective-permute-start(bf16[288,128]{1,0:T(8,128)(2,1)S(1)} %collective-permute-done.3.refs_1_), channel_id=1, source_target_pairs={{0,2},{1,3},{2,0},{3,1},{4,6},{5,7},{6,4},{7,5},{8,10},{9,11},{10,... | collective-permute-start | bytes 221192 | tf_op jit(solution)/shard_map/ppermute | solution.py:171
  18.2 4.5 %collective-permute-start.8 = (bf16[288,128]{1,0:T(8,128)(2,1)S(1)}, bf16[288,128]{1,0:T(8,128)(2,1)S(1)}, u32[]{:S(2)}, u32[]{:S(2)}) collective-permute-start(bf16[288,128]{1,0:T(8,128)(2,1)S(1)} %collective-permute-done.7.refs_2_), channel_id=1, source_target_pairs={{0,2},{1,3},{2,0},{3,1},{4,6},{5,7},{6,4},{7,5},{8,10},{9,11},{10,... | collective-permute-start | bytes 221192 | tf_op jit(solution)/shard_map/ppermute | solution.py:171
  19.0 4.2 %collective-permute-start.12 = (bf16[288,128]{1,0:T(8,128)(2,1)S(1)}, bf16[288,128]{1,0:T(8,128)(2,1)S(1)}, u32[]{:S(2)}, u32[]{:S(2)}) collective-permute-start(bf16[288,128]{1,0:T(8,128)(2,1)S(1)} %collective-permute-done.9.refs_1_), channel_id=1, source_target_pairs={{0,1},{1,0},{2,3},{3,2},{4,5},{5,4},{6,7},{7,6},{8,9},{9,8},{10,11... | collective-permute-start | bytes 221192 | tf_op jit(solution)/shard_map/ppermute | solution.py:171
  19.0 4.2 %collective-permute-start.13 = (bf16[288,128]{1,0:T(8,128)(2,1)S(1)}, bf16[288,128]{1,0:T(8,128)(2,1)S(1)}, u32[]{:S(2)}, u32[]{:S(2)}) collective-permute-start(bf16[288,128]{1,0:T(8,128)(2,1)S(1)} %collective-permute-done.7.refs_2_), channel_id=1, source_target_pairs={{0,1},{1,0},{2,3},{3,2},{4,5},{5,4},{6,7},{7,6},{8,9},{9,8},{10,11... | collective-permute-start | bytes 221192 | tf_op jit(solution)/shard_map/ppermute | solution.py:171
  20.0 3.1 %collective-permute-start.15 = (bf16[288,128]{1,0:T(8,128)(2,1)S(1)}, bf16[288,128]{1,0:T(8,128)(2,1)S(1)}, u32[]{:S(2)}, u32[]{:S(2)}) collective-permute-start(bf16[288,128]{1,0:T(8,128)(2,1)S(1)} %collective-permute-done.11.refs_4_), channel_id=1, source_target_pairs={{0,1},{1,0},{2,3},{3,2},{4,5},{5,4},{6,7},{7,6},{8,9},{9,8},{10,11... | collective-permute-start | bytes 221192 | tf_op jit(solution)/shard_map/ppermute | solution.py:171
  21.9 1.3 %collective-permute-start.14 = (bf16[288,128]{1,0:T(8,128)(2,1)S(1)}, bf16[288,128]{1,0:T(8,128)(2,1)S(1)}, u32[]{:S(2)}, u32[]{:S(2)}) collective-permute-start(bf16[288,128]{1,0:T(8,128)(2,1)S(1)} %collective-permute-done.10.refs_3_), channel_id=1, source_target_pairs={{0,1},{1,0},{2,3},{3,2},{4,5},{5,4},{6,7},{7,6},{8,9},{9,8},{10,11... | collective-permute-start | bytes 221192 | tf_op jit(solution)/shard_map/ppermute | solution.py:171
  22.7 1.3 %collective-permute-start.16 = (bf16[288,128]{1,0:T(8,128)(2,1)S(1)}, bf16[288,128]{1,0:T(8,128)(2,1)S(1)}, u32[]{:S(2)}, u32[]{:S(2)}) collective-permute-start(bf16[288,128]{1,0:T(8,128)(2,1)S(1)} %collective-permute-done.8.refs_0_), channel_id=1, source_target_pairs={{0,1},{1,0},{2,3},{3,2},{4,5},{5,4},{6,7},{7,6},{8,9},{9,8},{10,11... | collective-permute-start | bytes 221192 | tf_op jit(solution)/shard_map/ppermute | solution.py:171
  23.9 4.4 %copy-start.2 = (f32[2,64,576]{2,1,0:T(8,128)S(1)}, f32[2,64,576]{2,1,0:T(8,128)}, u32[]{:S(2)}) copy-start(f32[2,64,576]{2,1,0:T(8,128)} %momentum_ref.3) | copy-start | bytes 884740
  26.6 4.5 %collective-permute-start.17 = (bf16[288,128]{1,0:T(8,128)(2,1)S(1)}, bf16[288,128]{1,0:T(8,128)(2,1)S(1)}, u32[]{:S(2)}, u32[]{:S(2)}) collective-permute-start(bf16[288,128]{1,0:T(8,128)(2,1)S(1)} %shard_map.47.rows_ref), channel_id=1, source_target_pairs={{0,16},{16,0},{1,17},{17,1},{2,18},{18,2},{3,19},{19,3},{4,20},{20... | collective-permute-start | bytes 221192 | tf_op jit(solution)/shard_map/ppermute | solution.py:171

commit v4 on v3

--- a/solution.py
+++ b/solution.py
@@ -176,19 +176,19 @@
 
 
 def gather_and_finish(block, kept, rows, width):
+    z1 = exchange(block, "dp", 4)
     z2 = exchange(block, "dp", 8)
-    z1 = exchange(block, "dp", 4)
     y0 = exchange(block, "dp", 2)
     beside = exchange(kept, "outer", 1)
     z2, beside = lax.optimization_barrier((z2, beside))
     z3 = exchange(z2, "dp", 4)
-    y1 = exchange(z1, "dp", 2)
     y2 = exchange(z2, "dp", 2)
+    y1 = exchange(y0, "dp", 4)
     y3 = exchange(z3, "dp", 2)
-    near = [block, z1, z2]
+    near = [block, z2, z1]
     near = near + [exchange(v, "dp", 1) for v in near]
     gram = gram_of(near, rows, width)
-    far = [y0, z3, y1, y2]
+    far = [z3, y2, y0, y1]
     far = far + [exchange(v, "dp", 1) for v in far]
     gram, last = lax.optimization_barrier((gram, y3))
     gram = gram_of(far, rows, width, gram)

time: 32.1 us -> 31.9 us (level)
  starting transfers between devices: 17.3 us -> 16.9 us
    ppermute x18, starting transfers between devices: 17.3 us -> 16.9 us  [exchange(): lax.ppermute(value, axis, [(at, at ^ distance) for at in range(size)])]
where the time goes in v4:
time: 31.9 us; the launch traced here: 31.7 us
  starting transfers between devices  16.9 us (53%)
  Pallas kernels  7.04 us (22%)
  waiting for transfers between devices  5.16 us (16%)
  local copies, waits for them, and re-layouts  1.94 us (6%)
  between operations  0.72 us (2%)
    ppermute x18, starting transfers between devices, exchange(): lax.ppermute(value, axis, [(at, at ^ distance) for at in range(size)])  16.9 us
    ppermute x18, waiting for transfers between devices, exchange(): lax.ppermute(value, axis, [(at, at ^ distance) for at in range(size)])  5.16 us
    pallas_call x1, Pallas kernels, finish(): pl.pallas_call(functools.partial(finish_kernel, rows), out_shape=jax.Shap...  2.55 us
    unnamed x6, local copies, waits for them, and re-layouts  1.94 us
    pallas_call x2, Pallas kernels, gram_of(): pl.pallas_call(functools.partial(gram_kernel, rows, len(before)), out_sha...  1.37 us
    pallas_call x1, Pallas kernels, two_pods(): pl.pallas_call(momentum_kernel, out_shape=both, in_specs=[VMEM] * 5, scra...  0.81 us
    pallas_call x1, Pallas kernels, two_pods(): pl.pallas_call(functools.partial(update_kernel, update_scale, False), out...  0.76 us
    pallas_call x1, Pallas kernels, two_pods(): pl.pallas_call(functools.partial(update_kernel, update_scale, True), out_...  0.76 us
  transfers between devices with their start and end apart: 18, of which 7 were waited for; matrix products, arithmetic and copies ran while one was open for 0% of the time, Pallas kernels for 11%

profile of v4, /device:TPU:0, one launch (start us, length us, event | category | flops | bytes accessed | tf_op | source)
XLA Modules:
  0.0 31.7 jit_solution(14668039648933576124)
XLA Ops:
  0.6 1.0 %copy-done = f32[1,2,64,576]{3,2,1,0:T(8,128)S(1)} copy-done((f32[1,2,64,576]{3,2,1,0:T(8,128)S(1)}, f32[1,2,64,576]{3,2,1,0:T(8,128)}, u32[]{:S(2)}) %copy-start) | copy-done | bytes 294936
  1.6 0.3 shard_map.42.away_ref
  1.9 3.0 %collective-permute-start = (bf16[288,128]{1,0:T(8,128)(2,1)S(1)}, bf16[288,128]{1,0:T(8,128)(2,1)S(1)}, u32[]{:S(2)}, u32[]{:S(2)}) collective-permute-start(bf16[288,128]{1,0:T(8,128)(2,1)S(1)} %shard_map.42.away_ref), channel_id=1, source_target_pairs={{0,16},{16,0},{1,17},{17,1},{2,18},{18,2},{3,19},{19,3},{4,20},{20... | collective-permute-start | bytes 221192 | tf_op jit(solution)/shard_map/ppermute | solution.py:171
  4.9 1.0 %copy-done.1 = f32[2,64,576]{2,1,0:T(8,128)S(1)} copy-done((f32[2,64,576]{2,1,0:T(8,128)S(1)}, f32[2,64,576]{2,1,0:T(8,128)}, u32[]{:S(2)}) %copy-start.1) | copy-done | bytes 294936
  5.9 0.5 %shard_map.41 = (bf16[288,128]{1,0:T(8,128)(2,1)S(1)}, f32[288,128]{1,0:T(8,128)S(1)}) custom-call(f32[2,64,576]{2,1,0:T(8,128)S(1)} %bitcast.2, f32[2,64,576]{2,1,0:T(8,128)S(1)} %copy-done.1), custom_call_target="tpu_custom_call" | custom-call | tf_op jit(solution)/shard_map/pallas_call | solution.py:258
  6.4 0.1 collective-permute-start.2
  6.4 0.8 %collective-permute-done.arrived_ref = bf16[288,128]{1,0:T(8,128)(2,1)S(1)} collective-permute-done((bf16[288,128]{1,0:T(8,128)(2,1)S(1)}, bf16[288,128]{1,0:T(8,128)(2,1)S(1)}, u32[]{:S(2)}, u32[]{:S(2)}) %collective-permute-start) | collective-permute-done | bytes 73760 | tf_op jit(solution)/shard_map/ppermute | solution.py:171
  7.2 3.2 %collective-permute-start.1 = (bf16[288,128]{1,0:T(8,128)(2,1)S(1)}, bf16[288,128]{1,0:T(8,128)(2,1)S(1)}, u32[]{:S(2)}, u32[]{:S(2)}) collective-permute-start(bf16[288,128]{1,0:T(8,128)(2,1)S(1)} %shard_map.43.refs_0_.rows_ref), channel_id=1, source_target_pairs={{0,8},{1,9},{2,10},{3,11},{4,12},{5,13},{6,14},{7,15},{8,0},{9,1},... | collective-permute-start | bytes 221192 | tf_op jit(solution)/shard_map/ppermute | solution.py:171
  10.4 1.6 %collective-permute-start.3 = (bf16[288,128]{1,0:T(8,128)(2,1)S(1)}, bf16[288,128]{1,0:T(8,128)(2,1)S(1)}, u32[]{:S(2)}, u32[]{:S(2)}) collective-permute-start(bf16[288,128]{1,0:T(8,128)(2,1)S(1)} %shard_map.43.refs_0_.rows_ref), channel_id=1, source_target_pairs={{0,4},{1,5},{2,6},{3,7},{4,0},{5,1},{6,2},{7,3},{8,12},{9,13},{10,... | collective-permute-start | bytes 221192 | tf_op jit(solution)/shard_map/ppermute | solution.py:171
  12.0 0.0 collective-permute-start.4
  12.0 1.5 %collective-permute-start.10 = (bf16[288,128]{1,0:T(8,128)(2,1)S(1)}, bf16[288,128]{1,0:T(8,128)(2,1)S(1)}, u32[]{:S(2)}, u32[]{:S(2)}) collective-permute-start(bf16[288,128]{1,0:T(8,128)(2,1)S(1)} %shard_map.43.refs_0_.rows_ref), channel_id=1, source_target_pairs={{0,2},{1,3},{2,0},{3,1},{4,6},{5,7},{6,4},{7,5},{8,10},{9,11},{10,... | collective-permute-start | bytes 221192 | tf_op jit(solution)/shard_map/ppermute | solution.py:171
  13.5 1.1 %collective-permute-start.7 = (bf16[288,128]{1,0:T(8,128)(2,1)S(1)}, bf16[288,128]{1,0:T(8,128)(2,1)S(1)}, u32[]{:S(2)}, u32[]{:S(2)}) collective-permute-start(bf16[288,128]{1,0:T(8,128)(2,1)S(1)} %collective-permute-done.1.refs_1_), channel_id=1, source_target_pairs={{0,4},{1,5},{2,6},{3,7},{4,0},{5,1},{6,2},{7,3},{8,12},{9,13},{10,... | collective-permute-start | bytes 221192 | tf_op jit(solution)/shard_map/ppermute | solution.py:171
  14.7 0.1 collective-permute-done.3.refs_2_
  14.8 0.4 %collective-permute-start.6 = (bf16[288,128]{1,0:T(8,128)(2,1)S(1)}, bf16[288,128]{1,0:T(8,128)(2,1)S(1)}, u32[]{:S(2)}, u32[]{:S(2)}) collective-permute-start(bf16[288,128]{1,0:T(8,128)(2,1)S(1)} %collective-permute-done.3.refs_2_), channel_id=1, source_target_pairs={{0,1},{1,0},{2,3},{3,2},{4,5},{5,4},{6,7},{7,6},{8,9},{9,8},{10,11... | collective-permute-start | bytes 221192 | tf_op jit(solution)/shard_map/ppermute | solution.py:171
  15.2 1.5 %collective-permute-start.9 = (bf16[288,128]{1,0:T(8,128)(2,1)S(1)}, bf16[288,128]{1,0:T(8,128)(2,1)S(1)}, u32[]{:S(2)}, u32[]{:S(2)}) collective-permute-start(bf16[288,128]{1,0:T(8,128)(2,1)S(1)} %collective-permute-done.1.refs_1_), channel_id=1, source_target_pairs={{0,2},{1,3},{2,0},{3,1},{4,6},{5,7},{6,4},{7,5},{8,10},{9,11},{10,... | collective-permute-start | bytes 221192 | tf_op jit(solution)/shard_map/ppermute | solution.py:171
  16.7 1.7 %collective-permute-start.11 = (bf16[288,128]{1,0:T(8,128)(2,1)S(1)}, bf16[288,128]{1,0:T(8,128)(2,1)S(1)}, u32[]{:S(2)}, u32[]{:S(2)}) collective-permute-start(bf16[288,128]{1,0:T(8,128)(2,1)S(1)} %collective-permute-done.10.refs_3_), channel_id=1, source_target_pairs={{0,4},{1,5},{2,6},{3,7},{4,0},{5,1},{6,2},{7,3},{8,12},{9,13},{10,... | collective-permute-start | bytes 221192 | tf_op jit(solution)/shard_map/ppermute | solution.py:171
  18.5 0.5 %collective-permute-start.8 = (bf16[288,128]{1,0:T(8,128)(2,1)S(1)}, bf16[288,128]{1,0:T(8,128)(2,1)S(1)}, u32[]{:S(2)}, u32[]{:S(2)}) collective-permute-start(bf16[288,128]{1,0:T(8,128)(2,1)S(1)} %collective-permute-done.7.refs_1_), channel_id=1, source_target_pairs={{0,2},{1,3},{2,0},{3,1},{4,6},{5,7},{6,4},{7,5},{8,10},{9,11},{10,... | collective-permute-start | bytes 221192 | tf_op jit(solution)/shard_map/ppermute | solution.py:171
  19.0 0.5 %collective-permute-start.12 = (bf16[288,128]{1,0:T(8,128)(2,1)S(1)}, bf16[288,128]{1,0:T(8,128)(2,1)S(1)}, u32[]{:S(2)}, u32[]{:S(2)}) collective-permute-start(bf16[288,128]{1,0:T(8,128)(2,1)S(1)} %collective-permute-done.7.refs_1_), channel_id=1, source_target_pairs={{0,1},{1,0},{2,3},{3,2},{4,5},{5,4},{6,7},{7,6},{8,9},{9,8},{10,11... | collective-permute-start | bytes 221192 | tf_op jit(solution)/shard_map/ppermute | solution.py:171
  19.5 0.1 collective-permute-done.9.refs_2_
  19.5 0.0 collective-permute-start.13
  19.6 1.5 %collective-permute-done.11.refs_4_ = bf16[288,128]{1,0:T(8,128)(2,1)S(1)} collective-permute-done((bf16[288,128]{1,0:T(8,128)(2,1)S(1)}, bf16[288,128]{1,0:T(8,128)(2,1)S(1)}, u32[]{:S(2)}, u32[]{:S(2)}) %collective-permute-start.11) | collective-permute-done | bytes 73760 | tf_op jit(solution)/shard_map/ppermute | solution.py:171
  21.1 0.7 %shard_map.45.refs_0_ = f32[576,576]{1,0:T(8,128)S(1)} custom-call(bf16[288,128]{1,0:T(8,128)(2,1)S(1)} %shard_map.43.refs_0_.rows_ref, bf16[288,128]{1,0:T(8,128)(2,1)S(1)} %collective-permute-done.1.refs_1_, bf16[288,128]{1,0:T(8,128)(2,1)S(1)} %collective-permute-done.3.refs_2_, bf16[288,128]{1,0:T(8,128)(2,1)S(1)} %collective-permute-done.4.refs_3_, ...), custom_call_target="tpu_custom_call" | custom-call | tf_op jit(solution)/shard_map/pallas_call | solution.py:109
  21.8 1.0 %collective-permute-done.8.refs_0_ = bf16[288,128]{1,0:T(8,128)(2,1)S(1)} collective-permute-done((bf16[288,128]{1,0:T(8,128)(2,1)S(1)}, bf16[288,128]{1,0:T(8,128)(2,1)S(1)}, u32[]{:S(2)}, u32[]{:S(2)}) %collective-permute-start.8) | collective-permute-done | bytes 73760 | tf_op jit(solution)/shard_map/ppermute | solution.py:171
  22.8 0.7 %shard_map.46.sum_ref = f32[576,576]{1,0:T(8,128)S(1)} custom-call(f32[576,576]{1,0:T(8,128)S(1)} %shard_map.45.refs_0_, bf16[288,128]{1,0:T(8,128)(2,1)S(1)} %collective-permute-done.7.refs_1_, bf16[288,128]{1,0:T(8,128)(2,1)S(1)} %collective-permute-done.9.refs_2_, bf16[288,128]{1,0:T(8,128)(2,1)S(1)} %collective-permute-done.10.refs_3_, ...), custom_call_target="tpu_custom_call" | custom-call | tf_op jit(solution)/shard_map/pallas_call | solution.py:109
  23.5 0.0 copy-start.2
  23.6 0.5 %collective-permute-done.16.refs_1_ = bf16[288,128]{1,0:T(8,128)(2,1)S(1)} collective-permute-done((bf16[288,128]{1,0:T(8,128)(2,1)S(1)}, bf16[288,128]{1,0:T(8,128)(2,1)S(1)}, u32[]{:S(2)}, u32[]{:S(2)}) %collective-permute-start.16) | collective-permute-done | bytes 73760 | tf_op jit(solution)/shard_map/ppermute | solution.py:171
  24.1 2.5 %shard_map.47.rows_ref = bf16[288,128]{1,0:T(8,128)(2,1)S(1)} custom-call(f32[576,576]{1,0:T(8,128)S(1)} %shard_map.46.sum_ref, bf16[288,128]{1,0:T(8,128)(2,1)S(1)} %shard_map.43.refs_0_.rows_ref, bf16[288,128]{1,0:T(8,128)(2,1)S(1)} %collective-permute-done.8.refs_0_, bf16[288,128]{1,0:T(8,128)(2,1)S(1)} %collective-permute-done.16.refs_1_), custom_call_target="tpu_custom_call" | custom-call | tf_op jit(solution)/shard_map/pallas_call | solution.py:127
  26.6 1.7 %collective-permute-start.17 = (bf16[288,128]{1,0:T(8,128)(2,1)S(1)}, bf16[288,128]{1,0:T(8,128)(2,1)S(1)}, u32[]{:S(2)}, u32[]{:S(2)}) collective-permute-start(bf16[288,128]{1,0:T(8,128)(2,1)S(1)} %shard_map.47.rows_ref), channel_id=1, source_target_pairs={{0,16},{16,0},{1,17},{17,1},{2,18},{18,2},{3,19},{19,3},{4,20},{20... | collective-permute-start | bytes 221192 | tf_op jit(solution)/shard_map/ppermute | solution.py:171
  28.3 0.8 %shard_map.44 = f32[2,64,576]{2,1,0:T(8,128)} custom-call(f32[2,64,576]{2,1,0:T(8,128)S(1)} %copy-done.2, bf16[288,128]{1,0:T(8,128)(2,1)S(1)} %get-tuple-element.8.kept_ref, bf16[288,128]{1,0:T(8,128)(2,1)S(1)} %collective-permute-done.arrived_ref, bf16[288,128]{1,0:T(8,128)(2,1)S(1)} %shard_map.42.away_ref, ...), custom_call_target="tpu_custom_call" | custom-call | tf_op jit(solution)/shard_map/pallas_call | solution.py:272
  29.1 0.8 %shard_map.48.refs_0_ = f32[2,64,576]{2,1,0:T(8,128)} custom-call(bf16[288,128]{1,0:T(8,128)(2,1)S(1)} %shard_map.47.rows_ref), custom_call_target="tpu_custom_call" | custom-call | tf_op jit(solution)/shard_map/pallas_call | solution.py:282
  29.9 1.1 %collective-permute-done.17.rows_ref = bf16[288,128]{1,0:T(8,128)(2,1)S(1)} collective-permute-done((bf16[288,128]{1,0:T(8,128)(2,1)S(1)}, bf16[288,128]{1,0:T(8,128)(2,1)S(1)}, u32[]{:S(2)}, u32[]{:S(2)}) %collective-permute-start.17) | collective-permute-done | bytes 73760 | tf_op jit(solution)/shard_map/ppermute | solution.py:171
  31.0 0.8 %shard_map.49 = f32[2,64,576]{2,1,0:T(8,128)} custom-call(bf16[288,128]{1,0:T(8,128)(2,1)S(1)} %collective-permute-done.17.rows_ref, f32[2,64,576]{2,1,0:T(8,128)} %shard_map.48.refs_0_), custom_call_target="tpu_custom_call", output_to_operand_aliasing={{}: (1, {})} | custom-call | tf_op jit(solution)/shard_map/pallas_call | solution.py:290
  (19 shorter events, 0.1 us)
Async XLA Ops:
  0.6 1.0 %copy-start = (f32[1,2,64,576]{3,2,1,0:T(8,128)S(1)}, f32[1,2,64,576]{3,2,1,0:T(8,128)}, u32[]{:S(2)}) copy-start(f32[1,2,64,576]{3,2,1,0:T(8,128)} %param.2) | copy-start | bytes 884740
  1.9 5.3 %collective-permute-start = (bf16[288,128]{1,0:T(8,128)(2,1)S(1)}, bf16[288,128]{1,0:T(8,128)(2,1)S(1)}, u32[]{:S(2)}, u32[]{:S(2)}) collective-permute-start(bf16[288,128]{1,0:T(8,128)(2,1)S(1)} %shard_map.42.away_ref), channel_id=1, source_target_pairs={{0,16},{16,0},{1,17},{17,1},{2,18},{18,2},{3,19},{19,3},{4,20},{20... | collective-permute-start | bytes 221192 | tf_op jit(solution)/shard_map/ppermute | solution.py:171
  4.9 1.0 %copy-start.1 = (f32[2,64,576]{2,1,0:T(8,128)S(1)}, f32[2,64,576]{2,1,0:T(8,128)}, u32[]{:S(2)}) copy-start(f32[2,64,576]{2,1,0:T(8,128)} %momentum_ref.3) | copy-start | bytes 884740
  6.4 7.2 %collective-permute-start.2 = (bf16[288,128]{1,0:T(8,128)(2,1)S(1)}, bf16[288,128]{1,0:T(8,128)(2,1)S(1)}, u32[]{:S(2)}, u32[]{:S(2)}) collective-permute-start(bf16[288,128]{1,0:T(8,128)(2,1)S(1)} %get-tuple-element.8.kept_ref), channel_id=1, source_target_pairs={{0,16},{16,0},{1,17},{17,1},{2,18},{18,2},{3,19},{19,3},{4,20},{20... | collective-permute-start | bytes 221192 | tf_op jit(solution)/shard_map/ppermute | solution.py:171
  7.2 6.3 %collective-permute-start.1 = (bf16[288,128]{1,0:T(8,128)(2,1)S(1)}, bf16[288,128]{1,0:T(8,128)(2,1)S(1)}, u32[]{:S(2)}, u32[]{:S(2)}) collective-permute-start(bf16[288,128]{1,0:T(8,128)(2,1)S(1)} %shard_map.43.refs_0_.rows_ref), channel_id=1, source_target_pairs={{0,8},{1,9},{2,10},{3,11},{4,12},{5,13},{6,14},{7,15},{8,0},{9,1},... | collective-permute-start | bytes 221192 | tf_op jit(solution)/shard_map/ppermute | solution.py:171
  10.4 4.4 %collective-permute-start.3 = (bf16[288,128]{1,0:T(8,128)(2,1)S(1)}, bf16[288,128]{1,0:T(8,128)(2,1)S(1)}, u32[]{:S(2)}, u32[]{:S(2)}) collective-permute-start(bf16[288,128]{1,0:T(8,128)(2,1)S(1)} %shard_map.43.refs_0_.rows_ref), channel_id=1, source_target_pairs={{0,4},{1,5},{2,6},{3,7},{4,0},{5,1},{6,2},{7,3},{8,12},{9,13},{10,... | collective-permute-start | bytes 221192 | tf_op jit(solution)/shard_map/ppermute | solution.py:171
  12.0 3.2 %collective-permute-start.4 = (bf16[288,128]{1,0:T(8,128)(2,1)S(1)}, bf16[288,128]{1,0:T(8,128)(2,1)S(1)}, u32[]{:S(2)}, u32[]{:S(2)}) collective-permute-start(bf16[288,128]{1,0:T(8,128)(2,1)S(1)} %shard_map.43.refs_0_.rows_ref), channel_id=1, source_target_pairs={{0,1},{1,0},{2,3},{3,2},{4,5},{5,4},{6,7},{7,6},{8,9},{9,8},{10,11... | collective-permute-start | bytes 221192 | tf_op jit(solution)/shard_map/ppermute | solution.py:171
  12.0 4.7 %collective-permute-start.10 = (bf16[288,128]{1,0:T(8,128)(2,1)S(1)}, bf16[288,128]{1,0:T(8,128)(2,1)S(1)}, u32[]{:S(2)}, u32[]{:S(2)}) collective-permute-start(bf16[288,128]{1,0:T(8,128)(2,1)S(1)} %shard_map.43.refs_0_.rows_ref), channel_id=1, source_target_pairs={{0,2},{1,3},{2,0},{3,1},{4,6},{5,7},{6,4},{7,5},{8,10},{9,11},{10,... | collective-permute-start | bytes 221192 | tf_op jit(solution)/shard_map/ppermute | solution.py:171
  13.5 4.9 %collective-permute-start.7 = (bf16[288,128]{1,0:T(8,128)(2,1)S(1)}, bf16[288,128]{1,0:T(8,128)(2,1)S(1)}, u32[]{:S(2)}, u32[]{:S(2)}) collective-permute-start(bf16[288,128]{1,0:T(8,128)(2,1)S(1)} %collective-permute-done.1.refs_1_), channel_id=1, source_target_pairs={{0,4},{1,5},{2,6},{3,7},{4,0},{5,1},{6,2},{7,3},{8,12},{9,13},{10,... | collective-permute-start | bytes 221192 | tf_op jit(solution)/shard_map/ppermute | solution.py:171
  14.7 4.3 %collective-permute-start.5 = (bf16[288,128]{1,0:T(8,128)(2,1)S(1)}, bf16[288,128]{1,0:T(8,128)(2,1)S(1)}, u32[]{:S(2)}, u32[]{:S(2)}) collective-permute-start(bf16[288,128]{1,0:T(8,128)(2,1)S(1)} %collective-permute-done.1.refs_1_), channel_id=1, source_target_pairs={{0,1},{1,0},{2,3},{3,2},{4,5},{5,4},{6,7},{7,6},{8,9},{9,8},{10,11... | collective-permute-start | bytes 221192 | tf_op jit(solution)/shard_map/ppermute | solution.py:171
  14.8 4.2 %collective-permute-start.6 = (bf16[288,128]{1,0:T(8,128)(2,1)S(1)}, bf16[288,128]{1,0:T(8,128)(2,1)S(1)}, u32[]{:S(2)}, u32[]{:S(2)}) collective-permute-start(bf16[288,128]{1,0:T(8,128)(2,1)S(1)} %collective-permute-done.3.refs_2_), channel_id=1, source_target_pairs={{0,1},{1,0},{2,3},{3,2},{4,5},{5,4},{6,7},{7,6},{8,9},{9,8},{10,11... | collective-permute-start | bytes 221192 | tf_op jit(solution)/shard_map/ppermute | solution.py:171
  15.2 4.4 %collective-permute-start.9 = (bf16[288,128]{1,0:T(8,128)(2,1)S(1)}, bf16[288,128]{1,0:T(8,128)(2,1)S(1)}, u32[]{:S(2)}, u32[]{:S(2)}) collective-permute-start(bf16[288,128]{1,0:T(8,128)(2,1)S(1)} %collective-permute-done.1.refs_1_), channel_id=1, source_target_pairs={{0,2},{1,3},{2,0},{3,1},{4,6},{5,7},{6,4},{7,5},{8,10},{9,11},{10,... | collective-permute-start | bytes 221192 | tf_op jit(solution)/shard_map/ppermute | solution.py:171
  16.7 4.4 %collective-permute-start.11 = (bf16[288,128]{1,0:T(8,128)(2,1)S(1)}, bf16[288,128]{1,0:T(8,128)(2,1)S(1)}, u32[]{:S(2)}, u32[]{:S(2)}) collective-permute-start(bf16[288,128]{1,0:T(8,128)(2,1)S(1)} %collective-permute-done.10.refs_3_), channel_id=1, source_target_pairs={{0,4},{1,5},{2,6},{3,7},{4,0},{5,1},{6,2},{7,3},{8,12},{9,13},{10,... | collective-permute-start | bytes 221192 | tf_op jit(solution)/shard_map/ppermute | solution.py:171
  18.5 4.4 %collective-permute-start.8 = (bf16[288,128]{1,0:T(8,128)(2,1)S(1)}, bf16[288,128]{1,0:T(8,128)(2,1)S(1)}, u32[]{:S(2)}, u32[]{:S(2)}) collective-permute-start(bf16[288,128]{1,0:T(8,128)(2,1)S(1)} %collective-permute-done.7.refs_1_), channel_id=1, source_target_pairs={{0,2},{1,3},{2,0},{3,1},{4,6},{5,7},{6,4},{7,5},{8,10},{9,11},{10,... | collective-permute-start | bytes 221192 | tf_op jit(solution)/shard_map/ppermute | solution.py:171
  19.0 3.8 %collective-permute-start.14 = (bf16[288,128]{1,0:T(8,128)(2,1)S(1)}, bf16[288,128]{1,0:T(8,128)(2,1)S(1)}, u32[]{:S(2)}, u32[]{:S(2)}) collective-permute-start(bf16[288,128]{1,0:T(8,128)(2,1)S(1)} %collective-permute-done.10.refs_3_), channel_id=1, source_target_pairs={{0,1},{1,0},{2,3},{3,2},{4,5},{5,4},{6,7},{7,6},{8,9},{9,8},{10,11... | collective-permute-start | bytes 221192 | tf_op jit(solution)/shard_map/ppermute | solution.py:171
  19.0 3.8 %collective-permute-start.12 = (bf16[288,128]{1,0:T(8,128)(2,1)S(1)}, bf16[288,128]{1,0:T(8,128)(2,1)S(1)}, u32[]{:S(2)}, u32[]{:S(2)}) collective-permute-start(bf16[288,128]{1,0:T(8,128)(2,1)S(1)} %collective-permute-done.7.refs_1_), channel_id=1, source_target_pairs={{0,1},{1,0},{2,3},{3,2},{4,5},{5,4},{6,7},{7,6},{8,9},{9,8},{10,11... | collective-permute-start | bytes 221192 | tf_op jit(solution)/shard_map/ppermute | solution.py:171
  19.5 3.3 %collective-permute-start.13 = (bf16[288,128]{1,0:T(8,128)(2,1)S(1)}, bf16[288,128]{1,0:T(8,128)(2,1)S(1)}, u32[]{:S(2)}, u32[]{:S(2)}) collective-permute-start(bf16[288,128]{1,0:T(8,128)(2,1)S(1)} %collective-permute-done.9.refs_2_), channel_id=1, source_target_pairs={{0,1},{1,0},{2,3},{3,2},{4,5},{5,4},{6,7},{7,6},{8,9},{9,8},{10,11... | collective-permute-start | bytes 221192 | tf_op jit(solution)/shard_map/ppermute | solution.py:171
  21.1 1.7 %collective-permute-start.15 = (bf16[288,128]{1,0:T(8,128)(2,1)S(1)}, bf16[288,128]{1,0:T(8,128)(2,1)S(1)}, u32[]{:S(2)}, u32[]{:S(2)}) collective-permute-start(bf16[288,128]{1,0:T(8,128)(2,1)S(1)} %collective-permute-done.11.refs_4_), channel_id=1, source_target_pairs={{0,1},{1,0},{2,3},{3,2},{4,5},{5,4},{6,7},{7,6},{8,9},{9,8},{10,11... | collective-permute-start | bytes 221192 | tf_op jit(solution)/shard_map/ppermute | solution.py:171
  22.8 1.3 %collective-permute-start.16 = (bf16[288,128]{1,0:T(8,128)(2,1)S(1)}, bf16[288,128]{1,0:T(8,128)(2,1)S(1)}, u32[]{:S(2)}, u32[]{:S(2)}) collective-permute-start(bf16[288,128]{1,0:T(8,128)(2,1)S(1)} %collective-permute-done.8.refs_0_), channel_id=1, source_target_pairs={{0,1},{1,0},{2,3},{3,2},{4,5},{5,4},{6,7},{7,6},{8,9},{9,8},{10,11... | collective-permute-start | bytes 221192 | tf_op jit(solution)/shard_map/ppermute | solution.py:171
  23.5 4.7 %copy-start.2 = (f32[2,64,576]{2,1,0:T(8,128)S(1)}, f32[2,64,576]{2,1,0:T(8,128)}, u32[]{:S(2)}) copy-start(f32[2,64,576]{2,1,0:T(8,128)} %momentum_ref.3) | copy-start | bytes 884740
  26.6 4.4 %collective-permute-start.17 = (bf16[288,128]{1,0:T(8,128)(2,1)S(1)}, bf16[288,128]{1,0:T(8,128)(2,1)S(1)}, u32[]{:S(2)}, u32[]{:S(2)}) collective-permute-start(bf16[288,128]{1,0:T(8,128)(2,1)S(1)} %shard_map.47.rows_ref), channel_id=1, source_target_pairs={{0,16},{16,0},{1,17},{17,1},{2,18},{18,2},{3,19},{19,3},{4,20},{20... | collective-permute-start | bytes 221192 | tf_op jit(solution)/shard_map/ppermute | solution.py:171

commit v5 on v3

--- a/solution.py
+++ b/solution.py
@@ -195,11 +195,8 @@
     return finish(gram, block, [last, exchange(last, "dp", 1)], rows, width), beside
 
 
-def away_kernel(grads_ref, away_ref, held, done):
-    copy = pltpu.make_async_copy(grads_ref.at[1 - lax.axis_index("outer")], held, done)
-    copy.start()
-    copy.wait()
-    pack(held[...].astype(BF16), away_ref)
+def away_kernel(grads_ref, away_ref):
+    pack(grads_ref[1 - lax.axis_index("outer")].astype(BF16), away_ref)
 
 
 def base_kernel(grads_ref, momentum_ref, kept_ref, base_ref, held, done):
@@ -249,9 +246,8 @@
     away = pl.pallas_call(
         away_kernel,
         out_shape=rounded,
-        in_specs=[anywhere],
-        out_specs=VMEM,
-        scratch_shapes=[pltpu.VMEM(one, F32), pltpu.SemaphoreType.DMA],
+        in_specs=[VMEM],
+        out_specs=VMEM,
         compiler_params=SMALL,
     )(local)
     arrived = exchange(away, "outer", 1)

time: 32.1 us -> 31.8 us (level)
  no operation moved by 1% of the time
where the time goes in v5:
time: 31.8 us; the launch traced here: 31.6 us
  starting transfers between devices  17.2 us (54%)
  Pallas kernels  6.84 us (22%)
  waiting for transfers between devices  4.9 us (15%)
  local copies, waits for them, and re-layouts  1.94 us (6%)
  between operations  0.71 us (2%)
    ppermute x18, starting transfers between devices, exchange(): lax.ppermute(value, axis, [(at, at ^ distance) for at in range(size)])  17.2 us
    ppermute x18, waiting for transfers between devices, exchange(): lax.ppermute(value, axis, [(at, at ^ distance) for at in range(size)])  4.9 us
    pallas_call x1, Pallas kernels, finish(): pl.pallas_call(functools.partial(finish_kernel, rows), out_shape=jax.Shap...  2.54 us
    unnamed x6, local copies, waits for them, and re-layouts  1.94 us
    pallas_call x2, Pallas kernels, gram_of(): pl.pallas_call(functools.partial(gram_kernel, rows, len(before)), out_sha...  1.37 us
    pallas_call x1, Pallas kernels, two_pods(): pl.pallas_call(momentum_kernel, out_shape=both, in_specs=[VMEM] * 5, scra...  0.81 us
    pallas_call x1, Pallas kernels, two_pods(): pl.pallas_call(functools.partial(update_kernel, update_scale, False), out...  0.76 us
    pallas_call x1, Pallas kernels, two_pods(): pl.pallas_call(functools.partial(update_kernel, update_scale, True), out_...  0.76 us
  transfers between devices with their start and end apart: 18, of which 7 were waited for; matrix products, arithmetic and copies ran while one was open for 0% of the time, Pallas kernels for 11%

profile of v5, /device:TPU:0, one launch (start us, length us, event | category | flops | bytes accessed | tf_op | source)
XLA Modules:
  0.0 31.6 jit_solution(8121396761215385517)
XLA Ops:
  0.6 1.0 %copy-done = f32[1,2,64,576]{3,2,1,0:T(8,128)S(1)} copy-done((f32[1,2,64,576]{3,2,1,0:T(8,128)S(1)}, f32[1,2,64,576]{3,2,1,0:T(8,128)}, u32[]{:S(2)}) %copy-start) | copy-done | bytes 294936
  1.6 0.1 shard_map.42.away_ref
  1.7 2.9 %collective-permute-start = (bf16[288,128]{1,0:T(8,128)(2,1)S(1)}, bf16[288,128]{1,0:T(8,128)(2,1)S(1)}, u32[]{:S(2)}, u32[]{:S(2)}) collective-permute-start(bf16[288,128]{1,0:T(8,128)(2,1)S(1)} %shard_map.42.away_ref), channel_id=1, source_target_pairs={{0,16},{16,0},{1,17},{17,1},{2,18},{18,2},{3,19},{19,3},{4,20},{20... | collective-permute-start | bytes 221192 | tf_op jit(solution)/shard_map/ppermute | solution.py:171
  4.6 1.0 %copy-done.1 = f32[2,64,576]{2,1,0:T(8,128)S(1)} copy-done((f32[2,64,576]{2,1,0:T(8,128)S(1)}, f32[2,64,576]{2,1,0:T(8,128)}, u32[]{:S(2)}) %copy-start.1) | copy-done | bytes 294936
  5.6 0.5 %shard_map.41 = (bf16[288,128]{1,0:T(8,128)(2,1)S(1)}, f32[288,128]{1,0:T(8,128)S(1)}) custom-call(f32[2,64,576]{2,1,0:T(8,128)S(1)} %bitcast.2, f32[2,64,576]{2,1,0:T(8,128)S(1)} %copy-done.1), custom_call_target="tpu_custom_call" | custom-call | tf_op jit(solution)/shard_map/pallas_call | solution.py:254
  6.1 0.1 collective-permute-start.2
  6.2 0.8 %collective-permute-done.arrived_ref = bf16[288,128]{1,0:T(8,128)(2,1)S(1)} collective-permute-done((bf16[288,128]{1,0:T(8,128)(2,1)S(1)}, bf16[288,128]{1,0:T(8,128)(2,1)S(1)}, u32[]{:S(2)}, u32[]{:S(2)}) %collective-permute-start) | collective-permute-done | bytes 73760 | tf_op jit(solution)/shard_map/ppermute | solution.py:171
  7.0 3.2 %collective-permute-start.1 = (bf16[288,128]{1,0:T(8,128)(2,1)S(1)}, bf16[288,128]{1,0:T(8,128)(2,1)S(1)}, u32[]{:S(2)}, u32[]{:S(2)}) collective-permute-start(bf16[288,128]{1,0:T(8,128)(2,1)S(1)} %shard_map.43.refs_0_.rows_ref), channel_id=1, source_target_pairs={{0,8},{1,9},{2,10},{3,11},{4,12},{5,13},{6,14},{7,15},{8,0},{9,1},... | collective-permute-start | bytes 221192 | tf_op jit(solution)/shard_map/ppermute | solution.py:171
  10.2 1.6 %collective-permute-start.3 = (bf16[288,128]{1,0:T(8,128)(2,1)S(1)}, bf16[288,128]{1,0:T(8,128)(2,1)S(1)}, u32[]{:S(2)}, u32[]{:S(2)}) collective-permute-start(bf16[288,128]{1,0:T(8,128)(2,1)S(1)} %shard_map.43.refs_0_.rows_ref), channel_id=1, source_target_pairs={{0,4},{1,5},{2,6},{3,7},{4,0},{5,1},{6,2},{7,3},{8,12},{9,13},{10,... | collective-permute-start | bytes 221192 | tf_op jit(solution)/shard_map/ppermute | solution.py:171
  11.7 0.0 collective-permute-start.4
  11.8 1.5 %collective-permute-start.9 = (bf16[288,128]{1,0:T(8,128)(2,1)S(1)}, bf16[288,128]{1,0:T(8,128)(2,1)S(1)}, u32[]{:S(2)}, u32[]{:S(2)}) collective-permute-start(bf16[288,128]{1,0:T(8,128)(2,1)S(1)} %shard_map.43.refs_0_.rows_ref), channel_id=1, source_target_pairs={{0,2},{1,3},{2,0},{3,1},{4,6},{5,7},{6,4},{7,5},{8,10},{9,11},{10,... | collective-permute-start | bytes 221192 | tf_op jit(solution)/shard_map/ppermute | solution.py:171
  13.3 1.1 %collective-permute-start.7 = (bf16[288,128]{1,0:T(8,128)(2,1)S(1)}, bf16[288,128]{1,0:T(8,128)(2,1)S(1)}, u32[]{:S(2)}, u32[]{:S(2)}) collective-permute-start(bf16[288,128]{1,0:T(8,128)(2,1)S(1)} %collective-permute-done.1.refs_2_), channel_id=1, source_target_pairs={{0,4},{1,5},{2,6},{3,7},{4,0},{5,1},{6,2},{7,3},{8,12},{9,13},{10,... | collective-permute-start | bytes 221192 | tf_op jit(solution)/shard_map/ppermute | solution.py:171
  14.4 0.1 collective-permute-done.3.refs_1_
  14.5 0.4 %collective-permute-start.5 = (bf16[288,128]{1,0:T(8,128)(2,1)S(1)}, bf16[288,128]{1,0:T(8,128)(2,1)S(1)}, u32[]{:S(2)}, u32[]{:S(2)}) collective-permute-start(bf16[288,128]{1,0:T(8,128)(2,1)S(1)} %collective-permute-done.3.refs_1_), channel_id=1, source_target_pairs={{0,1},{1,0},{2,3},{3,2},{4,5},{5,4},{6,7},{7,6},{8,9},{9,8},{10,11... | collective-permute-start | bytes 221192 | tf_op jit(solution)/shard_map/ppermute | solution.py:171
  14.9 1.5 %collective-permute-start.11 = (bf16[288,128]{1,0:T(8,128)(2,1)S(1)}, bf16[288,128]{1,0:T(8,128)(2,1)S(1)}, u32[]{:S(2)}, u32[]{:S(2)}) collective-permute-start(bf16[288,128]{1,0:T(8,128)(2,1)S(1)} %collective-permute-done.1.refs_2_), channel_id=1, source_target_pairs={{0,2},{1,3},{2,0},{3,1},{4,6},{5,7},{6,4},{7,5},{8,10},{9,11},{10,... | collective-permute-start | bytes 221192 | tf_op jit(solution)/shard_map/ppermute | solution.py:171
  16.5 1.5 %collective-permute-start.10 = (bf16[288,128]{1,0:T(8,128)(2,1)S(1)}, bf16[288,128]{1,0:T(8,128)(2,1)S(1)}, u32[]{:S(2)}, u32[]{:S(2)}) collective-permute-start(bf16[288,128]{1,0:T(8,128)(2,1)S(1)} %collective-permute-done.3.refs_1_), channel_id=1, source_target_pairs={{0,2},{1,3},{2,0},{3,1},{4,6},{5,7},{6,4},{7,5},{8,10},{9,11},{10,... | collective-permute-start | bytes 221192 | tf_op jit(solution)/shard_map/ppermute | solution.py:171
  18.0 0.8 %collective-permute-start.8 = (bf16[288,128]{1,0:T(8,128)(2,1)S(1)}, bf16[288,128]{1,0:T(8,128)(2,1)S(1)}, u32[]{:S(2)}, u32[]{:S(2)}) collective-permute-start(bf16[288,128]{1,0:T(8,128)(2,1)S(1)} %collective-permute-done.7.refs_2_), channel_id=1, source_target_pairs={{0,2},{1,3},{2,0},{3,1},{4,6},{5,7},{6,4},{7,5},{8,10},{9,11},{10,... | collective-permute-start | bytes 221192 | tf_op jit(solution)/shard_map/ppermute | solution.py:171
  18.7 0.5 %collective-permute-start.13 = (bf16[288,128]{1,0:T(8,128)(2,1)S(1)}, bf16[288,128]{1,0:T(8,128)(2,1)S(1)}, u32[]{:S(2)}, u32[]{:S(2)}) collective-permute-start(bf16[288,128]{1,0:T(8,128)(2,1)S(1)} %collective-permute-done.7.refs_2_), channel_id=1, source_target_pairs={{0,1},{1,0},{2,3},{3,2},{4,5},{5,4},{6,7},{7,6},{8,9},{9,8},{10,11... | collective-permute-start | bytes 221192 | tf_op jit(solution)/shard_map/ppermute | solution.py:171
  19.2 0.6 %collective-permute-done.11.refs_4_ = bf16[288,128]{1,0:T(8,128)(2,1)S(1)} collective-permute-done((bf16[288,128]{1,0:T(8,128)(2,1)S(1)}, bf16[288,128]{1,0:T(8,128)(2,1)S(1)}, u32[]{:S(2)}, u32[]{:S(2)}) %collective-permute-start.11) | collective-permute-done | bytes 73760 | tf_op jit(solution)/shard_map/ppermute | solution.py:171
  19.8 1.8 %collective-permute-done.10.refs_3_ = bf16[288,128]{1,0:T(8,128)(2,1)S(1)} collective-permute-done((bf16[288,128]{1,0:T(8,128)(2,1)S(1)}, bf16[288,128]{1,0:T(8,128)(2,1)S(1)}, u32[]{:S(2)}, u32[]{:S(2)}) %collective-permute-start.10) | collective-permute-done | bytes 73760 | tf_op jit(solution)/shard_map/ppermute | solution.py:171
  21.6 0.7 %shard_map.45.refs_0_ = f32[576,576]{1,0:T(8,128)S(1)} custom-call(bf16[288,128]{1,0:T(8,128)(2,1)S(1)} %shard_map.43.refs_0_.rows_ref, bf16[288,128]{1,0:T(8,128)(2,1)S(1)} %collective-permute-done.3.refs_1_, bf16[288,128]{1,0:T(8,128)(2,1)S(1)} %collective-permute-done.1.refs_2_, bf16[288,128]{1,0:T(8,128)(2,1)S(1)} %collective-permute-done.4.refs_3_, ...), custom_call_target="tpu_custom_call" | custom-call | tf_op jit(solution)/shard_map/pallas_call | solution.py:109
  22.3 0.1 collective-permute-done.8.refs_0_
  22.4 0.4 %collective-permute-start.16 = (bf16[288,128]{1,0:T(8,128)(2,1)S(1)}, bf16[288,128]{1,0:T(8,128)(2,1)S(1)}, u32[]{:S(2)}, u32[]{:S(2)}) collective-permute-start(bf16[288,128]{1,0:T(8,128)(2,1)S(1)} %collective-permute-done.8.refs_0_), channel_id=1, source_target_pairs={{0,1},{1,0},{2,3},{3,2},{4,5},{5,4},{6,7},{7,6},{8,9},{9,8},{10,11... | collective-permute-start | bytes 221192 | tf_op jit(solution)/shard_map/ppermute | solution.py:171
  22.9 0.7 %shard_map.46.sum_ref = f32[576,576]{1,0:T(8,128)S(1)} custom-call(f32[576,576]{1,0:T(8,128)S(1)} %shard_map.45.refs_0_, bf16[288,128]{1,0:T(8,128)(2,1)S(1)} %collective-permute-done.9.refs_1_, bf16[288,128]{1,0:T(8,128)(2,1)S(1)} %collective-permute-done.7.refs_2_, bf16[288,128]{1,0:T(8,128)(2,1)S(1)} %collective-permute-done.10.refs_3_, ...), custom_call_target="tpu_custom_call" | custom-call | tf_op jit(solution)/shard_map/pallas_call | solution.py:109
  23.6 0.0 copy-start.2
  23.6 0.2 collective-permute-done.16.refs_1_
  23.8 2.5 %shard_map.47.rows_ref = bf16[288,128]{1,0:T(8,128)(2,1)S(1)} custom-call(f32[576,576]{1,0:T(8,128)S(1)} %shard_map.46.sum_ref, bf16[288,128]{1,0:T(8,128)(2,1)S(1)} %shard_map.43.refs_0_.rows_ref, bf16[288,128]{1,0:T(8,128)(2,1)S(1)} %collective-permute-done.8.refs_0_, bf16[288,128]{1,0:T(8,128)(2,1)S(1)} %collective-permute-done.16.refs_1_), custom_call_target="tpu_custom_call" | custom-call | tf_op jit(solution)/shard_map/pallas_call | solution.py:127
  26.3 1.7 %collective-permute-start.17 = (bf16[288,128]{1,0:T(8,128)(2,1)S(1)}, bf16[288,128]{1,0:T(8,128)(2,1)S(1)}, u32[]{:S(2)}, u32[]{:S(2)}) collective-permute-start(bf16[288,128]{1,0:T(8,128)(2,1)S(1)} %shard_map.47.rows_ref), channel_id=1, source_target_pairs={{0,16},{16,0},{1,17},{17,1},{2,18},{18,2},{3,19},{19,3},{4,20},{20... | collective-permute-start | bytes 221192 | tf_op jit(solution)/shard_map/ppermute | solution.py:171
  28.0 0.8 %shard_map.44 = f32[2,64,576]{2,1,0:T(8,128)} custom-call(f32[2,64,576]{2,1,0:T(8,128)S(1)} %copy-done.2, bf16[288,128]{1,0:T(8,128)(2,1)S(1)} %get-tuple-element.8.kept_ref, bf16[288,128]{1,0:T(8,128)(2,1)S(1)} %collective-permute-done.arrived_ref, bf16[288,128]{1,0:T(8,128)(2,1)S(1)} %shard_map.42.away_ref, ...), custom_call_target="tpu_custom_call" | custom-call | tf_op jit(solution)/shard_map/pallas_call | solution.py:268
  28.8 0.8 %shard_map.48.refs_0_ = f32[2,64,576]{2,1,0:T(8,128)} custom-call(bf16[288,128]{1,0:T(8,128)(2,1)S(1)} %shard_map.47.rows_ref), custom_call_target="tpu_custom_call" | custom-call | tf_op jit(solution)/shard_map/pallas_call | solution.py:278
  29.6 1.3 %collective-permute-done.17.rows_ref = bf16[288,128]{1,0:T(8,128)(2,1)S(1)} collective-permute-done((bf16[288,128]{1,0:T(8,128)(2,1)S(1)}, bf16[288,128]{1,0:T(8,128)(2,1)S(1)}, u32[]{:S(2)}, u32[]{:S(2)}) %collective-permute-start.17) | collective-permute-done | bytes 73760 | tf_op jit(solution)/shard_map/ppermute | solution.py:171
  30.9 0.8 %shard_map.49 = f32[2,64,576]{2,1,0:T(8,128)} custom-call(bf16[288,128]{1,0:T(8,128)(2,1)S(1)} %collective-permute-done.17.rows_ref, f32[2,64,576]{2,1,0:T(8,128)} %shard_map.48.refs_0_), custom_call_target="tpu_custom_call", output_to_operand_aliasing={{}: (1, {})} | custom-call | tf_op jit(solution)/shard_map/pallas_call | solution.py:286
  (19 shorter events, 0.1 us)
Async XLA Ops:
  0.6 1.0 %copy-start = (f32[1,2,64,576]{3,2,1,0:T(8,128)S(1)}, f32[1,2,64,576]{3,2,1,0:T(8,128)}, u32[]{:S(2)}) copy-start(f32[1,2,64,576]{3,2,1,0:T(8,128)} %param.2) | copy-start | bytes 884740
  1.7 5.3 %collective-permute-start = (bf16[288,128]{1,0:T(8,128)(2,1)S(1)}, bf16[288,128]{1,0:T(8,128)(2,1)S(1)}, u32[]{:S(2)}, u32[]{:S(2)}) collective-permute-start(bf16[288,128]{1,0:T(8,128)(2,1)S(1)} %shard_map.42.away_ref), channel_id=1, source_target_pairs={{0,16},{16,0},{1,17},{17,1},{2,18},{18,2},{3,19},{19,3},{4,20},{20... | collective-permute-start | bytes 221192 | tf_op jit(solution)/shard_map/ppermute | solution.py:171
  4.6 1.0 %copy-start.1 = (f32[2,64,576]{2,1,0:T(8,128)S(1)}, f32[2,64,576]{2,1,0:T(8,128)}, u32[]{:S(2)}) copy-start(f32[2,64,576]{2,1,0:T(8,128)} %momentum_ref.3) | copy-start | bytes 884740
  6.1 7.2 %collective-permute-start.2 = (bf16[288,128]{1,0:T(8,128)(2,1)S(1)}, bf16[288,128]{1,0:T(8,128)(2,1)S(1)}, u32[]{:S(2)}, u32[]{:S(2)}) collective-permute-start(bf16[288,128]{1,0:T(8,128)(2,1)S(1)} %get-tuple-element.8.kept_ref), channel_id=1, source_target_pairs={{0,16},{16,0},{1,17},{17,1},{2,18},{18,2},{3,19},{19,3},{4,20},{20... | collective-permute-start | bytes 221192 | tf_op jit(solution)/shard_map/ppermute | solution.py:171
  7.0 6.3 %collective-permute-start.1 = (bf16[288,128]{1,0:T(8,128)(2,1)S(1)}, bf16[288,128]{1,0:T(8,128)(2,1)S(1)}, u32[]{:S(2)}, u32[]{:S(2)}) collective-permute-start(bf16[288,128]{1,0:T(8,128)(2,1)S(1)} %shard_map.43.refs_0_.rows_ref), channel_id=1, source_target_pairs={{0,8},{1,9},{2,10},{3,11},{4,12},{5,13},{6,14},{7,15},{8,0},{9,1},... | collective-permute-start | bytes 221192 | tf_op jit(solution)/shard_map/ppermute | solution.py:171
  10.2 4.4 %collective-permute-start.3 = (bf16[288,128]{1,0:T(8,128)(2,1)S(1)}, bf16[288,128]{1,0:T(8,128)(2,1)S(1)}, u32[]{:S(2)}, u32[]{:S(2)}) collective-permute-start(bf16[288,128]{1,0:T(8,128)(2,1)S(1)} %shard_map.43.refs_0_.rows_ref), channel_id=1, source_target_pairs={{0,4},{1,5},{2,6},{3,7},{4,0},{5,1},{6,2},{7,3},{8,12},{9,13},{10,... | collective-permute-start | bytes 221192 | tf_op jit(solution)/shard_map/ppermute | solution.py:171
  11.7 3.2 %collective-permute-start.4 = (bf16[288,128]{1,0:T(8,128)(2,1)S(1)}, bf16[288,128]{1,0:T(8,128)(2,1)S(1)}, u32[]{:S(2)}, u32[]{:S(2)}) collective-permute-start(bf16[288,128]{1,0:T(8,128)(2,1)S(1)} %shard_map.43.refs_0_.rows_ref), channel_id=1, source_target_pairs={{0,1},{1,0},{2,3},{3,2},{4,5},{5,4},{6,7},{7,6},{8,9},{9,8},{10,11... | collective-permute-start | bytes 221192 | tf_op jit(solution)/shard_map/ppermute | solution.py:171
  11.8 4.7 %collective-permute-start.9 = (bf16[288,128]{1,0:T(8,128)(2,1)S(1)}, bf16[288,128]{1,0:T(8,128)(2,1)S(1)}, u32[]{:S(2)}, u32[]{:S(2)}) collective-permute-start(bf16[288,128]{1,0:T(8,128)(2,1)S(1)} %shard_map.43.refs_0_.rows_ref), channel_id=1, source_target_pairs={{0,2},{1,3},{2,0},{3,1},{4,6},{5,7},{6,4},{7,5},{8,10},{9,11},{10,... | collective-permute-start | bytes 221192 | tf_op jit(solution)/shard_map/ppermute | solution.py:171
  13.3 4.7 %collective-permute-start.7 = (bf16[288,128]{1,0:T(8,128)(2,1)S(1)}, bf16[288,128]{1,0:T(8,128)(2,1)S(1)}, u32[]{:S(2)}, u32[]{:S(2)}) collective-permute-start(bf16[288,128]{1,0:T(8,128)(2,1)S(1)} %collective-permute-done.1.refs_2_), channel_id=1, source_target_pairs={{0,4},{1,5},{2,6},{3,7},{4,0},{5,1},{6,2},{7,3},{8,12},{9,13},{10,... | collective-permute-start | bytes 221192 | tf_op jit(solution)/shard_map/ppermute | solution.py:171
  14.4 4.3 %collective-permute-start.6 = (bf16[288,128]{1,0:T(8,128)(2,1)S(1)}, bf16[288,128]{1,0:T(8,128)(2,1)S(1)}, u32[]{:S(2)}, u32[]{:S(2)}) collective-permute-start(bf16[288,128]{1,0:T(8,128)(2,1)S(1)} %collective-permute-done.1.refs_2_), channel_id=1, source_target_pairs={{0,1},{1,0},{2,3},{3,2},{4,5},{5,4},{6,7},{7,6},{8,9},{9,8},{10,11... | collective-permute-start | bytes 221192 | tf_op jit(solution)/shard_map/ppermute | solution.py:171
  14.5 4.2 %collective-permute-start.5 = (bf16[288,128]{1,0:T(8,128)(2,1)S(1)}, bf16[288,128]{1,0:T(8,128)(2,1)S(1)}, u32[]{:S(2)}, u32[]{:S(2)}) collective-permute-start(bf16[288,128]{1,0:T(8,128)(2,1)S(1)} %collective-permute-done.3.refs_1_), channel_id=1, source_target_pairs={{0,1},{1,0},{2,3},{3,2},{4,5},{5,4},{6,7},{7,6},{8,9},{9,8},{10,11... | collective-permute-start | bytes 221192 | tf_op jit(solution)/shard_map/ppermute | solution.py:171
  14.9 4.8 %collective-permute-start.11 = (bf16[288,128]{1,0:T(8,128)(2,1)S(1)}, bf16[288,128]{1,0:T(8,128)(2,1)S(1)}, u32[]{:S(2)}, u32[]{:S(2)}) collective-permute-start(bf16[288,128]{1,0:T(8,128)(2,1)S(1)} %collective-permute-done.1.refs_2_), channel_id=1, source_target_pairs={{0,2},{1,3},{2,0},{3,1},{4,6},{5,7},{6,4},{7,5},{8,10},{9,11},{10,... | collective-permute-start | bytes 221192 | tf_op jit(solution)/shard_map/ppermute | solution.py:171
  16.5 5.2 %collective-permute-start.10 = (bf16[288,128]{1,0:T(8,128)(2,1)S(1)}, bf16[288,128]{1,0:T(8,128)(2,1)S(1)}, u32[]{:S(2)}, u32[]{:S(2)}) collective-permute-start(bf16[288,128]{1,0:T(8,128)(2,1)S(1)} %collective-permute-done.3.refs_1_), channel_id=1, source_target_pairs={{0,2},{1,3},{2,0},{3,1},{4,6},{5,7},{6,4},{7,5},{8,10},{9,11},{10,... | collective-permute-start | bytes 221192 | tf_op jit(solution)/shard_map/ppermute | solution.py:171
  18.0 4.5 %collective-permute-start.8 = (bf16[288,128]{1,0:T(8,128)(2,1)S(1)}, bf16[288,128]{1,0:T(8,128)(2,1)S(1)}, u32[]{:S(2)}, u32[]{:S(2)}) collective-permute-start(bf16[288,128]{1,0:T(8,128)(2,1)S(1)} %collective-permute-done.7.refs_2_), channel_id=1, source_target_pairs={{0,2},{1,3},{2,0},{3,1},{4,6},{5,7},{6,4},{7,5},{8,10},{9,11},{10,... | collective-permute-start | bytes 221192 | tf_op jit(solution)/shard_map/ppermute | solution.py:171
  18.7 4.2 %collective-permute-start.12 = (bf16[288,128]{1,0:T(8,128)(2,1)S(1)}, bf16[288,128]{1,0:T(8,128)(2,1)S(1)}, u32[]{:S(2)}, u32[]{:S(2)}) collective-permute-start(bf16[288,128]{1,0:T(8,128)(2,1)S(1)} %collective-permute-done.9.refs_1_), channel_id=1, source_target_pairs={{0,1},{1,0},{2,3},{3,2},{4,5},{5,4},{6,7},{7,6},{8,9},{9,8},{10,11... | collective-permute-start | bytes 221192 | tf_op jit(solution)/shard_map/ppermute | solution.py:171
  18.7 4.2 %collective-permute-start.13 = (bf16[288,128]{1,0:T(8,128)(2,1)S(1)}, bf16[288,128]{1,0:T(8,128)(2,1)S(1)}, u32[]{:S(2)}, u32[]{:S(2)}) collective-permute-start(bf16[288,128]{1,0:T(8,128)(2,1)S(1)} %collective-permute-done.7.refs_2_), channel_id=1, source_target_pairs={{0,1},{1,0},{2,3},{3,2},{4,5},{5,4},{6,7},{7,6},{8,9},{9,8},{10,11... | collective-permute-start | bytes 221192 | tf_op jit(solution)/shard_map/ppermute | solution.py:171
  19.8 3.1 %collective-permute-start.15 = (bf16[288,128]{1,0:T(8,128)(2,1)S(1)}, bf16[288,128]{1,0:T(8,128)(2,1)S(1)}, u32[]{:S(2)}, u32[]{:S(2)}) collective-permute-start(bf16[288,128]{1,0:T(8,128)(2,1)S(1)} %collective-permute-done.11.refs_4_), channel_id=1, source_target_pairs={{0,1},{1,0},{2,3},{3,2},{4,5},{5,4},{6,7},{7,6},{8,9},{9,8},{10,11... | collective-permute-start | bytes 221192 | tf_op jit(solution)/shard_map/ppermute | solution.py:171
  21.6 1.3 %collective-permute-start.14 = (bf16[288,128]{1,0:T(8,128)(2,1)S(1)}, bf16[288,128]{1,0:T(8,128)(2,1)S(1)}, u32[]{:S(2)}, u32[]{:S(2)}) collective-permute-start(bf16[288,128]{1,0:T(8,128)(2,1)S(1)} %collective-permute-done.10.refs_3_), channel_id=1, source_target_pairs={{0,1},{1,0},{2,3},{3,2},{4,5},{5,4},{6,7},{7,6},{8,9},{9,8},{10,11... | collective-permute-start | bytes 221192 | tf_op jit(solution)/shard_map/ppermute | solution.py:171
  22.4 1.3 %collective-permute-start.16 = (bf16[288,128]{1,0:T(8,128)(2,1)S(1)}, bf16[288,128]{1,0:T(8,128)(2,1)S(1)}, u32[]{:S(2)}, u32[]{:S(2)}) collective-permute-start(bf16[288,128]{1,0:T(8,128)(2,1)S(1)} %collective-permute-done.8.refs_0_), channel_id=1, source_target_pairs={{0,1},{1,0},{2,3},{3,2},{4,5},{5,4},{6,7},{7,6},{8,9},{9,8},{10,11... | collective-permute-start | bytes 221192 | tf_op jit(solution)/shard_map/ppermute | solution.py:171
  23.6 4.4 %copy-start.2 = (f32[2,64,576]{2,1,0:T(8,128)S(1)}, f32[2,64,576]{2,1,0:T(8,128)}, u32[]{:S(2)}) copy-start(f32[2,64,576]{2,1,0:T(8,128)} %momentum_ref.3) | copy-start | bytes 884740
  26.3 4.5 %collective-permute-start.17 = (bf16[288,128]{1,0:T(8,128)(2,1)S(1)}, bf16[288,128]{1,0:T(8,128)(2,1)S(1)}, u32[]{:S(2)}, u32[]{:S(2)}) collective-permute-start(bf16[288,128]{1,0:T(8,128)(2,1)S(1)} %shard_map.47.rows_ref), channel_id=1, source_target_pairs={{0,16},{16,0},{1,17},{17,1},{2,18},{18,2},{3,19},{19,3},{4,20},{20... | collective-permute-start | bytes 221192 | tf_op jit(solution)/shard_map/ppermute | solution.py:171

commit v6 on v5

--- a/solution.py
+++ b/solution.py
@@ -227,11 +227,24 @@
 
 def update_kernel(scale, own, rows_ref, *refs):
     out_ref, held, done = refs[-3:]
+    rows, width = held.shape
+    whole = width // 128
+    half = rows // 2
     mine = lax.axis_index("outer")
-    unpack(scale * rows_ref[...].astype(F32), 0, held, 0, *held.shape)
-    copy = pltpu.make_async_copy(held, out_ref.at[mine if own else 1 - mine], done)
-    copy.start()
-    copy.wait()
+    target = out_ref.at[mine if own else 1 - mine]
+    copies = []
+    for part in range(2):
+        at = half * part
+        for tile in range(whole):
+            block = rows_ref[rows * tile + at : rows * tile + at + half, :].astype(F32)
+            held[at : at + half, 128 * tile : 128 * (tile + 1)] = scale * block
+        rest = rows_ref[rows * whole : rows * whole + half, :].astype(F32)
+        held[at : at + half, 128 * whole :] = scale * rest[:, 64 * part : 64 * (part + 1)]
+        span = pl.ds(at, half)
+        copies.append(pltpu.make_async_copy(held.at[span], target.at[span], done.at[part]))
+        copies[-1].start()
+    for copy in copies:
+        copy.wait()
 
 
 def two_pods(local, momentum):
@@ -274,7 +287,7 @@
     )(momentum, kept, arrived, away, arrived_too)
 
     other = exchange(mine, "outer", 1)
-    scratch = [pltpu.VMEM(one, F32), pltpu.SemaphoreType.DMA]
+    scratch = [pltpu.VMEM(one, F32), pltpu.SemaphoreType.DMA((2,))]
     half = pl.pallas_call(
         functools.partial(update_kernel, update_scale, True),
         out_shape=both,

time: 31.8 us -> 31.8 us (level)
  no operation moved by 1% of the time
where the time goes in v6:
time: 31.8 us; the launch traced here: 31.6 us
  starting transfers between devices  17.2 us (54%)
  Pallas kernels  6.78 us (21%)
  waiting for transfers between devices  4.93 us (16%)
  local copies, waits for them, and re-layouts  1.94 us (6%)
  between operations  0.71 us (2%)
    ppermute x18, starting transfers between devices, exchange(): lax.ppermute(value, axis, [(at, at ^ distance) for at in range(size)])  17.2 us
    ppermute x18, waiting for transfers between devices, exchange(): lax.ppermute(value, axis, [(at, at ^ distance) for at in range(size)])  4.93 us
    pallas_call x1, Pallas kernels, finish(): pl.pallas_call(functools.partial(finish_kernel, rows), out_shape=jax.Shap...  2.54 us
    unnamed x6, local copies, waits for them, and re-layouts  1.94 us
    pallas_call x2, Pallas kernels, gram_of(): pl.pallas_call(functools.partial(gram_kernel, rows, len(before)), out_sha...  1.37 us
    pallas_call x1, Pallas kernels, two_pods(): pl.pallas_call(momentum_kernel, out_shape=both, in_specs=[VMEM] * 5, scra...  0.81 us
    pallas_call x1, Pallas kernels, two_pods(): pl.pallas_call(functools.partial(update_kernel, update_scale, False), out...  0.72 us
    pallas_call x1, Pallas kernels, two_pods(): pl.pallas_call(functools.partial(update_kernel, update_scale, True), out_...  0.72 us
  transfers between devices with their start and end apart: 18, of which 7 were waited for; matrix products, arithmetic and copies ran while one was open for 0% of the time, Pallas kernels for 11%

profile of v6, /device:TPU:0, one launch (start us, length us, event | category | flops | bytes accessed | tf_op | source)
XLA Modules:
  0.0 31.6 jit_solution(948146962073380956)
XLA Ops:
  0.6 1.0 %copy-done = f32[1,2,64,576]{3,2,1,0:T(8,128)S(1)} copy-done((f32[1,2,64,576]{3,2,1,0:T(8,128)S(1)}, f32[1,2,64,576]{3,2,1,0:T(8,128)}, u32[]{:S(2)}) %copy-start) | copy-done | bytes 294936
  1.6 0.1 shard_map.42.away_ref
  1.7 2.9 %collective-permute-start = (bf16[288,128]{1,0:T(8,128)(2,1)S(1)}, bf16[288,128]{1,0:T(8,128)(2,1)S(1)}, u32[]{:S(2)}, u32[]{:S(2)}) collective-permute-start(bf16[288,128]{1,0:T(8,128)(2,1)S(1)} %shard_map.42.away_ref), channel_id=1, source_target_pairs={{0,16},{16,0},{1,17},{17,1},{2,18},{18,2},{3,19},{19,3},{4,20},{20... | collective-permute-start | bytes 221192 | tf_op jit(solution)/shard_map/ppermute | solution.py:171
  4.6 1.0 %copy-done.1 = f32[2,64,576]{2,1,0:T(8,128)S(1)} copy-done((f32[2,64,576]{2,1,0:T(8,128)S(1)}, f32[2,64,576]{2,1,0:T(8,128)}, u32[]{:S(2)}) %copy-start.1) | copy-done | bytes 294936
  5.6 0.5 %shard_map.41 = (bf16[288,128]{1,0:T(8,128)(2,1)S(1)}, f32[288,128]{1,0:T(8,128)S(1)}) custom-call(f32[2,64,576]{2,1,0:T(8,128)S(1)} %bitcast.2, f32[2,64,576]{2,1,0:T(8,128)S(1)} %copy-done.1), custom_call_target="tpu_custom_call" | custom-call | tf_op jit(solution)/shard_map/pallas_call | solution.py:267
  6.1 0.1 collective-permute-start.2
  6.2 0.8 %collective-permute-done.arrived_ref = bf16[288,128]{1,0:T(8,128)(2,1)S(1)} collective-permute-done((bf16[288,128]{1,0:T(8,128)(2,1)S(1)}, bf16[288,128]{1,0:T(8,128)(2,1)S(1)}, u32[]{:S(2)}, u32[]{:S(2)}) %collective-permute-start) | collective-permute-done | bytes 73760 | tf_op jit(solution)/shard_map/ppermute | solution.py:171
  7.0 3.2 %collective-permute-start.1 = (bf16[288,128]{1,0:T(8,128)(2,1)S(1)}, bf16[288,128]{1,0:T(8,128)(2,1)S(1)}, u32[]{:S(2)}, u32[]{:S(2)}) collective-permute-start(bf16[288,128]{1,0:T(8,128)(2,1)S(1)} %shard_map.43.refs_0_.rows_ref), channel_id=1, source_target_pairs={{0,8},{1,9},{2,10},{3,11},{4,12},{5,13},{6,14},{7,15},{8,0},{9,1},... | collective-permute-start | bytes 221192 | tf_op jit(solution)/shard_map/ppermute | solution.py:171
  10.2 1.6 %collective-permute-start.3 = (bf16[288,128]{1,0:T(8,128)(2,1)S(1)}, bf16[288,128]{1,0:T(8,128)(2,1)S(1)}, u32[]{:S(2)}, u32[]{:S(2)}) collective-permute-start(bf16[288,128]{1,0:T(8,128)(2,1)S(1)} %shard_map.43.refs_0_.rows_ref), channel_id=1, source_target_pairs={{0,4},{1,5},{2,6},{3,7},{4,0},{5,1},{6,2},{7,3},{8,12},{9,13},{10,... | collective-permute-start | bytes 221192 | tf_op jit(solution)/shard_map/ppermute | solution.py:171
  11.7 0.0 collective-permute-start.4
  11.8 1.5 %collective-permute-start.9 = (bf16[288,128]{1,0:T(8,128)(2,1)S(1)}, bf16[288,128]{1,0:T(8,128)(2,1)S(1)}, u32[]{:S(2)}, u32[]{:S(2)}) collective-permute-start(bf16[288,128]{1,0:T(8,128)(2,1)S(1)} %shard_map.43.refs_0_.rows_ref), channel_id=1, source_target_pairs={{0,2},{1,3},{2,0},{3,1},{4,6},{5,7},{6,4},{7,5},{8,10},{9,11},{10,... | collective-permute-start | bytes 221192 | tf_op jit(solution)/shard_map/ppermute | solution.py:171
  13.3 1.1 %collective-permute-start.7 = (bf16[288,128]{1,0:T(8,128)(2,1)S(1)}, bf16[288,128]{1,0:T(8,128)(2,1)S(1)}, u32[]{:S(2)}, u32[]{:S(2)}) collective-permute-start(bf16[288,128]{1,0:T(8,128)(2,1)S(1)} %collective-permute-done.1.refs_2_), channel_id=1, source_target_pairs={{0,4},{1,5},{2,6},{3,7},{4,0},{5,1},{6,2},{7,3},{8,12},{9,13},{10,... | collective-permute-start | bytes 221192 | tf_op jit(solution)/shard_map/ppermute | solution.py:171
  14.4 0.1 collective-permute-done.3.refs_1_
  14.5 0.4 %collective-permute-start.5 = (bf16[288,128]{1,0:T(8,128)(2,1)S(1)}, bf16[288,128]{1,0:T(8,128)(2,1)S(1)}, u32[]{:S(2)}, u32[]{:S(2)}) collective-permute-start(bf16[288,128]{1,0:T(8,128)(2,1)S(1)} %collective-permute-done.3.refs_1_), channel_id=1, source_target_pairs={{0,1},{1,0},{2,3},{3,2},{4,5},{5,4},{6,7},{7,6},{8,9},{9,8},{10,11... | collective-permute-start | bytes 221192 | tf_op jit(solution)/shard_map/ppermute | solution.py:171
  14.9 1.5 %collective-permute-start.11 = (bf16[288,128]{1,0:T(8,128)(2,1)S(1)}, bf16[288,128]{1,0:T(8,128)(2,1)S(1)}, u32[]{:S(2)}, u32[]{:S(2)}) collective-permute-start(bf16[288,128]{1,0:T(8,128)(2,1)S(1)} %collective-permute-done.1.refs_2_), channel_id=1, source_target_pairs={{0,2},{1,3},{2,0},{3,1},{4,6},{5,7},{6,4},{7,5},{8,10},{9,11},{10,... | collective-permute-start | bytes 221192 | tf_op jit(solution)/shard_map/ppermute | solution.py:171
  16.5 1.5 %collective-permute-start.10 = (bf16[288,128]{1,0:T(8,128)(2,1)S(1)}, bf16[288,128]{1,0:T(8,128)(2,1)S(1)}, u32[]{:S(2)}, u32[]{:S(2)}) collective-permute-start(bf16[288,128]{1,0:T(8,128)(2,1)S(1)} %collective-permute-done.3.refs_1_), channel_id=1, source_target_pairs={{0,2},{1,3},{2,0},{3,1},{4,6},{5,7},{6,4},{7,5},{8,10},{9,11},{10,... | collective-permute-start | bytes 221192 | tf_op jit(solution)/shard_map/ppermute | solution.py:171
  18.0 0.8 %collective-permute-start.8 = (bf16[288,128]{1,0:T(8,128)(2,1)S(1)}, bf16[288,128]{1,0:T(8,128)(2,1)S(1)}, u32[]{:S(2)}, u32[]{:S(2)}) collective-permute-start(bf16[288,128]{1,0:T(8,128)(2,1)S(1)} %collective-permute-done.7.refs_2_), channel_id=1, source_target_pairs={{0,2},{1,3},{2,0},{3,1},{4,6},{5,7},{6,4},{7,5},{8,10},{9,11},{10,... | collective-permute-start | bytes 221192 | tf_op jit(solution)/shard_map/ppermute | solution.py:171
  18.7 0.5 %collective-permute-start.13 = (bf16[288,128]{1,0:T(8,128)(2,1)S(1)}, bf16[288,128]{1,0:T(8,128)(2,1)S(1)}, u32[]{:S(2)}, u32[]{:S(2)}) collective-permute-start(bf16[288,128]{1,0:T(8,128)(2,1)S(1)} %collective-permute-done.7.refs_2_), channel_id=1, source_target_pairs={{0,1},{1,0},{2,3},{3,2},{4,5},{5,4},{6,7},{7,6},{8,9},{9,8},{10,11... | collective-permute-start | bytes 221192 | tf_op jit(solution)/shard_map/ppermute | solution.py:171
  19.2 0.6 %collective-permute-done.11.refs_4_ = bf16[288,128]{1,0:T(8,128)(2,1)S(1)} collective-permute-done((bf16[288,128]{1,0:T(8,128)(2,1)S(1)}, bf16[288,128]{1,0:T(8,128)(2,1)S(1)}, u32[]{:S(2)}, u32[]{:S(2)}) %collective-permute-start.11) | collective-permute-done | bytes 73760 | tf_op jit(solution)/shard_map/ppermute | solution.py:171
  19.8 1.8 %collective-permute-done.10.refs_3_ = bf16[288,128]{1,0:T(8,128)(2,1)S(1)} collective-permute-done((bf16[288,128]{1,0:T(8,128)(2,1)S(1)}, bf16[288,128]{1,0:T(8,128)(2,1)S(1)}, u32[]{:S(2)}, u32[]{:S(2)}) %collective-permute-start.10) | collective-permute-done | bytes 73760 | tf_op jit(solution)/shard_map/ppermute | solution.py:171
  21.6 0.7 %shard_map.45.refs_0_ = f32[576,576]{1,0:T(8,128)S(1)} custom-call(bf16[288,128]{1,0:T(8,128)(2,1)S(1)} %shard_map.43.refs_0_.rows_ref, bf16[288,128]{1,0:T(8,128)(2,1)S(1)} %collective-permute-done.3.refs_1_, bf16[288,128]{1,0:T(8,128)(2,1)S(1)} %collective-permute-done.1.refs_2_, bf16[288,128]{1,0:T(8,128)(2,1)S(1)} %collective-permute-done.4.refs_3_, ...), custom_call_target="tpu_custom_call" | custom-call | tf_op jit(solution)/shard_map/pallas_call | solution.py:109
  22.3 0.1 collective-permute-done.8.refs_0_
  22.4 0.4 %collective-permute-start.16 = (bf16[288,128]{1,0:T(8,128)(2,1)S(1)}, bf16[288,128]{1,0:T(8,128)(2,1)S(1)}, u32[]{:S(2)}, u32[]{:S(2)}) collective-permute-start(bf16[288,128]{1,0:T(8,128)(2,1)S(1)} %collective-permute-done.8.refs_0_), channel_id=1, source_target_pairs={{0,1},{1,0},{2,3},{3,2},{4,5},{5,4},{6,7},{7,6},{8,9},{9,8},{10,11... | collective-permute-start | bytes 221192 | tf_op jit(solution)/shard_map/ppermute | solution.py:171
  22.9 0.7 %shard_map.46.sum_ref = f32[576,576]{1,0:T(8,128)S(1)} custom-call(f32[576,576]{1,0:T(8,128)S(1)} %shard_map.45.refs_0_, bf16[288,128]{1,0:T(8,128)(2,1)S(1)} %collective-permute-done.9.refs_1_, bf16[288,128]{1,0:T(8,128)(2,1)S(1)} %collective-permute-done.7.refs_2_, bf16[288,128]{1,0:T(8,128)(2,1)S(1)} %collective-permute-done.10.refs_3_, ...), custom_call_target="tpu_custom_call" | custom-call | tf_op jit(solution)/shard_map/pallas_call | solution.py:109
  23.6 0.0 copy-start.2
  23.6 0.2 collective-permute-done.16.refs_1_
  23.8 2.5 %shard_map.47.rows_ref = bf16[288,128]{1,0:T(8,128)(2,1)S(1)} custom-call(f32[576,576]{1,0:T(8,128)S(1)} %shard_map.46.sum_ref, bf16[288,128]{1,0:T(8,128)(2,1)S(1)} %shard_map.43.refs_0_.rows_ref, bf16[288,128]{1,0:T(8,128)(2,1)S(1)} %collective-permute-done.8.refs_0_, bf16[288,128]{1,0:T(8,128)(2,1)S(1)} %collective-permute-done.16.refs_1_), custom_call_target="tpu_custom_call" | custom-call | tf_op jit(solution)/shard_map/pallas_call | solution.py:127
  26.3 1.7 %collective-permute-start.17 = (bf16[288,128]{1,0:T(8,128)(2,1)S(1)}, bf16[288,128]{1,0:T(8,128)(2,1)S(1)}, u32[]{:S(2)}, u32[]{:S(2)}) collective-permute-start(bf16[288,128]{1,0:T(8,128)(2,1)S(1)} %shard_map.47.rows_ref), channel_id=1, source_target_pairs={{0,16},{16,0},{1,17},{17,1},{2,18},{18,2},{3,19},{19,3},{4,20},{20... | collective-permute-start | bytes 221192 | tf_op jit(solution)/shard_map/ppermute | solution.py:171
  28.0 0.8 %shard_map.44 = f32[2,64,576]{2,1,0:T(8,128)} custom-call(f32[2,64,576]{2,1,0:T(8,128)S(1)} %copy-done.2, bf16[288,128]{1,0:T(8,128)(2,1)S(1)} %get-tuple-element.8.kept_ref, bf16[288,128]{1,0:T(8,128)(2,1)S(1)} %collective-permute-done.arrived_ref, bf16[288,128]{1,0:T(8,128)(2,1)S(1)} %shard_map.42.away_ref, ...), custom_call_target="tpu_custom_call" | custom-call | tf_op jit(solution)/shard_map/pallas_call | solution.py:281
  28.8 0.7 %shard_map.48.refs_0_ = f32[2,64,576]{2,1,0:T(8,128)} custom-call(bf16[288,128]{1,0:T(8,128)(2,1)S(1)} %shard_map.47.rows_ref), custom_call_target="tpu_custom_call" | custom-call | tf_op jit(solution)/shard_map/pallas_call | solution.py:291
  29.5 1.3 %collective-permute-done.17.rows_ref = bf16[288,128]{1,0:T(8,128)(2,1)S(1)} collective-permute-done((bf16[288,128]{1,0:T(8,128)(2,1)S(1)}, bf16[288,128]{1,0:T(8,128)(2,1)S(1)}, u32[]{:S(2)}, u32[]{:S(2)}) %collective-permute-start.17) | collective-permute-done | bytes 73760 | tf_op jit(solution)/shard_map/ppermute | solution.py:171
  30.9 0.7 %shard_map.49 = f32[2,64,576]{2,1,0:T(8,128)} custom-call(bf16[288,128]{1,0:T(8,128)(2,1)S(1)} %collective-permute-done.17.rows_ref, f32[2,64,576]{2,1,0:T(8,128)} %shard_map.48.refs_0_), custom_call_target="tpu_custom_call", output_to_operand_aliasing={{}: (1, {})} | custom-call | tf_op jit(solution)/shard_map/pallas_call | solution.py:299
  (19 shorter events, 0.1 us)
Async XLA Ops:
  0.6 1.0 %copy-start = (f32[1,2,64,576]{3,2,1,0:T(8,128)S(1)}, f32[1,2,64,576]{3,2,1,0:T(8,128)}, u32[]{:S(2)}) copy-start(f32[1,2,64,576]{3,2,1,0:T(8,128)} %param.2) | copy-start | bytes 884740
  1.7 5.3 %collective-permute-start = (bf16[288,128]{1,0:T(8,128)(2,1)S(1)}, bf16[288,128]{1,0:T(8,128)(2,1)S(1)}, u32[]{:S(2)}, u32[]{:S(2)}) collective-permute-start(bf16[288,128]{1,0:T(8,128)(2,1)S(1)} %shard_map.42.away_ref), channel_id=1, source_target_pairs={{0,16},{16,0},{1,17},{17,1},{2,18},{18,2},{3,19},{19,3},{4,20},{20... | collective-permute-start | bytes 221192 | tf_op jit(solution)/shard_map/ppermute | solution.py:171
  4.6 1.0 %copy-start.1 = (f32[2,64,576]{2,1,0:T(8,128)S(1)}, f32[2,64,576]{2,1,0:T(8,128)}, u32[]{:S(2)}) copy-start(f32[2,64,576]{2,1,0:T(8,128)} %momentum_ref.3) | copy-start | bytes 884740
  6.1 7.2 %collective-permute-start.2 = (bf16[288,128]{1,0:T(8,128)(2,1)S(1)}, bf16[288,128]{1,0:T(8,128)(2,1)S(1)}, u32[]{:S(2)}, u32[]{:S(2)}) collective-permute-start(bf16[288,128]{1,0:T(8,128)(2,1)S(1)} %get-tuple-element.8.kept_ref), channel_id=1, source_target_pairs={{0,16},{16,0},{1,17},{17,1},{2,18},{18,2},{3,19},{19,3},{4,20},{20... | collective-permute-start | bytes 221192 | tf_op jit(solution)/shard_map/ppermute | solution.py:171
  7.0 6.3 %collective-permute-start.1 = (bf16[288,128]{1,0:T(8,128)(2,1)S(1)}, bf16[288,128]{1,0:T(8,128)(2,1)S(1)}, u32[]{:S(2)}, u32[]{:S(2)}) collective-permute-start(bf16[288,128]{1,0:T(8,128)(2,1)S(1)} %shard_map.43.refs_0_.rows_ref), channel_id=1, source_target_pairs={{0,8},{1,9},{2,10},{3,11},{4,12},{5,13},{6,14},{7,15},{8,0},{9,1},... | collective-permute-start | bytes 221192 | tf_op jit(solution)/shard_map/ppermute | solution.py:171
  10.2 4.4 %collective-permute-start.3 = (bf16[288,128]{1,0:T(8,128)(2,1)S(1)}, bf16[288,128]{1,0:T(8,128)(2,1)S(1)}, u32[]{:S(2)}, u32[]{:S(2)}) collective-permute-start(bf16[288,128]{1,0:T(8,128)(2,1)S(1)} %shard_map.43.refs_0_.rows_ref), channel_id=1, source_target_pairs={{0,4},{1,5},{2,6},{3,7},{4,0},{5,1},{6,2},{7,3},{8,12},{9,13},{10,... | collective-permute-start | bytes 221192 | tf_op jit(solution)/shard_map/ppermute | solution.py:171
  11.7 3.2 %collective-permute-start.4 = (bf16[288,128]{1,0:T(8,128)(2,1)S(1)}, bf16[288,128]{1,0:T(8,128)(2,1)S(1)}, u32[]{:S(2)}, u32[]{:S(2)}) collective-permute-start(bf16[288,128]{1,0:T(8,128)(2,1)S(1)} %shard_map.43.refs_0_.rows_ref), channel_id=1, source_target_pairs={{0,1},{1,0},{2,3},{3,2},{4,5},{5,4},{6,7},{7,6},{8,9},{9,8},{10,11... | collective-permute-start | bytes 221192 | tf_op jit(solution)/shard_map/ppermute | solution.py:171
  11.8 4.7 %collective-permute-start.9 = (bf16[288,128]{1,0:T(8,128)(2,1)S(1)}, bf16[288,128]{1,0:T(8,128)(2,1)S(1)}, u32[]{:S(2)}, u32[]{:S(2)}) collective-permute-start(bf16[288,128]{1,0:T(8,128)(2,1)S(1)} %shard_map.43.refs_0_.rows_ref), channel_id=1, source_target_pairs={{0,2},{1,3},{2,0},{3,1},{4,6},{5,7},{6,4},{7,5},{8,10},{9,11},{10,... | collective-permute-start | bytes 221192 | tf_op jit(solution)/shard_map/ppermute | solution.py:171
  13.3 4.7 %collective-permute-start.7 = (bf16[288,128]{1,0:T(8,128)(2,1)S(1)}, bf16[288,128]{1,0:T(8,128)(2,1)S(1)}, u32[]{:S(2)}, u32[]{:S(2)}) collective-permute-start(bf16[288,128]{1,0:T(8,128)(2,1)S(1)} %collective-permute-done.1.refs_2_), channel_id=1, source_target_pairs={{0,4},{1,5},{2,6},{3,7},{4,0},{5,1},{6,2},{7,3},{8,12},{9,13},{10,... | collective-permute-start | bytes 221192 | tf_op jit(solution)/shard_map/ppermute | solution.py:171
  14.4 4.3 %collective-permute-start.6 = (bf16[288,128]{1,0:T(8,128)(2,1)S(1)}, bf16[288,128]{1,0:T(8,128)(2,1)S(1)}, u32[]{:S(2)}, u32[]{:S(2)}) collective-permute-start(bf16[288,128]{1,0:T(8,128)(2,1)S(1)} %collective-permute-done.1.refs_2_), channel_id=1, source_target_pairs={{0,1},{1,0},{2,3},{3,2},{4,5},{5,4},{6,7},{7,6},{8,9},{9,8},{10,11... | collective-permute-start | bytes 221192 | tf_op jit(solution)/shard_map/ppermute | solution.py:171
  14.5 4.2 %collective-permute-start.5 = (bf16[288,128]{1,0:T(8,128)(2,1)S(1)}, bf16[288,128]{1,0:T(8,128)(2,1)S(1)}, u32[]{:S(2)}, u32[]{:S(2)}) collective-permute-start(bf16[288,128]{1,0:T(8,128)(2,1)S(1)} %collective-permute-done.3.refs_1_), channel_id=1, source_target_pairs={{0,1},{1,0},{2,3},{3,2},{4,5},{5,4},{6,7},{7,6},{8,9},{9,8},{10,11... | collective-permute-start | bytes 221192 | tf_op jit(solution)/shard_map/ppermute | solution.py:171
  14.9 4.8 %collective-permute-start.11 = (bf16[288,128]{1,0:T(8,128)(2,1)S(1)}, bf16[288,128]{1,0:T(8,128)(2,1)S(1)}, u32[]{:S(2)}, u32[]{:S(2)}) collective-permute-start(bf16[288,128]{1,0:T(8,128)(2,1)S(1)} %collective-permute-done.1.refs_2_), channel_id=1, source_target_pairs={{0,2},{1,3},{2,0},{3,1},{4,6},{5,7},{6,4},{7,5},{8,10},{9,11},{10,... | collective-permute-start | bytes 221192 | tf_op jit(solution)/shard_map/ppermute | solution.py:171
  16.5 5.2 %collective-permute-start.10 = (bf16[288,128]{1,0:T(8,128)(2,1)S(1)}, bf16[288,128]{1,0:T(8,128)(2,1)S(1)}, u32[]{:S(2)}, u32[]{:S(2)}) collective-permute-start(bf16[288,128]{1,0:T(8,128)(2,1)S(1)} %collective-permute-done.3.refs_1_), channel_id=1, source_target_pairs={{0,2},{1,3},{2,0},{3,1},{4,6},{5,7},{6,4},{7,5},{8,10},{9,11},{10,... | collective-permute-start | bytes 221192 | tf_op jit(solution)/shard_map/ppermute | solution.py:171
  18.0 4.5 %collective-permute-start.8 = (bf16[288,128]{1,0:T(8,128)(2,1)S(1)}, bf16[288,128]{1,0:T(8,128)(2,1)S(1)}, u32[]{:S(2)}, u32[]{:S(2)}) collective-permute-start(bf16[288,128]{1,0:T(8,128)(2,1)S(1)} %collective-permute-done.7.refs_2_), channel_id=1, source_target_pairs={{0,2},{1,3},{2,0},{3,1},{4,6},{5,7},{6,4},{7,5},{8,10},{9,11},{10,... | collective-permute-start | bytes 221192 | tf_op jit(solution)/shard_map/ppermute | solution.py:171
  18.7 4.2 %collective-permute-start.12 = (bf16[288,128]{1,0:T(8,128)(2,1)S(1)}, bf16[288,128]{1,0:T(8,128)(2,1)S(1)}, u32[]{:S(2)}, u32[]{:S(2)}) collective-permute-start(bf16[288,128]{1,0:T(8,128)(2,1)S(1)} %collective-permute-done.9.refs_1_), channel_id=1, source_target_pairs={{0,1},{1,0},{2,3},{3,2},{4,5},{5,4},{6,7},{7,6},{8,9},{9,8},{10,11... | collective-permute-start | bytes 221192 | tf_op jit(solution)/shard_map/ppermute | solution.py:171
  18.7 4.2 %collective-permute-start.13 = (bf16[288,128]{1,0:T(8,128)(2,1)S(1)}, bf16[288,128]{1,0:T(8,128)(2,1)S(1)}, u32[]{:S(2)}, u32[]{:S(2)}) collective-permute-start(bf16[288,128]{1,0:T(8,128)(2,1)S(1)} %collective-permute-done.7.refs_2_), channel_id=1, source_target_pairs={{0,1},{1,0},{2,3},{3,2},{4,5},{5,4},{6,7},{7,6},{8,9},{9,8},{10,11... | collective-permute-start | bytes 221192 | tf_op jit(solution)/shard_map/ppermute | solution.py:171
  19.8 3.1 %collective-permute-start.15 = (bf16[288,128]{1,0:T(8,128)(2,1)S(1)}, bf16[288,128]{1,0:T(8,128)(2,1)S(1)}, u32[]{:S(2)}, u32[]{:S(2)}) collective-permute-start(bf16[288,128]{1,0:T(8,128)(2,1)S(1)} %collective-permute-done.11.refs_4_), channel_id=1, source_target_pairs={{0,1},{1,0},{2,3},{3,2},{4,5},{5,4},{6,7},{7,6},{8,9},{9,8},{10,11... | collective-permute-start | bytes 221192 | tf_op jit(solution)/shard_map/ppermute | solution.py:171
  21.6 1.3 %collective-permute-start.14 = (bf16[288,128]{1,0:T(8,128)(2,1)S(1)}, bf16[288,128]{1,0:T(8,128)(2,1)S(1)}, u32[]{:S(2)}, u32[]{:S(2)}) collective-permute-start(bf16[288,128]{1,0:T(8,128)(2,1)S(1)} %collective-permute-done.10.refs_3_), channel_id=1, source_target_pairs={{0,1},{1,0},{2,3},{3,2},{4,5},{5,4},{6,7},{7,6},{8,9},{9,8},{10,11... | collective-permute-start | bytes 221192 | tf_op jit(solution)/shard_map/ppermute | solution.py:171
  22.4 1.3 %collective-permute-start.16 = (bf16[288,128]{1,0:T(8,128)(2,1)S(1)}, bf16[288,128]{1,0:T(8,128)(2,1)S(1)}, u32[]{:S(2)}, u32[]{:S(2)}) collective-permute-start(bf16[288,128]{1,0:T(8,128)(2,1)S(1)} %collective-permute-done.8.refs_0_), channel_id=1, source_target_pairs={{0,1},{1,0},{2,3},{3,2},{4,5},{5,4},{6,7},{7,6},{8,9},{9,8},{10,11... | collective-permute-start | bytes 221192 | tf_op jit(solution)/shard_map/ppermute | solution.py:171
  23.6 4.4 %copy-start.2 = (f32[2,64,576]{2,1,0:T(8,128)S(1)}, f32[2,64,576]{2,1,0:T(8,128)}, u32[]{:S(2)}) copy-start(f32[2,64,576]{2,1,0:T(8,128)} %momentum_ref.3) | copy-start | bytes 884740
  26.3 4.5 %collective-permute-start.17 = (bf16[288,128]{1,0:T(8,128)(2,1)S(1)}, bf16[288,128]{1,0:T(8,128)(2,1)S(1)}, u32[]{:S(2)}, u32[]{:S(2)}) collective-permute-start(bf16[288,128]{1,0:T(8,128)(2,1)S(1)} %shard_map.47.rows_ref), channel_id=1, source_target_pairs={{0,16},{16,0},{1,17},{17,1},{2,18},{18,2},{3,19},{19,3},{4,20},{20... | collective-permute-start | bytes 221192 | tf_op jit(solution)/shard_map/ppermute | solution.py:171
